TPU v7x, 512 devices: a whole 4x8x8 slice. The times are simulated.
512 devices in a mesh: ctx: 128 (over z, y_hi, x, core), tp: 4 (over y_lo).
Axes of the slice: x: 4, y: 8 (y_hi: 2, y_lo: 4; y = y_hi * 4 + y_lo), z: 8, core: 2. Of those that a mesh axis runs over, the one named last changes fastest.
Arguments:
- series: bfloat16 [131072, 1024], P(('ctx', 'tp'))
- w_query: bfloat16 [1024, 1024], P(None, 'tp')
- w_key: bfloat16 [1024, 1024], P(None, 'tp')
- w_value: bfloat16 [1024, 1024], P(None, 'tp'), may hold values from -0.1875 to 0.1875
- block_pos: int32 [128], replicated, may hold values from 0 to 127, as said below
Outputs:
- attended: bfloat16 [131072, 1024], P('ctx', 'tp')
Inputs may be any that keep to these rules, and one draw needn't show every extreme that they name: Each block position appears exactly once, and block_pos[127] < block_pos[0].
All inputs are finite; a program needn't handle non-finite values.
Results may differ from a plain program's by a relative error of at most 0.0072.
Values may be sent and summed in bfloat16 or wider, within the bound.
No kernel may reach another device: no remote copies, remote signals or barrier semaphores. Data moves between devices by JAX's collectives and lax.ppermute only.
A program may use at most 64 MiB of HBM per device.

v0:
```python
import jax
import jax.numpy as jnp
from jax import lax
from jax.sharding import PartitionSpec as P

HD = 128


def passed_along(block, axis, distance):
    devices = range(lax.axis_size(axis))
    route = [((i - distance) % len(devices), i) for i in devices]
    return lax.ppermute(block, axis, route)


def attend_rows(query, keys, values, allowed, heads_here):
    count = query.shape[0]
    q_heads = query.reshape(count, heads_here, HD)
    k_heads = keys.reshape(keys.shape[0], heads_here, HD)
    v_heads = values.reshape(values.shape[0], heads_here, HD)
    scores = jnp.einsum("qhd,khd->hqk", q_heads, k_heads, preferred_element_type=jnp.float32)
    scores = scores / jnp.sqrt(jnp.float32(HD))
    scores = jnp.where(allowed[None], scores, -jnp.inf)
    top = jnp.max(scores, axis=-1, keepdims=True)
    weights = jnp.where(allowed[None], jnp.exp(scores - top), jnp.float32(0.0))
    total = jnp.sum(weights, axis=-1)
    mixed = jnp.einsum(
        "hqk,khd->qhd", weights.astype(jnp.bfloat16), v_heads, preferred_element_type=jnp.float32
    )
    mixed = mixed / jnp.transpose(total)[:, :, None]
    return mixed.reshape(count, heads_here * HD).astype(jnp.bfloat16)


def body(series, w_query, w_key, w_value, block_pos):
    width = w_query.shape[1]
    heads_here = width // HD
    piece = lax.all_gather(series, "tp", axis=0, tiled=True)
    joined = jnp.concatenate(
        [
            jnp.dot(piece, weight, preferred_element_type=jnp.float32).astype(jnp.bfloat16)
            for weight in (w_query, w_key, w_value)
        ],
        axis=1,
    )
    block_rows = joined.shape[0]
    query = joined[:, :width]
    keys = joined[:, width : 2 * width]
    values = joined[:, 2 * width :]
    previous = passed_along(jnp.stack([keys, values]), "ctx", 1)
    ctx_count = lax.axis_size("ctx")
    here = lax.axis_index("ctx")
    own_pos = block_pos[here]
    prev_pos = block_pos[(here + ctx_count - 1) % ctx_count]
    visible = prev_pos < own_pos
    q_rows = min(512, block_rows)
    results = []
    for number in range(block_rows // q_rows):
        start = number * q_rows
        q_block = query[start : start + q_rows]
        row_index = start + jnp.arange(q_rows)
        col_index = jnp.arange(block_rows)
        causal = col_index[None, :] <= row_index[:, None]
        allowed = jnp.concatenate([jnp.broadcast_to(visible, (q_rows, block_rows)), causal], axis=1)
        key_rows = jnp.concatenate([previous[0], keys], 0)
        value_rows = jnp.concatenate([previous[1], values], 0)
        results.append(attend_rows(q_block, key_rows, value_rows, allowed, heads_here))
    return jnp.concatenate(results, axis=0)


def solution(mesh):
    in_specs = (P(("ctx", "tp"), None), P(None, "tp"), P(None, "tp"), P(None, "tp"), P())
    out_specs = P("ctx", "tp")
    return jax.shard_map(body, mesh=mesh, in_specs=in_specs, out_specs=out_specs, check_vma=False)
```

profile of v0, /device:TPU:16, one launch (start us, length us, event | category | flops | bytes accessed | tf_op | source)
XLA Modules:
  0.0 141.4 jit_solution(9603754007117141902)
XLA Ops:
  6.5 0.0 copy-start
  6.5 0.0 all-gather.2.cloned.1.call-start
  6.5 0.7 all-gather.2.cloned.1.call-update
  7.3 0.0 copy-start.5
  7.3 59.0 %all-gather.2.cloned.1.call-done = bf16[1024,1024]{1,0:T(8,128)(2,1)} async-done(((bf16[256,1024]{1,0:T(8,128)(2,1)}), bf16[1024,1024]{1,0:T(8,128)(2,1)}) %all-gather.2.cloned.1.call-update) | async-done | bytes 2097168 | tf_op jit(solution)/shard_map/all_gather | solution.py:36
  66.2 0.0 copy-done
  66.2 2.3 %convolution_convert_fusion.2 = bf16[1024,256]{0,1:T(8,128)(2,1)S(1)} fusion(bf16[1024,1024]{1,0:T(8,128)(2,1)} %all-gather.2.cloned.1.call-done, bf16[1024,256]{1,0:T(8,128)(2,1)S(1)} %copy-done), kind=kOutput, calls=%fused_computation.22 | convolution fusion | flops 537133056 | bytes 3145728 | tf_op jit(solution)/shard_map/dot_general | solution.py:39
  68.6 2.4 %convolution_convert_fusion.1 = bf16[1024,256]{0,1:T(8,128)(2,1)S(1)} fusion(bf16[1024,1024]{1,0:T(8,128)(2,1)} %all-gather.2.cloned.1.call-done, bf16[1024,256]{1,0:T(8,128)(2,1)} %param.8), kind=kOutput, calls=%fused_computation.21 | convolution fusion | flops 537133056 | bytes 3145728 | tf_op jit(solution)/shard_map/dot_general | solution.py:39
  71.0 0.0 copy-start.3
  71.0 0.8 copy-done.3
  71.8 0.1 pad_maximum_fusion
  71.9 1.9 %collective-permute-start = (bf16[2,1024,256]{1,2,0:T(8,128)(2,1)S(1)}, bf16[2,1024,256]{1,2,0:T(8,128)(2,1)S(1)}, u32[]{:S(2)}, u32[]{:S(2)}) collective-permute-start(bf16[2,1024,256]{1,2,0:T(8,128)(2,1)S(1)} %pad_maximum_fusion), channel_id=1, source_target_pairs={{508,0},{0,4},{4,8},{8,12},{12,16},{16,20},{20,24},{24,28},{28,32}... | collective-permute-start | bytes 3145736 | tf_op jit(solution)/shard_map/ppermute | solution.py:12
  73.9 0.0 copy-done.5
  73.9 0.6 fusion.44
  75.7 0.1 iota_compare_fusion.1
  75.9 1.3 concatenate.30
  77.2 0.4 iota_compare_fusion
  77.6 1.3 concatenate.34
  78.9 1.0 copy.7
  79.9 2.4 %convolution_convert_fusion = bf16[1024,256]{0,1:T(8,128)(2,1)S(1)} fusion(bf16[1024,1024]{1,0:T(8,128)(2,1)} %all-gather.2.cloned.1.call-done, bf16[1024,256]{1,0:T(8,128)(2,1)} %param.6), kind=kOutput, calls=%fused_computation.20 | convolution fusion | flops 537133056 | bytes 3145728 | tf_op jit(solution)/shard_map/dot_general | solution.py:39
  82.3 0.7 fusion.43
  83.1 24.5 %collective-permute-done = bf16[2,1024,256]{1,2,0:T(8,128)(2,1)S(1)} collective-permute-done((bf16[2,1024,256]{1,2,0:T(8,128)(2,1)S(1)}, bf16[2,1024,256]{1,2,0:T(8,128)(2,1)S(1)}, u32[]{:S(2)}, u32[]{:S(2)}) %collective-permute-start) | collective-permute-done | bytes 1048608 | tf_op jit(solution)/shard_map/ppermute | solution.py:12
  107.6 0.9 fusion.42
  108.5 0.3 copy.6
  108.8 0.0 copy-start.4
  108.8 8.0 %fusion.46 = (f32[2,512]{1,0:T(2,128)S(1)}, bf16[2,512,2048]{2,1,0:T(8,128)(2,1)}) fusion(pred[512,2048]{1,0:T(8,128)(4,1)} %concatenate.30, bf16[512,2,128]{0,2,1:T(8,128)(2,1)S(1)} %bitcast.48, bf16[1024,2,128]{2,0,1:T(8,128)(2,1)} %copy.7, bf16[1024,2,128]{2,0,1:T(8,128)(2,1)S(1)} %copy.6), kind=kOutput, calls=%fused_computation.46 | convolution fusion | flops 551553024 | bytes 6557696 | tf_op jit(solution)/shard_map/sub | solution.py:24
  116.8 0.0 copy-start.1
  116.8 0.0 copy-start.2
  116.8 0.0 copy-done.4
  116.8 4.7 %fusion.29 = bf16[512,2,128]{0,2,1:T(8,128)(2,1)} fusion(bf16[2,512,2048]{2,1,0:T(8,128)(2,1)} %get-tuple-element.14, bf16[1024,2,128]{0,2,1:T(8,128)(2,1)S(1)} %bitcast.41, bf16[1024,2,128]{0,2,1:T(8,128)(2,1)} %bitcast.43, f32[512,2]{0,1:T(2,128)S(1)} %bitcast.50), kind=kOutput, calls=%fused_computation.28 | convolution fusion | flops 539230208 | bytes 5509120 | tf_op jit(solution)/shard_map/hqk,khd->qhd/dot_general | solution.py:26
  121.5 1.1 copy.10
  122.5 0.0 copy-done.1
  122.5 0.0 copy-done.2
  122.6 7.2 %fusion.45 = (f32[2,512]{1,0:T(2,128)S(1)}, bf16[2,512,2048]{2,1,0:T(8,128)(2,1)}) fusion(pred[512,2048]{1,0:T(8,128)(4,1)S(1)} %copy-done.1, bf16[512,2,128]{0,2,1:T(8,128)(2,1)} %bitcast.47, bf16[1024,2,128]{2,0,1:T(8,128)(2,1)S(1)} %copy-done.2, bf16[1024,2,128]{2,0,1:T(8,128)(2,1)S(1)} %copy.6), kind=kOutput, calls=%fused_computation.45 | convolution fusion | flops 551553024 | bytes 6557696 | tf_op jit(solution)/shard_map/sub | solution.py:24
  129.7 3.9 %fusion.26 = bf16[512,2,128]{0,2,1:T(8,128)(2,1)S(1)} fusion(bf16[2,512,2048]{2,1,0:T(8,128)(2,1)} %get-tuple-element.12, bf16[1024,2,128]{0,2,1:T(8,128)(2,1)S(1)} %bitcast.42, bf16[1024,2,128]{0,2,1:T(8,128)(2,1)} %bitcast.44, f32[512,2]{0,1:T(2,128)S(1)} %bitcast.49), kind=kOutput, calls=%fused_computation.27 | convolution fusion | flops 539230208 | bytes 5509120 | tf_op jit(solution)/shard_map/hqk,khd->qhd/dot_general | solution.py:26
  133.6 0.1 copy.11
  133.8 0.8 pad_maximum_fusion.5
  (1 shorter events, 0.0 us)
Async XLA Ops:
  6.5 59.7 %copy-start = (bf16[1024,256]{1,0:T(8,128)(2,1)S(1)}, bf16[1024,256]{1,0:T(8,128)(2,1)}, u32[]{:S(2)}) copy-start(bf16[1024,256]{1,0:T(8,128)(2,1)} %param.7) | copy-start | bytes 1572868
  6.5 59.7 %all-gather.2.cloned.1.call-start = ((), (), s32[]{:S(2)}) async-start(), calls=%async_computation | async-start | bytes 2621440 | tf_op jit(solution)/shard_map/all_gather | solution.py:36
  7.3 66.6 %copy-start.5 = (s32[128]{0:T(128)S(1)}, s32[128]{0:T(128)}, u32[]{:S(2)}) copy-start(s32[128]{0:T(128)} %param.9) | copy-start | bytes 1540
  71.0 0.8 copy-start.3
  71.9 35.7 %collective-permute-start = (bf16[2,1024,256]{1,2,0:T(8,128)(2,1)S(1)}, bf16[2,1024,256]{1,2,0:T(8,128)(2,1)S(1)}, u32[]{:S(2)}, u32[]{:S(2)}) collective-permute-start(bf16[2,1024,256]{1,2,0:T(8,128)(2,1)S(1)} %pad_maximum_fusion), channel_id=1, source_target_pairs={{508,0},{0,4},{4,8},{8,12},{12,16},{16,20},{20,24},{24,28},{28,32}... | collective-permute-start | bytes 3145736 | tf_op jit(solution)/shard_map/ppermute | solution.py:12
  108.8 8.0 %copy-start.4 = (bf16[1024,256]{0,1:T(8,128)(2,1)S(1)}, bf16[1024,256]{0,1:T(8,128)(2,1)}, u32[]{:S(2)}) copy-start(bf16[1024,256]{0,1:T(8,128)(2,1)} %copy-done.3) | copy-start | bytes 1572868
  116.8 5.8 %copy-start.1 = (pred[512,2048]{1,0:T(8,128)(4,1)S(1)}, pred[512,2048]{1,0:T(8,128)(4,1)}, u32[]{:S(2)}) copy-start(pred[512,2048]{1,0:T(8,128)(4,1)} %concatenate.34) | copy-start | bytes 3145732
  116.8 5.8 %copy-start.2 = (bf16[1024,2,128]{2,0,1:T(8,128)(2,1)S(1)}, bf16[1024,2,128]{2,0,1:T(8,128)(2,1)}, u32[]{:S(2)}) copy-start(bf16[1024,2,128]{2,0,1:T(8,128)(2,1)} %copy.7) | copy-start | bytes 1572868
Sparse Core Ops, SparseCore 0:
  9.5 56.7 all-gather.1
where the time goes:
time: 142 us; the launch traced here: 141 us
  waiting for transfers between devices  84.2 us (59%)
  matrix products  30.9 us (22%)
  between operations  14.8 us (10%)
  local copies, waits for them, and re-layouts  8.12 us (6%)
  starting transfers between devices  1.92 us (1%)
  other arithmetic  1.44 us (1%)
    all_gather x1, waiting for transfers between devices, body(): piece = lax.all_gather(series, 'tp', axis=0, tiled=True)  59 us
    ppermute x1, waiting for transfers between devices, passed_along(): return lax.ppermute(block, axis, route)  24.5 us
    sub x2, matrix products, attend_rows(): weights = jnp.where(allowed[None], jnp.exp(scores - top), jnp.float32(0.0))  15.2 us
    dot_general x2, matrix products, attend_rows(): jnp.einsum('hqk,khd->qhd', weights.astype(jnp.bfloat16), v_heads, preferr...  8.57 us
    dot_general x3, matrix products, body(): jnp.dot(piece, weight, preferred_element_type=jnp.float32)  7.19 us
  transfers between devices with their start and end apart: 2, of which 2 were waited for; matrix products, arithmetic and copies ran while one was open for 6% of the time, Pallas kernels for 0%

commit v1 on v0

v1 whole, which is shorter than its diff:
```python
import math

import jax
import jax.numpy as jnp
from jax import lax
from jax.experimental import pallas as pl
from jax.experimental.pallas import tpu as pltpu
from jax.sharding import PartitionSpec as P

HD = 128
HEADS = 2
WIDTH = HEADS * HD
CHUNK = 256
BLOCK = 4 * CHUNK
HEAD = 3 * CHUNK
DEPTH = 1024
SCALE = math.log2(math.e) / math.sqrt(HD)
ROW = 8

BF16 = jnp.bfloat16
F32 = jnp.float32
VMEM = pl.BlockSpec(memory_space=pltpu.VMEM)
SMEM = pl.BlockSpec(memory_space=pltpu.SMEM)
ANY = pl.BlockSpec(memory_space=pl.ANY)


def shape(rows, columns, dtype=BF16):
    return jax.ShapeDtypeStruct((rows, columns), dtype)


STATE = (shape(8, BLOCK, F32), shape(WIDTH, BLOCK, F32))


def run(body, out, specs, flops, *args, alias=None, scratch=()):
    return pl.pallas_call(
        body,
        out_shape=out,
        in_specs=specs,
        out_specs=jax.tree.map(lambda _: VMEM, out),
        scratch_shapes=list(scratch),
        input_output_aliases=alias or {},
        compiler_params=pltpu.CompilerParams(vmem_limit_bytes=20 << 20),
        cost_estimate=pl.CostEstimate(flops=flops, bytes_accessed=1 << 20, transcendentals=0),
    )(*args)


def dot(a, b, dims):
    return lax.dot_general(a, b, (dims, ((), ())), preferred_element_type=F32)


def project(rows, weight):
    return jnp.dot(rows, weight, preferred_element_type=F32).astype(BF16)


def head(number):
    return slice(number * HD, (number + 1) * HD)


def scores(keys, query):
    return dot(keys, query, ((1,), (1,))) * SCALE


def mixed(values, weights):
    return dot(values, weights.astype(BF16), ((0,), (0,)))


def positions(tp, chunks, axis):
    parts = []
    for chunk in chunks:
        size = (CHUNK, 1) if axis == 0 else (1, CHUNK)
        parts.append(lax.broadcasted_iota(jnp.int32, size, axis) + (tp ^ chunk) * CHUNK)
    return jnp.concatenate(parts, axis)


def first(found, values):
    top = jnp.max(found, axis=0, keepdims=True)
    weights = jnp.exp2(found - top)
    return top, jnp.sum(weights, axis=0, keepdims=True), mixed(values, weights)


def further(top0, total0, mix0, found, values):
    top = jnp.maximum(top0, jnp.max(found, axis=0, keepdims=True))
    weights = jnp.exp2(found - top)
    fade = jnp.exp2(top0 - top)
    total = total0 * fade + jnp.sum(weights, axis=0, keepdims=True)
    return top, total, mix0 * fade + mixed(values, weights)


def project_own_body(x, wq, wk, wv, q, kv):
    q[...] = project(x[...], wq[...])
    kv[:, :WIDTH] = project(x[...], wk[...])
    kv[:, WIDTH:] = project(x[...], wv[...])


def project_middle_body(xb, xc, qa, kva, wq, wk, wv, q, kv):
    q[:CHUNK] = qa[...]
    kv[:CHUNK] = kva[...]
    for place, x in ((1, xb), (2, xc)):
        rows = slice(place * CHUNK, (place + 1) * CHUNK)
        q[rows] = project(x[...], wq[...])
        kv[rows, :WIDTH] = project(x[...], wk[...])
        kv[rows, WIDTH:] = project(x[...], wv[...])


def project_last_body(info, outer, inner, wq, wk, wv, q, kv):
    middle = jnp.logical_or(info[0] == 1, info[0] == 2)
    x = jnp.where(middle, inner[...], outer[...])
    q[...] = project(x, wq[...])
    kv[:, :WIDTH] = project(x, wk[...])
    kv[:, WIDTH:] = project(x, wv[...])


def project_far_body(info, kva, xb, xc, xd, wk, wv, kv, x, w, sems):
    @pl.when(info[2] == 1)
    def _():
        copies = [pltpu.make_async_copy(source, x.at[n], sems.at[n]) for n, source in enumerate((xb, xc, xd))]
        copies += [pltpu.make_async_copy(source, w.at[n], sems.at[3 + n]) for n, source in enumerate((wk, wv))]
        copies.append(pltpu.make_async_copy(kva, kv.at[:CHUNK], sems.at[5]))
        for copy in copies:
            copy.start()
        for copy in copies:
            copy.wait()
        for n in range(3):
            rows = slice((n + 1) * CHUNK, (n + 2) * CHUNK)
            kv[rows, :WIDTH] = project(x[n], w[0])
            kv[rows, WIDTH:] = project(x[n], w[1])


def own_first_body(info, q, kv, state, mix):
    seen = positions(info[0], range(3), 0) <= positions(info[0], range(3), 1)
    for h in range(HEADS):
        found = jnp.where(seen, scores(kv[:, head(h)], q[:, head(h)]), -jnp.inf)
        top, total, part = first(found, kv[:, head(HEADS + h)])
        state[h : h + 1, :HEAD] = top
        state[HEADS + h : HEADS + h + 1, :HEAD] = total
        mix[head(h), :HEAD] = part


def before_first_body(info, q, near, far, state0, mix0, state, mix):
    @pl.when(info[1] == 1)
    def _():
        for h in range(HEADS):
            keys = jnp.where(info[2] == 1, far[:HEAD, head(h)], near[:, head(h)])
            values = jnp.where(info[2] == 1, far[:HEAD, head(HEADS + h)], near[:, head(HEADS + h)])
            top, total, part = further(
                state0[h : h + 1, :HEAD],
                state0[HEADS + h : HEADS + h + 1, :HEAD],
                mix0[head(h), :HEAD],
                scores(keys, q[:, head(h)]),
                values,
            )
            state[h : h + 1, :HEAD] = top
            state[HEADS + h : HEADS + h + 1, :HEAD] = total
            mix[head(h), :HEAD] = part

    @pl.when(info[1] == 0)
    def _():
        state[...] = state0[...]
        mix[...] = mix0[...]


def own_last_body(info, q, qd, kv, kvd, near, far, state0, mix0, state, mix):
    tp = info[0]
    seen = jnp.concatenate(
        [
            positions(tp, range(4), 0) <= positions(tp, (3,), 1),
            jnp.broadcast_to(info[1] == 1, (HEAD, CHUNK)),
        ],
        0,
    )
    seen_last = positions(tp, (3,), 0) <= positions(tp, range(3), 1)
    for h in range(HEADS):
        v = head(HEADS + h)
        keys = jnp.where(info[2] == 1, far[:HEAD, head(h)], near[:, head(h)])
        values = jnp.where(info[2] == 1, far[:HEAD, v], near[:, v])
        keys = jnp.concatenate([kv[:, head(h)], kvd[:, head(h)], keys], 0)
        values = jnp.concatenate([kv[:, v], kvd[:, v], values], 0)
        found = jnp.where(seen, scores(keys, qd[:, head(h)]), -jnp.inf)
        top, total, part = first(found, values)
        state[h : h + 1, HEAD:] = top
        state[HEADS + h : HEADS + h + 1, HEAD:] = total
        mix[head(h), HEAD:] = part
        top, total, part = further(
            state0[h : h + 1, :HEAD],
            state0[HEADS + h : HEADS + h + 1, :HEAD],
            mix0[head(h), :HEAD],
            jnp.where(seen_last, scores(kvd[:, head(h)], q[:, head(h)]), -jnp.inf),
            kvd[:, v],
        )
        state[h : h + 1, :HEAD] = top
        state[HEADS + h : HEADS + h + 1, :HEAD] = total
        mix[head(h), :HEAD] = part


def before_last_body(info, q, qd, near, far, state, mix, out):
    def store(h, total, part):
        part = (part / total).astype(BF16)
        for chunk in range(4):
            rows = pl.ds(pl.multiple_of((info[0] ^ chunk) * CHUNK, CHUNK), CHUNK)
            out[rows, head(h)] = part[:, chunk * CHUNK : (chunk + 1) * CHUNK].T

    for h in range(HEADS):
        total0 = state[HEADS + h : HEADS + h + 1, :]

        @pl.when(info[1] == 1)
        def _():
            v = head(HEADS + h)
            keys = jnp.where(info[2] == 1, far[HEAD:, head(h)], near[:, head(h)])
            values = jnp.where(info[2] == 1, far[HEAD:, v], near[:, v])
            query = jnp.concatenate([q[:, head(h)], qd[:, head(h)]], 0)
            _, total, part = further(state[h : h + 1, :], total0, mix[head(h), :], scores(keys, query), values)
            store(h, total, part)

        @pl.when(info[1] == 0)
        def _():
            store(h, total0, mix[head(h), :])


PAIR = 2 * 2 * HEADS * CHUNK * CHUNK * HD
TP = 4


def device(ctx, tp):
    return ctx * TP + tp


def line_ends(ctx_count):
    return [(i, (i + ctx_count - 1) % ctx_count) for i in range(0, ctx_count, ROW)]


def body(series, w_query, w_key, w_value, block_pos):
    ctx_count = lax.axis_size("ctx")
    here = lax.axis_index("ctx")
    tp = lax.axis_index("tp")
    before = (here + ctx_count - 1) % ctx_count
    visible = block_pos[before] < block_pos[here]
    far_here = here % ROW == 0
    info = jnp.stack([tp, visible.astype(jnp.int32), far_here.astype(jnp.int32)]).astype(jnp.int32)
    weights = (w_query, w_key, w_value)
    ends = line_ends(ctx_count)

    def swap(x, pairs):
        return lax.ppermute(x, "tp", pairs)

    def to_next(x):
        return lax.ppermute(x, "ctx", [(i - 1, i) for i in range(ctx_count) if i % ROW])

    def send(x, route):
        return lax.ppermute(x, ("ctx", "tp"), route)

    def aside(x, line, shards=range(TP), stay=()):
        route = [(device(last, t), device(last - ROW + 1 + line, t)) for _, last in ends for t in shards]
        return send(x, route + [(device(last, t), device(last, t)) for _, last in ends for t in stay])

    def across(x, chunk, line):
        return send(
            x,
            [(device(last - ROW + 1 + line(t ^ chunk), t ^ chunk), device(i, t)) for i, last in ends for t in range(TP)],
        )

    qa, kva = run(
        project_own_body,
        (shape(CHUNK, WIDTH), shape(CHUNK, 2 * WIDTH)),
        [VMEM] * 4,
        2 * CHUNK * DEPTH * 3 * WIDTH,
        series,
        *weights,
    )
    far_c = aside(series, 5)
    far_b = aside(series, 1, (1, 2), (0, 3))
    far_a = aside(kva, 3)
    xc = swap(series, [(t, t ^ 2) for t in range(TP)])
    xb = swap(series, [(t, t ^ 1) for t in range(TP)])
    far_d = across(series, 3, lambda t: 7)
    far_c = across(far_c, 2, lambda t: 5)
    far_b = across(far_b, 1, lambda t: 1 if t in (1, 2) else 7)
    far_a = across(far_a, 0, lambda t: 3)
    xc, xb, own = lax.optimization_barrier((xc, xb, series))
    outer = swap(xc, [(2, 3), (1, 0)])
    inner = swap(own, [(1, 2), (2, 1)])
    q, kv = run(
        project_middle_body,
        (shape(HEAD, WIDTH), shape(HEAD, 2 * WIDTH)),
        [VMEM] * 7,
        4 * CHUNK * DEPTH * 3 * WIDTH,
        xb,
        xc,
        qa,
        kva,
        *weights,
    )
    near = to_next(kv)
    state, mix = run(own_first_body, STATE, [SMEM] + [VMEM] * 2, 9 * PAIR, info, q, kv)
    kv_far = run(
        project_far_body,
        shape(BLOCK, 2 * WIDTH),
        [SMEM] + [ANY] * 6,
        8 * CHUNK * DEPTH * 2 * WIDTH,
        info,
        far_a,
        far_b,
        far_c,
        far_d,
        w_key,
        w_value,
        scratch=(
            pltpu.VMEM((3, CHUNK, DEPTH), BF16),
            pltpu.VMEM((2, DEPTH, WIDTH), BF16),
            pltpu.SemaphoreType.DMA((6,)),
        ),
    )
    outer, inner, kv_far = lax.optimization_barrier((outer, inner, kv_far))
    qd, kvd = run(
        project_last_body,
        (shape(CHUNK, WIDTH), shape(CHUNK, 2 * WIDTH)),
        [SMEM] + [VMEM] * 5,
        2 * CHUNK * DEPTH * 3 * WIDTH,
        info,
        outer,
        inner,
        *weights,
    )
    near_last = to_next(kvd)
    near, qd = lax.optimization_barrier((near, qd))
    state, mix = run(
        before_first_body,
        STATE,
        [SMEM] + [VMEM] * 5,
        9 * PAIR,
        info,
        q,
        near,
        kv_far,
        state,
        mix,
        alias={4: 0, 5: 1},
    )
    state, mix = run(
        own_last_body,
        STATE,
        [SMEM] + [VMEM] * 8,
        10 * PAIR,
        info,
        q,
        qd,
        kv,
        kvd,
        near,
        kv_far,
        state,
        mix,
        alias={7: 0, 8: 1},
    )
    return run(
        before_last_body,
        shape(BLOCK, WIDTH),
        [SMEM] + [VMEM] * 6,
        4 * PAIR,
        info,
        q,
        qd,
        near_last,
        kv_far,
        state,
        mix,
    )


def solution(mesh):
    in_specs = (P(("ctx", "tp"), None), P(None, "tp"), P(None, "tp"), P(None, "tp"), P())
    out_specs = P("ctx", "tp")
    return jax.shard_map(body, mesh=mesh, in_specs=in_specs, out_specs=out_specs, check_vma=False)
```

time: 142 us -> 89 us (0.63)
  the two profiles are of different devices: /device:TPU:16 before, /device:TPU:8 now
where the time goes in v1:
time: 89 us; the launch traced here: 88.1 us
  starting transfers between devices  33.7 us (38%)
  waiting for transfers between devices  23.9 us (27%)
  Pallas kernels  21.2 us (24%)
  local copies, waits for them, and re-layouts  7.84 us (9%)
  between operations  1.39 us (2%)
    pallas_call x8, Pallas kernels, run(): pl.pallas_call(body, out_shape=out, in_specs=specs, out_specs=jax.tree.ma...  21.2 us
    ppermute x4, starting transfers between devices, swap(): return lax.ppermute(x, 'tp', pairs)  14.3 us
    ppermute x4, waiting for transfers between devices, swap(): return lax.ppermute(x, 'tp', pairs)  13 us
    ppermute x7, waiting for transfers between devices, send(): return lax.ppermute(x, ('ctx', 'tp'), route)  10.9 us
    ppermute x2, starting transfers between devices, to_next(): lax.ppermute(x, 'ctx', [(i - 1, i) for i in range(ctx_count) if i % ROW])  10.7 us
    ppermute x7, starting transfers between devices, send(): return lax.ppermute(x, ('ctx', 'tp'), route)  8.74 us
    unnamed x22, local copies, waits for them, and re-layouts  7.25 us
  transfers between devices with their start and end apart: 13, of which 5 were waited for; matrix products, arithmetic and copies ran while one was open for 1% of the time, Pallas kernels for 21%

profile of v1, /device:TPU:8, one launch (start us, length us, event | category | flops | bytes accessed | tf_op | source)
XLA Modules:
  0.0 88.1 jit_solution(450871867542563135)
XLA Ops:
  0.0 4.5 %collective-permute-start = (bf16[256,1024]{1,0:T(8,128)(2,1)}, bf16[256,1024]{1,0:T(8,128)(2,1)}, u32[]{:S(2)}, u32[]{:S(2)}) collective-permute-start(bf16[256,1024]{1,0:T(8,128)(2,1)} %x.1), channel_id=1, source_target_pairs={{0,2},{1,3},{2,0},{3,1},{4,6},{5,7},{6,4},{7,5},{8,10},{9,11},{10,... | collective-permute-start | bytes 1572872 | tf_op jit(solution)/shard_map/ppermute | solution.py:243
  4.5 0.0 copy-start
  4.5 1.0 %copy-done = bf16[1024,256]{1,0:T(8,128)(2,1)S(1)} copy-done((bf16[1024,256]{1,0:T(8,128)(2,1)S(1)}, bf16[1024,256]{1,0:T(8,128)(2,1)}, u32[]{:S(2)}) %copy-start) | copy-done | bytes 524312
  5.5 0.0 copy-start.2
  5.5 1.0 %copy-done.2 = bf16[1024,256]{1,0:T(8,128)(2,1)S(1)} copy-done((bf16[1024,256]{1,0:T(8,128)(2,1)S(1)}, bf16[1024,256]{1,0:T(8,128)(2,1)}, u32[]{:S(2)}) %copy-start.2) | copy-done | bytes 524312
  6.6 0.0 copy-start.4
  6.6 1.0 %copy-done.4 = bf16[1024,256]{1,0:T(8,128)(2,1)S(1)} copy-done((bf16[1024,256]{1,0:T(8,128)(2,1)S(1)}, bf16[1024,256]{1,0:T(8,128)(2,1)}, u32[]{:S(2)}) %copy-start.4) | copy-done | bytes 524312
  7.6 0.0 copy-start.1
  7.6 0.0 copy-start.3
  7.6 0.0 copy-start.5
  7.6 1.7 %shard_map.55 = (bf16[256,256]{1,0:T(8,128)(2,1)S(1)}, bf16[256,512]{1,0:T(8,128)(2,1)S(1)}) custom-call(bf16[256,1024]{1,0:T(8,128)(2,1)} %x.1, bf16[1024,256]{1,0:T(8,128)(2,1)S(1)} %copy-done, bf16[1024,256]{1,0:T(8,128)(2,1)S(1)} %copy-done.2, bf16[1024,256]{1,0:T(8,128)(2,1)S(1)} %copy-done.4), custom_call_target="tpu_custom_call" | custom-call | flops 402653184 | bytes 1048576 | tf_op jit(solution)/shard_map/pallas_call | solution.py:35
  9.4 0.7 collective-permute-start.5
  10.1 5.2 %collective-permute-start.1 = (bf16[256,1024]{1,0:T(8,128)(2,1)}, bf16[256,1024]{1,0:T(8,128)(2,1)S(1)}, u32[]{:S(2)}, u32[]{:S(2)}) collective-permute-start(bf16[256,1024]{1,0:T(8,128)(2,1)} %x.1), channel_id=1, source_target_pairs={{0,1},{1,0},{2,3},{3,2},{4,5},{5,4},{6,7},{7,6},{8,9},{9,8},{10,11... | collective-permute-start | bytes 1572872 | tf_op jit(solution)/shard_map/ppermute | solution.py:243
  15.2 1.5 %collective-permute-start.9 = (bf16[256,1024]{1,0:T(8,128)(2,1)}, bf16[256,1024]{1,0:T(8,128)(2,1)}, u32[]{:S(2)}, u32[]{:S(2)}) collective-permute-start(bf16[256,1024]{1,0:T(8,128)(2,1)} %x.1), channel_id=1, source_target_pairs={{508,500},{509,501},{510,502},{511,503},{28,20},{29,21},{30,22},{3... | collective-permute-start | bytes 1572872 | tf_op jit(solution)/shard_map/ppermute | solution.py:249
  16.7 1.4 %collective-permute-start.7 = (bf16[256,1024]{1,0:T(8,128)(2,1)}, bf16[256,1024]{1,0:T(8,128)(2,1)}, u32[]{:S(2)}, u32[]{:S(2)}) collective-permute-start(bf16[256,1024]{1,0:T(8,128)(2,1)} %x.1), channel_id=1, source_target_pairs={{509,485},{510,486},{29,5},{30,6},{61,37},{62,38},{93,69},{94,70},... | collective-permute-start | bytes 1572872 | tf_op jit(solution)/shard_map/ppermute | solution.py:249
  18.2 0.0 collective-permute-done.5
  18.2 1.3 %collective-permute-start.11 = (bf16[256,1024]{1,0:T(8,128)(2,1)}, bf16[256,1024]{1,0:T(8,128)(2,1)S(1)}, u32[]{:S(2)}, u32[]{:S(2)}) collective-permute-start(bf16[256,1024]{1,0:T(8,128)(2,1)} %x.1), channel_id=1, source_target_pairs={{511,0},{510,1},{509,2},{508,3},{31,32},{30,33},{29,34},{28,35},{6... | collective-permute-start | bytes 1572872 | tf_op jit(solution)/shard_map/ppermute | solution.py:249
  19.4 7.8 %collective-permute-done.xc = bf16[256,1024]{1,0:T(8,128)(2,1)} collective-permute-done((bf16[256,1024]{1,0:T(8,128)(2,1)}, bf16[256,1024]{1,0:T(8,128)(2,1)}, u32[]{:S(2)}, u32[]{:S(2)}) %collective-permute-start) | collective-permute-done | bytes 524320 | tf_op jit(solution)/shard_map/ppermute | solution.py:243
  27.2 1.3 %collective-permute-start.6 = (bf16[256,512]{1,0:T(8,128)(2,1)S(1)}, bf16[256,512]{1,0:T(8,128)(2,1)S(1)}, u32[]{:S(2)}, u32[]{:S(2)}) collective-permute-start(bf16[256,512]{1,0:T(8,128)(2,1)S(1)} %collective-permute-done.5), channel_id=1, source_target_pairs={{492,0},{493,1},{494,2},{495,3},{12,32},{13,33},{14,34},{15,35},{4... | collective-permute-start | bytes 786440 | tf_op jit(solution)/shard_map/ppermute | solution.py:249
  28.5 5.2 %collective-permute-done.1.xb = bf16[256,1024]{1,0:T(8,128)(2,1)S(1)} collective-permute-done((bf16[256,1024]{1,0:T(8,128)(2,1)}, bf16[256,1024]{1,0:T(8,128)(2,1)S(1)}, u32[]{:S(2)}, u32[]{:S(2)}) %collective-permute-start.1) | collective-permute-done | bytes 524320 | tf_op jit(solution)/shard_map/ppermute | solution.py:243
  33.7 0.0 collective-permute-done.9
  33.7 1.3 %collective-permute-start.10 = (bf16[256,1024]{1,0:T(8,128)(2,1)}, bf16[256,1024]{1,0:T(8,128)(2,1)}, u32[]{:S(2)}, u32[]{:S(2)}) collective-permute-start(bf16[256,1024]{1,0:T(8,128)(2,1)} %collective-permute-done.9), channel_id=1, source_target_pairs={{502,0},{503,1},{500,2},{501,3},{22,32},{23,33},{20,34},{21,35},{5... | collective-permute-start | bytes 1572872 | tf_op jit(solution)/shard_map/ppermute | solution.py:249
  35.0 0.0 collective-permute-done.7
  35.0 1.3 %collective-permute-start.8 = (bf16[256,1024]{1,0:T(8,128)(2,1)}, bf16[256,1024]{1,0:T(8,128)(2,1)}, u32[]{:S(2)}, u32[]{:S(2)}) collective-permute-start(bf16[256,1024]{1,0:T(8,128)(2,1)} %collective-permute-done.7), channel_id=1, source_target_pairs={{485,0},{508,1},{511,2},{486,3},{5,32},{28,33},{31,34},{6,35},{37,... | collective-permute-start | bytes 1572872 | tf_op jit(solution)/shard_map/ppermute | solution.py:249
  36.3 0.0 copy-done.1
  36.3 0.0 copy-done.3
  36.3 0.0 copy-done.5
  36.3 2.0 %shard_map.56 = (bf16[768,256]{1,0:T(8,128)(2,1)S(1)}, bf16[768,512]{1,0:T(8,128)(2,1)S(1)}) custom-call(bf16[256,1024]{1,0:T(8,128)(2,1)S(1)} %collective-permute-done.1.xb, bf16[256,1024]{1,0:T(8,128)(2,1)} %collective-permute-done.xc, bf16[256,256]{1,0:T(8,128)(2,1)S(1)} %get-tuple-element.27.qa, bf16[256,512]{1,0:T(8,128)(2,1)S(1)} %get-tuple-element.28.kva, ...), custom_call_target="tpu_custom_call" | custom-call | flops 805306368 | bytes 1048576 | tf_op jit(solution)/shard_map/pallas_call | solution.py:35
  38.4 9.4 %collective-permute-start.2 = (bf16[768,512]{1,0:T(8,128)(2,1)S(1)}, bf16[768,512]{1,0:T(8,128)(2,1)S(1)}, u32[]{:S(2)}, u32[]{:S(2)}) collective-permute-start(bf16[768,512]{1,0:T(8,128)(2,1)S(1)} %get-tuple-element.30.kv), channel_id=1, source_target_pairs={{0,4},{4,8},{8,12},{12,16},{16,20},{20,24},{24,28},{32,36},{36,40}... | collective-permute-start | bytes 2359304 | tf_op jit(solution)/shard_map/ppermute | solution.py:246
  47.7 6.9 %collective-permute-done.6.kva = bf16[256,512]{1,0:T(8,128)(2,1)S(1)} collective-permute-done((bf16[256,512]{1,0:T(8,128)(2,1)S(1)}, bf16[256,512]{1,0:T(8,128)(2,1)S(1)}, u32[]{:S(2)}, u32[]{:S(2)}) %collective-permute-start.6) | collective-permute-done | bytes 262176 | tf_op jit(solution)/shard_map/ppermute | solution.py:249
  54.7 0.0 copy-start.8
  54.7 0.7 copy-done.8
  55.3 2.1 %collective-permute-start.3 = (bf16[256,1024]{1,0:T(8,128)(2,1)}, bf16[256,1024]{1,0:T(8,128)(2,1)}, u32[]{:S(2)}, u32[]{:S(2)}) collective-permute-start(bf16[256,1024]{1,0:T(8,128)(2,1)} %collective-permute-done.xc), channel_id=1, source_target_pairs={{2,3},{1,0},{6,7},{5,4},{10,11},{9,8},{14,15},{13,12},{18,19},{17,... | collective-permute-start | bytes 1572872 | tf_op jit(solution)/shard_map/ppermute | solution.py:243
  57.4 0.0 collective-permute-done.11.xd
  57.4 0.0 copy-start.6
  57.4 0.8 copy-done.6
  58.2 2.6 %collective-permute-start.4 = (bf16[256,1024]{1,0:T(8,128)(2,1)}, bf16[256,1024]{1,0:T(8,128)(2,1)}, u32[]{:S(2)}, u32[]{:S(2)}) collective-permute-start(bf16[256,1024]{1,0:T(8,128)(2,1)} %x.1), channel_id=1, source_target_pairs={{1,2},{2,1},{5,6},{6,5},{9,10},{10,9},{13,14},{14,13},{17,18},{18,... | collective-permute-start | bytes 1572872 | tf_op jit(solution)/shard_map/ppermute | solution.py:243
  60.8 0.0 copy-start.10
  60.9 0.6 copy-done.10
  61.5 0.6 fusion
  63.2 0.1 pad_add_fusion.info
  63.3 3.6 %collective-permute-done.10.xc = bf16[256,1024]{1,0:T(8,128)(2,1)} collective-permute-done((bf16[256,1024]{1,0:T(8,128)(2,1)}, bf16[256,1024]{1,0:T(8,128)(2,1)}, u32[]{:S(2)}, u32[]{:S(2)}) %collective-permute-start.10) | collective-permute-done | bytes 524320 | tf_op jit(solution)/shard_map/ppermute | solution.py:249
  66.9 0.4 collective-permute-done.8.xb
  67.3 0.0 copy-start.7
  67.3 1.0 %copy-done.7 = bf16[256,1024]{1,0:T(8,128)(2,1)S(1)} copy-done((bf16[256,1024]{1,0:T(8,128)(2,1)S(1)}, bf16[256,1024]{1,0:T(8,128)(2,1)}, u32[]{:S(2)}) %copy-start.7) | copy-done | bytes 524312
  68.3 0.0 copy-start.9
  68.3 0.9 %copy-done.9 = bf16[256,512]{1,0:T(8,128)(2,1)S(1)} copy-done((bf16[256,512]{1,0:T(8,128)(2,1)S(1)}, bf16[256,512]{1,0:T(8,128)(2,1)}, u32[]{:S(2)}) %copy-start.9) | copy-done | bytes 262168
  69.3 2.8 %shard_map.57.far = bf16[1024,512]{1,0:T(8,128)(2,1)S(1)} custom-call(s32[3]{0:T(128)S(1)} %pad_add_fusion.info, bf16[256,512]{1,0:T(8,128)(2,1)S(1)} %copy-done.9, bf16[256,1024]{1,0:T(8,128)(2,1)} %collective-permute-done.8.xb, bf16[256,1024]{1,0:T(8,128)(2,1)} %collective-permute-done.10.xc, bf16[256,1024]{1,0:T(8,128)(2,1)S(1)} %copy-done.7, ...), custom_call_target="tpu_custom_call" | custom-call | flops 1073741824 | bytes 1048576 | tf_op jit(solution)/shard_map/pallas_call | solution.py:35
  72.1 0.0 collective-permute-done.3.outer
  72.1 0.0 collective-permute-done.4.inner
  72.1 1.8 %shard_map.58 = (bf16[256,256]{1,0:T(8,128)(2,1)S(1)}, bf16[256,512]{1,0:T(8,128)(2,1)S(1)}) custom-call(s32[3]{0:T(128)S(1)} %pad_add_fusion.info, bf16[256,1024]{1,0:T(8,128)(2,1)} %collective-permute-done.3.outer, bf16[256,1024]{1,0:T(8,128)(2,1)} %collective-permute-done.4.inner, bf16[1024,256]{1,0:T(8,128)(2,1)S(1)} %copy-done.1, ...), custom_call_target="tpu_custom_call" | custom-call | flops 402653184 | bytes 1048576 | tf_op jit(solution)/shard_map/pallas_call | solution.py:35
  73.9 1.3 %collective-permute-start.12 = (bf16[256,512]{1,0:T(8,128)(2,1)S(1)}, bf16[256,512]{1,0:T(8,128)(2,1)S(1)}, u32[]{:S(2)}, u32[]{:S(2)}) collective-permute-start(bf16[256,512]{1,0:T(8,128)(2,1)S(1)} %get-tuple-element.36.kvd), channel_id=1, source_target_pairs={{0,4},{4,8},{8,12},{12,16},{16,20},{20,24},{24,28},{32,36},{36,40}... | collective-permute-start | bytes 786440 | tf_op jit(solution)/shard_map/ppermute | solution.py:246
  75.2 2.5 %shard_map.59 = (f32[8,1024]{1,0:T(8,128)S(1)}, f32[256,1024]{1,0:T(8,128)S(1)}) custom-call(s32[3]{0:T(128)S(1)} %pad_add_fusion.info, bf16[768,256]{1,0:T(8,128)(2,1)S(1)} %get-tuple-element.29.q, bf16[768,512]{1,0:T(8,128)(2,1)S(1)} %get-tuple-element.30.kv), custom_call_target="tpu_custom_call" | custom-call | flops 603979776 | bytes 1048576 | tf_op jit(solution)/shard_map/pallas_call | solution.py:35
  77.7 0.0 collective-permute-done.2.near
  77.7 3.3 %shard_map.60 = (f32[8,1024]{1,0:T(8,128)S(1)}, f32[256,1024]{1,0:T(8,128)S(1)}) custom-call(s32[3]{0:T(128)S(1)} %pad_add_fusion.info, bf16[768,256]{1,0:T(8,128)(2,1)S(1)} %get-tuple-element.29.q, bf16[768,512]{1,0:T(8,128)(2,1)S(1)} %collective-permute-done.2.near, ...), custom_call_target="tpu_custom_call", output_to_operand_aliasing={{0}: (4, {}), {1}: (5, {})} | custom-call | flops 603979776 | bytes 1048576 | tf_op jit(solution)/shard_map/pallas_call | solution.py:35
  81.0 4.1 %shard_map.61 = (f32[8,1024]{1,0:T(8,128)S(1)}, f32[256,1024]{1,0:T(8,128)S(1)}) custom-call(s32[3]{0:T(128)S(1)} %pad_add_fusion.info, bf16[768,256]{1,0:T(8,128)(2,1)S(1)} %get-tuple-element.29.q, bf16[256,256]{1,0:T(8,128)(2,1)S(1)} %get-tuple-element.35.qd, ...), custom_call_target="tpu_custom_call", output_to_operand_aliasing={{0}: (7, {}), {1}: (8, {})} | custom-call | flops 671088640 | bytes 1048576 | tf_op jit(solution)/shard_map/pallas_call | solution.py:35
  85.1 0.0 collective-permute-done.12.near
  85.1 3.0 %shard_map.62 = bf16[1024,256]{1,0:T(8,128)(2,1)} custom-call(s32[3]{0:T(128)S(1)} %pad_add_fusion.info, bf16[768,256]{1,0:T(8,128)(2,1)S(1)} %get-tuple-element.29.q, bf16[256,256]{1,0:T(8,128)(2,1)S(1)} %get-tuple-element.35.qd, bf16[256,512]{1,0:T(8,128)(2,1)S(1)} %collective-permute-done.12.near, bf16[1024,512]{1,0:T(8,128)(2,1)S(1)} %shard_map.57.far, ...), custom_call_target="tpu_custom_call" | custom-call | flops 268435456 | bytes 1048576 | tf_op jit(solution)/shard_map/pallas_call | solution.py:35
Async XLA Ops:
  0.0 27.2 %collective-permute-start = (bf16[256,1024]{1,0:T(8,128)(2,1)}, bf16[256,1024]{1,0:T(8,128)(2,1)}, u32[]{:S(2)}, u32[]{:S(2)}) collective-permute-start(bf16[256,1024]{1,0:T(8,128)(2,1)} %x.1), channel_id=1, source_target_pairs={{0,2},{1,3},{2,0},{3,1},{4,6},{5,7},{6,4},{7,5},{8,10},{9,11},{10,... | collective-permute-start | bytes 1572872 | tf_op jit(solution)/shard_map/ppermute | solution.py:243
  4.5 1.0 %copy-start = (bf16[1024,256]{1,0:T(8,128)(2,1)S(1)}, bf16[1024,256]{1,0:T(8,128)(2,1)}, u32[]{:S(2)}) copy-start(bf16[1024,256]{1,0:T(8,128)(2,1)} %wq.5) | copy-start | bytes 1572868
  5.5 1.0 %copy-start.2 = (bf16[1024,256]{1,0:T(8,128)(2,1)S(1)}, bf16[1024,256]{1,0:T(8,128)(2,1)}, u32[]{:S(2)}) copy-start(bf16[1024,256]{1,0:T(8,128)(2,1)} %wk.7) | copy-start | bytes 1572868
  6.6 1.0 %copy-start.4 = (bf16[1024,256]{1,0:T(8,128)(2,1)S(1)}, bf16[1024,256]{1,0:T(8,128)(2,1)}, u32[]{:S(2)}) copy-start(bf16[1024,256]{1,0:T(8,128)(2,1)} %wv.7) | copy-start | bytes 1572868
  7.6 28.7 %copy-start.1 = (bf16[1024,256]{1,0:T(8,128)(2,1)S(1)}, bf16[1024,256]{1,0:T(8,128)(2,1)}, u32[]{:S(2)}) copy-start(bf16[1024,256]{1,0:T(8,128)(2,1)} %wq.5) | copy-start | bytes 1572868
  7.6 28.7 %copy-start.3 = (bf16[1024,256]{1,0:T(8,128)(2,1)S(1)}, bf16[1024,256]{1,0:T(8,128)(2,1)}, u32[]{:S(2)}) copy-start(bf16[1024,256]{1,0:T(8,128)(2,1)} %wk.7) | copy-start | bytes 1572868
  7.6 28.7 %copy-start.5 = (bf16[1024,256]{1,0:T(8,128)(2,1)S(1)}, bf16[1024,256]{1,0:T(8,128)(2,1)}, u32[]{:S(2)}) copy-start(bf16[1024,256]{1,0:T(8,128)(2,1)} %wv.7) | copy-start | bytes 1572868
  9.4 8.8 %collective-permute-start.5 = (bf16[256,512]{1,0:T(8,128)(2,1)S(1)}, bf16[256,512]{1,0:T(8,128)(2,1)S(1)}, u32[]{:S(2)}, u32[]{:S(2)}) collective-permute-start(bf16[256,512]{1,0:T(8,128)(2,1)S(1)} %get-tuple-element.28.kva), channel_id=1, source_target_pairs={{508,492},{509,493},{510,494},{511,495},{28,12},{29,13},{30,14},{3... | collective-permute-start | bytes 786440 | tf_op jit(solution)/shard_map/ppermute | solution.py:249
  10.1 23.6 %collective-permute-start.1 = (bf16[256,1024]{1,0:T(8,128)(2,1)}, bf16[256,1024]{1,0:T(8,128)(2,1)S(1)}, u32[]{:S(2)}, u32[]{:S(2)}) collective-permute-start(bf16[256,1024]{1,0:T(8,128)(2,1)} %x.1), channel_id=1, source_target_pairs={{0,1},{1,0},{2,3},{3,2},{4,5},{5,4},{6,7},{7,6},{8,9},{9,8},{10,11... | collective-permute-start | bytes 1572872 | tf_op jit(solution)/shard_map/ppermute | solution.py:243
  15.2 18.5 %collective-permute-start.9 = (bf16[256,1024]{1,0:T(8,128)(2,1)}, bf16[256,1024]{1,0:T(8,128)(2,1)}, u32[]{:S(2)}, u32[]{:S(2)}) collective-permute-start(bf16[256,1024]{1,0:T(8,128)(2,1)} %x.1), channel_id=1, source_target_pairs={{508,500},{509,501},{510,502},{511,503},{28,20},{29,21},{30,22},{3... | collective-permute-start | bytes 1572872 | tf_op jit(solution)/shard_map/ppermute | solution.py:249
  16.7 18.3 %collective-permute-start.7 = (bf16[256,1024]{1,0:T(8,128)(2,1)}, bf16[256,1024]{1,0:T(8,128)(2,1)}, u32[]{:S(2)}, u32[]{:S(2)}) collective-permute-start(bf16[256,1024]{1,0:T(8,128)(2,1)} %x.1), channel_id=1, source_target_pairs={{509,485},{510,486},{29,5},{30,6},{61,37},{62,38},{93,69},{94,70},... | collective-permute-start | bytes 1572872 | tf_op jit(solution)/shard_map/ppermute | solution.py:249
  18.2 39.3 %collective-permute-start.11 = (bf16[256,1024]{1,0:T(8,128)(2,1)}, bf16[256,1024]{1,0:T(8,128)(2,1)S(1)}, u32[]{:S(2)}, u32[]{:S(2)}) collective-permute-start(bf16[256,1024]{1,0:T(8,128)(2,1)} %x.1), channel_id=1, source_target_pairs={{511,0},{510,1},{509,2},{508,3},{31,32},{30,33},{29,34},{28,35},{6... | collective-permute-start | bytes 1572872 | tf_op jit(solution)/shard_map/ppermute | solution.py:249
  27.2 27.5 %collective-permute-start.6 = (bf16[256,512]{1,0:T(8,128)(2,1)S(1)}, bf16[256,512]{1,0:T(8,128)(2,1)S(1)}, u32[]{:S(2)}, u32[]{:S(2)}) collective-permute-start(bf16[256,512]{1,0:T(8,128)(2,1)S(1)} %collective-permute-done.5), channel_id=1, source_target_pairs={{492,0},{493,1},{494,2},{495,3},{12,32},{13,33},{14,34},{15,35},{4... | collective-permute-start | bytes 786440 | tf_op jit(solution)/shard_map/ppermute | solution.py:249
  33.7 33.2 %collective-permute-start.10 = (bf16[256,1024]{1,0:T(8,128)(2,1)}, bf16[256,1024]{1,0:T(8,128)(2,1)}, u32[]{:S(2)}, u32[]{:S(2)}) collective-permute-start(bf16[256,1024]{1,0:T(8,128)(2,1)} %collective-permute-done.9), channel_id=1, source_target_pairs={{502,0},{503,1},{500,2},{501,3},{22,32},{23,33},{20,34},{21,35},{5... | collective-permute-start | bytes 1572872 | tf_op jit(solution)/shard_map/ppermute | solution.py:249
  35.0 32.3 %collective-permute-start.8 = (bf16[256,1024]{1,0:T(8,128)(2,1)}, bf16[256,1024]{1,0:T(8,128)(2,1)}, u32[]{:S(2)}, u32[]{:S(2)}) collective-permute-start(bf16[256,1024]{1,0:T(8,128)(2,1)} %collective-permute-done.7), channel_id=1, source_target_pairs={{485,0},{508,1},{511,2},{486,3},{5,32},{28,33},{31,34},{6,35},{37,... | collective-permute-start | bytes 1572872 | tf_op jit(solution)/shard_map/ppermute | solution.py:249
  38.4 39.3 %collective-permute-start.2 = (bf16[768,512]{1,0:T(8,128)(2,1)S(1)}, bf16[768,512]{1,0:T(8,128)(2,1)S(1)}, u32[]{:S(2)}, u32[]{:S(2)}) collective-permute-start(bf16[768,512]{1,0:T(8,128)(2,1)S(1)} %get-tuple-element.30.kv), channel_id=1, source_target_pairs={{0,4},{4,8},{8,12},{12,16},{16,20},{20,24},{24,28},{32,36},{36,40}... | collective-permute-start | bytes 2359304 | tf_op jit(solution)/shard_map/ppermute | solution.py:246
  54.7 0.7 copy-start.8
  55.3 16.7 %collective-permute-start.3 = (bf16[256,1024]{1,0:T(8,128)(2,1)}, bf16[256,1024]{1,0:T(8,128)(2,1)}, u32[]{:S(2)}, u32[]{:S(2)}) collective-permute-start(bf16[256,1024]{1,0:T(8,128)(2,1)} %collective-permute-done.xc), channel_id=1, source_target_pairs={{2,3},{1,0},{6,7},{5,4},{10,11},{9,8},{14,15},{13,12},{18,19},{17,... | collective-permute-start | bytes 1572872 | tf_op jit(solution)/shard_map/ppermute | solution.py:243
  57.4 0.8 copy-start.6
  58.2 13.8 %collective-permute-start.4 = (bf16[256,1024]{1,0:T(8,128)(2,1)}, bf16[256,1024]{1,0:T(8,128)(2,1)}, u32[]{:S(2)}, u32[]{:S(2)}) collective-permute-start(bf16[256,1024]{1,0:T(8,128)(2,1)} %x.1), channel_id=1, source_target_pairs={{1,2},{2,1},{5,6},{6,5},{9,10},{10,9},{13,14},{14,13},{17,18},{18,... | collective-permute-start | bytes 1572872 | tf_op jit(solution)/shard_map/ppermute | solution.py:243
  60.8 0.7 copy-start.10
  67.3 1.0 %copy-start.7 = (bf16[256,1024]{1,0:T(8,128)(2,1)S(1)}, bf16[256,1024]{1,0:T(8,128)(2,1)}, u32[]{:S(2)}) copy-start(bf16[256,1024]{1,0:T(8,128)(2,1)} %copy-done.6) | copy-start | bytes 1572868
  68.3 0.9 %copy-start.9 = (bf16[256,512]{1,0:T(8,128)(2,1)S(1)}, bf16[256,512]{1,0:T(8,128)(2,1)}, u32[]{:S(2)}) copy-start(bf16[256,512]{1,0:T(8,128)(2,1)} %copy-done.8) | copy-start | bytes 786436
  73.9 11.3 %collective-permute-start.12 = (bf16[256,512]{1,0:T(8,128)(2,1)S(1)}, bf16[256,512]{1,0:T(8,128)(2,1)S(1)}, u32[]{:S(2)}, u32[]{:S(2)}) collective-permute-start(bf16[256,512]{1,0:T(8,128)(2,1)S(1)} %get-tuple-element.36.kvd), channel_id=1, source_target_pairs={{0,4},{4,8},{8,12},{12,16},{16,20},{20,24},{24,28},{32,36},{36,40}... | collective-permute-start | bytes 786440 | tf_op jit(solution)/shard_map/ppermute | solution.py:246

commit v2 on v1

v2 whole, which is shorter than its diff:
```python
import math

import jax
import jax.numpy as jnp
from jax import lax
from jax.experimental import pallas as pl
from jax.experimental.pallas import tpu as pltpu
from jax.sharding import PartitionSpec as P

HD = 128
HEADS = 2
WIDTH = HEADS * HD
CHUNK = 256
BLOCK = 4 * CHUNK
HEAD = 3 * CHUNK
DEPTH = 1024
SCALE = math.log2(math.e) / math.sqrt(HD)
ROW = 8
LAST = ROW - 1
LEAVE = (None, (3, 1, 1, 3), (5,) * 4, (LAST, 3, 3, LAST))

BF16 = jnp.bfloat16
F32 = jnp.float32
VMEM = pl.BlockSpec(memory_space=pltpu.VMEM)
SMEM = pl.BlockSpec(memory_space=pltpu.SMEM)
ANY = pl.BlockSpec(memory_space=pl.ANY)


def shape(rows, columns, dtype=BF16):
    return jax.ShapeDtypeStruct((rows, columns), dtype)


STATE = (shape(8, BLOCK, F32), shape(WIDTH, BLOCK, F32))


def run(name, body, out, specs, flops, *args, alias=None, scratch=(), out_specs=None):
    call = pl.pallas_call(
        body,
        out_shape=out,
        in_specs=specs,
        out_specs=out_specs or jax.tree.map(lambda _: VMEM, out),
        scratch_shapes=list(scratch),
        input_output_aliases=alias or {},
        compiler_params=pltpu.CompilerParams(vmem_limit_bytes=20 << 20),
        cost_estimate=pl.CostEstimate(flops=flops, bytes_accessed=0, transcendentals=0),
    )
    with jax.named_scope("n_" + name):
        return call(*args)


def dot(a, b, dims):
    return lax.dot_general(a, b, (dims, ((), ())), preferred_element_type=F32)


def project(rows, weight):
    return jnp.dot(rows, weight, preferred_element_type=F32).astype(BF16)


def head(number):
    return slice(number * HD, (number + 1) * HD)


def scores(keys, query):
    return dot(keys, query, ((1,), (1,))) * SCALE


def mixed(values, weights):
    return dot(values, weights.astype(BF16), ((0,), (0,)))


def positions(tp, chunks, axis):
    parts = []
    for chunk in chunks:
        size = (CHUNK, 1) if axis == 0 else (1, CHUNK)
        parts.append(lax.broadcasted_iota(jnp.int32, size, axis) + (tp ^ chunk) * CHUNK)
    return jnp.concatenate(parts, axis)


def first(found, values):
    top = jnp.max(found, axis=0, keepdims=True)
    weights = jnp.exp2(found - top)
    return top, jnp.sum(weights, axis=0, keepdims=True), mixed(values, weights)


def further(top0, total0, mix0, found, values):
    top = jnp.maximum(top0, jnp.max(found, axis=0, keepdims=True))
    weights = jnp.exp2(found - top)
    fade = jnp.exp2(top0 - top)
    total = total0 * fade + jnp.sum(weights, axis=0, keepdims=True)
    return top, total, mix0 * fade + mixed(values, weights)


def project_own_body(info, x, wq, wk, wv, q, kv):
    q[...] = project(x[...], wq[...])
    kv[:, :WIDTH] = project(x[...], wk[...])
    kv[:, WIDTH:] = project(x[...], wv[...])


def project_middle_body(xb, xc, qa, kva, wq, wk, wv, q, kv):
    q[:CHUNK] = qa[...]
    kv[:CHUNK] = kva[...]
    for place, x in ((1, xb), (2, xc)):
        rows = slice(place * CHUNK, (place + 1) * CHUNK)
        q[rows] = project(x[...], wq[...])
        kv[rows, :WIDTH] = project(x[...], wk[...])
        kv[rows, WIDTH:] = project(x[...], wv[...])


def project_last_body(info, outer, inner, wq, wk, wv, q, kv):
    middle = jnp.logical_or(info[0] == 1, info[0] == 2)
    x = jnp.where(middle, inner[...], outer[...])
    q[...] = project(x, wq[...])
    kv[:, :WIDTH] = project(x, wk[...])
    kv[:, WIDTH:] = project(x, wv[...])


def project_far_body(info, kva, xb, xc, xd, wk, wv, kv, kvd, x, w, sems):
    @pl.when(info[2] == 1)
    def _():
        copies = [pltpu.make_async_copy(source, x.at[n], sems.at[n]) for n, source in enumerate((xb, xc, xd))]
        copies += [pltpu.make_async_copy(source, w.at[n], sems.at[3 + n]) for n, source in enumerate((wk, wv))]
        copies.append(pltpu.make_async_copy(kva, kv.at[:CHUNK], sems.at[5]))
        for copy in copies:
            copy.start()
        for copy in copies:
            copy.wait()
        for n in range(3):
            out, rows = (kv, slice((n + 1) * CHUNK, (n + 2) * CHUNK)) if n < 2 else (kvd, slice(0, CHUNK))
            out[rows, :WIDTH] = project(x[n], w[0])
            out[rows, WIDTH:] = project(x[n], w[1])


def own_first_body(info, q, kv, state, mix):
    seen = positions(info[0], range(3), 0) <= positions(info[0], range(3), 1)
    for h in range(HEADS):
        found = jnp.where(seen, scores(kv[:, head(h)], q[:, head(h)]), -jnp.inf)
        top, total, part = first(found, kv[:, head(HEADS + h)])
        state[h : h + 1, :HEAD] = top
        state[HEADS + h : HEADS + h + 1, :HEAD] = total
        mix[head(h), :HEAD] = part


def pieces(units, states):
    found = []
    for query, parts in units:
        found.append([scores(keys, query) if seen is None else jnp.where(seen, scores(keys, query), -jnp.inf) for keys, _, seen in parts])
    ready = []
    for number, tiles in enumerate(found):
        top = tiles[0].max(axis=0, keepdims=True)
        for tile in tiles[1:]:
            top = jnp.maximum(top, tile.max(axis=0, keepdims=True))
        if states[number] is not None:
            top = jnp.maximum(top, states[number][0])
        weights = [jnp.exp2(tile - top) for tile in tiles]
        total = sum(w.sum(axis=0, keepdims=True) for w in weights)
        ready.append((top, total, [w.astype(BF16) for w in weights]))
    results = []
    for number, (top, total, weights) in enumerate(ready):
        part = sum(
            dot(values, w, ((0,), (0,))) for (_, values, _), w in zip(units[number][1], weights, strict=True)
        )
        if states[number] is not None:
            top0, total0, mix0 = states[number]
            fade = jnp.exp2(top0 - top)
            total = total + total0 * fade
            part = part + mix0 * fade
        results.append((top, total, part))
    return results


def middle_body(info, q, qd, kv, kvd, near, far, state0, mix0, state, mix):
    tp = info[0]
    last = tp ^ 3
    diagonal = positions(tp, (3,), 0) <= positions(tp, (3,), 1)

    def work(visible):
        for h in range(HEADS):
            k, v = head(h), head(HEADS + h)
            s, l = slice(h, h + 1), slice(HEADS + h, HEADS + h + 1)
            units, states, columns = [], [], []
            before = tuple(jnp.where(info[2] == 1, far[:, p], near[:, p]) for p in (k, v)) if visible else ()
            for chunk in range(4):
                rows = slice(chunk * CHUNK, (chunk + 1) * CHUNK)
                columns.append(rows)
                if chunk < 3:
                    parts = [(kvd[:, k], kvd[:, v], last < (tp ^ chunk))]
                    states.append((state0[s, rows], state0[l, rows], mix0[k, rows]))
                else:
                    parts = [(kvd[:, k], kvd[:, v], diagonal)]
                    for other in range(3):
                        these = slice(other * CHUNK, (other + 1) * CHUNK)
                        parts.append((kv[these, k], kv[these, v], (tp ^ other) < last))
                    states.append(None)
                if visible:
                    parts.append((*before, None))
                units.append((q[rows, k] if chunk < 3 else qd[:, k], parts))
            for rows, (top, total, part) in zip(columns, pieces(units, states), strict=True):
                state[s, rows] = top
                state[l, rows] = total
                mix[k, rows] = part

    @pl.when(info[1] == 1)
    def _():
        work(True)

    @pl.when(info[1] == 0)
    def _():
        work(False)


def last_body(info, q, qd, near, far, state, mix, out, held, done, sems):
    def finish(chunk, results):
        for h, (total, part) in enumerate(results):
            held[chunk, :, head(h)] = (part / total).astype(BF16).T
        rows = pl.ds(pl.multiple_of((info[0] ^ chunk) * CHUNK, CHUNK), CHUNK)
        pltpu.make_async_copy(held.at[chunk], out.at[rows], sems.at[chunk]).start()

    @pl.when(info[2] == 1)
    def _():
        copy = pltpu.make_async_copy(far, done, sems.at[4])
        copy.start()
        copy.wait()

    @pl.when(info[2] == 0)
    def _():
        done[...] = near[...]

    @pl.when(info[1] == 1)
    def _():
        for chunk in range(4):
            rows = slice(chunk * CHUNK, (chunk + 1) * CHUNK)
            units, states = [], []
            for h in range(HEADS):
                k, v = head(h), head(HEADS + h)
                units.append((q[rows, k] if chunk < 3 else qd[:, k], [(done[:, k], done[:, v], None)]))
                states.append((state[h : h + 1, rows], state[HEADS + h : HEADS + h + 1, rows], mix[k, rows]))
            finish(chunk, [(total, part) for _, total, part in pieces(units, states)])

    @pl.when(info[1] == 0)
    def _():
        for chunk in range(4):
            rows = slice(chunk * CHUNK, (chunk + 1) * CHUNK)
            finish(chunk, [(state[HEADS + h : HEADS + h + 1, rows], mix[head(h), rows]) for h in range(HEADS)])

    for chunk in range(4):
        rows = pl.ds(pl.multiple_of((info[0] ^ chunk) * CHUNK, CHUNK), CHUNK)
        pltpu.make_async_copy(held.at[chunk], out.at[rows], sems.at[chunk]).wait()


EARLY = 20_000_000_000
FAR = 4_000_000_000
TP = 4


def device(ctx, tp):
    return ctx * TP + tp


def line_ends(ctx_count):
    return [(i, (i + ctx_count - 1) % ctx_count) for i in range(0, ctx_count, ROW)]


def body(series, w_query, w_key, w_value, block_pos):
    ctx_count = lax.axis_size("ctx")
    here = lax.axis_index("ctx")
    tp = lax.axis_index("tp")
    before = (here + ctx_count - 1) % ctx_count
    visible = block_pos[before] < block_pos[here]
    far_here = here % ROW == 0
    info = jnp.stack([tp, visible.astype(jnp.int32), far_here.astype(jnp.int32)]).astype(jnp.int32)
    weights = (w_query, w_key, w_value)
    ends = line_ends(ctx_count)

    def send(name, x, route):
        with jax.named_scope("n_" + name):
            return lax.ppermute(x, ("ctx", "tp"), route)

    def swap(name, x, pairs):
        return send(name, x, [(device(i, a), device(i, b)) for i in range(ctx_count) for a, b in pairs])

    def to_next(name, x):
        return send(name, x, [(device(i - 1, t), device(i, t)) for i in range(ctx_count) if i % ROW for t in range(TP)])

    def place(last, first, line):
        return first // (2 * ROW) * (2 * ROW) + last % (2 * ROW) - LAST + line

    def aside(name, x, places):
        return send(name, x, [(device(last, t), device(place(last, i, places[t]), t)) for i, last in ends for t in range(TP)])

    def across(name, x, chunk, places=None):
        route = []
        for i, last in ends:
            for t in range(TP):
                shard = t ^ chunk
                source = last if places is None else place(last, i, places[shard])
                route.append((device(source, shard), device(i, t)))
        return send(name, x, route)

    xc = swap("xc", series, [(t, t ^ 2) for t in range(TP)])
    xb = swap("xb", series, [(t, t ^ 1) for t in range(TP)])
    qa, kva = run(
        "own",
        project_own_body,
        (shape(CHUNK, WIDTH), shape(CHUNK, 2 * WIDTH)),
        [SMEM] + [VMEM] * 4,
        0,
        info,
        series,
        *weights,
    )
    far_b, far_c, far_d = (aside(f"aside{chunk}", series, LEAVE[chunk]) for chunk in (1, 2, 3))
    xc, xb, own, qa, kva = lax.optimization_barrier((xc, xb, series, qa, kva))
    outer = swap("outer", xc, [(2, 3), (1, 0)])
    far_a, far_b, far_c, far_d = (
        across(f"across{chunk}", x, chunk, LEAVE[chunk]) for chunk, x in enumerate((kva, far_b, far_c, far_d))
    )
    own, far_d = lax.optimization_barrier((own, far_d))
    inner = swap("inner", own, [(1, 2), (2, 1)])
    q, kv = run(
        "middle",
        project_middle_body,
        (shape(HEAD, WIDTH), shape(HEAD, 2 * WIDTH)),
        [VMEM] * 7,
        0,
        xb,
        xc,
        qa,
        kva,
        *weights,
    )
    kv, far_c = lax.optimization_barrier((kv, far_c))
    near = to_next("near", kv)
    state, mix = run(
        "attend_own",
        own_first_body, STATE, [SMEM] + [VMEM] * 2, 0, info, q, kv)
    mix, far_a, far_b, far_c, far_d = lax.optimization_barrier((mix, far_a, far_b, far_c, far_d))
    far, far_last = run(
        "far",
        project_far_body,
        (shape(HEAD, 2 * WIDTH), shape(CHUNK, 2 * WIDTH)),
        [SMEM] + [ANY] * 6,
        FAR,
        info,
        far_a,
        far_b,
        far_c,
        far_d,
        w_key,
        w_value,
        scratch=(
            pltpu.VMEM((3, CHUNK, DEPTH), BF16),
            pltpu.VMEM((2, DEPTH, WIDTH), BF16),
            pltpu.SemaphoreType.DMA((6,)),
        ),
    )
    outer, inner, mix, far = lax.optimization_barrier((outer, inner, mix, far))
    qd, kvd = run(
        "last",
        project_last_body,
        (shape(CHUNK, WIDTH), shape(CHUNK, 2 * WIDTH)),
        [SMEM] + [VMEM] * 5,
        EARLY,
        info,
        outer,
        inner,
        *weights,
    )
    near_last = to_next("near_last", kvd)
    near, qd = lax.optimization_barrier((near, qd))
    state, mix = run(
        "attend_most",
        middle_body,
        STATE,
        [SMEM] + [VMEM] * 8,
        0,
        info,
        q,
        qd,
        kv,
        kvd,
        near,
        far,
        state,
        mix,
        alias={7: 0, 8: 1},
    )
    return run(
        "attend_last",
        last_body,
        shape(BLOCK, WIDTH),
        [SMEM] + [VMEM] * 3 + [ANY] + [VMEM] * 2,
        0,
        info,
        q,
        qd,
        near_last,
        far_last,
        state,
        mix,
        out_specs=ANY,
        scratch=(
            pltpu.VMEM((4, CHUNK, WIDTH), BF16),
            pltpu.VMEM((CHUNK, 2 * WIDTH), BF16),
            pltpu.SemaphoreType.DMA((5,)),
        ),
    )


def solution(mesh):
    in_specs = (P(("ctx", "tp"), None), P(None, "tp"), P(None, "tp"), P(None, "tp"), P())
    out_specs = P("ctx", "tp")
    return jax.shard_map(body, mesh=mesh, in_specs=in_specs, out_specs=out_specs, check_vma=False)
```

time: 89 us -> 72.6 us (0.82)
  starting transfers between devices: 33.7 us -> 27.3 us
  Pallas kernels: 21.2 us -> 15.6 us
  local copies, waits for them, and re-layouts: 7.84 us -> 4.43 us
  waiting for transfers between devices: 23.9 us -> 22.8 us
    ppermute x6 -> x0, starting transfers between devices: 25 us -> none  [the longest x4 14.3 us: swap(): return lax.ppermute(x, 'tp', pairs)]
    ppermute x7 -> x13, starting transfers between devices: 8.74 us -> 27.3 us  [send(): return lax.ppermute(x, ('ctx', 'tp'), route)]
    ppermute x6 -> x0, waiting for transfers between devices: 13 us -> none  [the longest x4 13 us: swap(): return lax.ppermute(x, 'tp', pairs)]
    ppermute x7 -> x13, waiting for transfers between devices: 10.9 us -> 22.8 us  [send(): return lax.ppermute(x, ('ctx', 'tp'), route)]
    pallas_call x8 -> x7, Pallas kernels: 21.2 us -> 15.6 us  [run(): return call(*args)]
    unnamed x22 -> x14, local copies, waits for them, and re-layouts: 7.25 us -> 3.78 us
  transfers between devices with their start and end apart: 13 -> 13, of which waited for: 5 -> 3; matrix products, arithmetic and copies ran while one was open for 1% -> 1% of each run, Pallas kernels for 21% -> 18%
where the time goes in v2:
time: 72.6 us; the launch traced here: 71.8 us
  starting transfers between devices  27.3 us (38%)
  waiting for transfers between devices  22.8 us (31%)
  Pallas kernels  15.6 us (21%)
  local copies, waits for them, and re-layouts  4.43 us (6%)
  between operations  1.56 us (2%)
    ppermute x13, starting transfers between devices, send(): return lax.ppermute(x, ('ctx', 'tp'), route)  27.3 us
    ppermute x13, waiting for transfers between devices, send(): return lax.ppermute(x, ('ctx', 'tp'), route)  22.8 us
    pallas_call x7, Pallas kernels, run(): return call(*args)  15.6 us
    unnamed x14, local copies, waits for them, and re-layouts  3.78 us
  transfers between devices with their start and end apart: 13, of which 3 were waited for; matrix products, arithmetic and copies ran while one was open for 1% of the time, Pallas kernels for 18%

profile of v2, /device:TPU:8, one launch (start us, length us, event | category | flops | bytes accessed | tf_op | source)
XLA Modules:
  0.0 71.8 jit_solution(18431989227335117344)
XLA Ops:
  0.0 1.5 %collective-permute-start.6 = (bf16[256,1024]{1,0:T(8,128)(2,1)}, bf16[256,1024]{1,0:T(8,128)(2,1)}, u32[]{:S(2)}, u32[]{:S(2)}) collective-permute-start(bf16[256,1024]{1,0:T(8,128)(2,1)} %x.1), channel_id=1, source_target_pairs={{508,60},{509,45},{510,46},{511,63},{28,28},{29,13},{30,14},{31,31... | collective-permute-start | bytes 1572872 | tf_op jit(solution)/shard_map/n_aside3/ppermute | solution.py:276
  1.5 1.5 %collective-permute-start.2 = (bf16[256,1024]{1,0:T(8,128)(2,1)}, bf16[256,1024]{1,0:T(8,128)(2,1)}, u32[]{:S(2)}, u32[]{:S(2)}) collective-permute-start(bf16[256,1024]{1,0:T(8,128)(2,1)} %x.1), channel_id=1, source_target_pairs={{508,52},{509,53},{510,54},{511,55},{28,20},{29,21},{30,22},{31,23... | collective-permute-start | bytes 1572872 | tf_op jit(solution)/shard_map/n_aside2/ppermute | solution.py:276
  2.9 0.7 collective-permute-start.10
  3.6 4.5 %collective-permute-start = (bf16[256,1024]{1,0:T(8,128)(2,1)}, bf16[256,1024]{1,0:T(8,128)(2,1)S(1)}, u32[]{:S(2)}, u32[]{:S(2)}) collective-permute-start(bf16[256,1024]{1,0:T(8,128)(2,1)} %x.1), channel_id=1, source_target_pairs={{0,2},{1,3},{2,0},{3,1},{4,6},{5,7},{6,4},{7,5},{8,10},{9,11},{10,... | collective-permute-start | bytes 1572872 | tf_op jit(solution)/shard_map/n_xc/ppermute | solution.py:276
  8.1 5.2 %collective-permute-start.1 = (bf16[256,1024]{1,0:T(8,128)(2,1)}, bf16[256,1024]{1,0:T(8,128)(2,1)S(1)}, u32[]{:S(2)}, u32[]{:S(2)}) collective-permute-start(bf16[256,1024]{1,0:T(8,128)(2,1)} %x.1), channel_id=1, source_target_pairs={{0,1},{1,0},{2,3},{3,2},{4,5},{5,4},{6,7},{7,6},{8,9},{9,8},{10,11... | collective-permute-start | bytes 1572872 | tf_op jit(solution)/shard_map/n_xb/ppermute | solution.py:276
  13.3 0.0 collective-permute-done.6
  13.3 1.3 %collective-permute-start.7 = (bf16[256,1024]{1,0:T(8,128)(2,1)}, bf16[256,1024]{1,0:T(8,128)(2,1)S(1)}, u32[]{:S(2)}, u32[]{:S(2)}) collective-permute-start(bf16[256,1024]{1,0:T(8,128)(2,1)} %collective-permute-done.6), channel_id=1, source_target_pairs={{63,0},{46,1},{45,2},{60,3},{31,32},{14,33},{13,34},{28,35},{127,6... | collective-permute-start | bytes 1572872 | tf_op jit(solution)/shard_map/n_across3/ppermute | solution.py:276
  14.6 0.0 collective-permute-done.2
  14.6 1.3 %collective-permute-start.3 = (bf16[256,1024]{1,0:T(8,128)(2,1)}, bf16[256,1024]{1,0:T(8,128)(2,1)S(1)}, u32[]{:S(2)}, u32[]{:S(2)}) collective-permute-start(bf16[256,1024]{1,0:T(8,128)(2,1)} %collective-permute-done.2), channel_id=1, source_target_pairs={{54,0},{55,1},{52,2},{53,3},{22,32},{23,33},{20,34},{21,35},{118,6... | collective-permute-start | bytes 1572872 | tf_op jit(solution)/shard_map/n_across2/ppermute | solution.py:276
  15.9 0.0 collective-permute-done.10
  15.9 1.3 %collective-permute-start.11 = (bf16[256,1024]{1,0:T(8,128)(2,1)S(1)}, bf16[256,1024]{1,0:T(8,128)(2,1)S(1)}, u32[]{:S(2)}, u32[]{:S(2)}) collective-permute-start(bf16[256,1024]{1,0:T(8,128)(2,1)S(1)} %collective-permute-done.10), channel_id=1, source_target_pairs={{37,0},{44,1},{47,2},{38,3},{5,32},{12,33},{15,34},{6,35},{101,64}... | collective-permute-start | bytes 1572872 | tf_op jit(solution)/shard_map/n_across1/ppermute | solution.py:276
  17.2 0.0 copy-start.6
  17.2 0.6 copy-done.6
  17.9 0.6 fusion
  19.8 0.1 pad_add_fusion.info
  19.9 0.0 copy-start
  19.9 1.0 %copy-done = bf16[1024,256]{1,0:T(8,128)(2,1)S(1)} copy-done((bf16[1024,256]{1,0:T(8,128)(2,1)S(1)}, bf16[1024,256]{1,0:T(8,128)(2,1)}, u32[]{:S(2)}) %copy-start) | copy-done | bytes 524312
  20.9 0.0 copy-start.2
  21.0 1.0 %copy-done.2 = bf16[1024,256]{1,0:T(8,128)(2,1)S(1)} copy-done((bf16[1024,256]{1,0:T(8,128)(2,1)S(1)}, bf16[1024,256]{1,0:T(8,128)(2,1)}, u32[]{:S(2)}) %copy-start.2) | copy-done | bytes 524312
  22.0 0.0 copy-start.4
  22.0 1.0 %copy-done.4 = bf16[1024,256]{1,0:T(8,128)(2,1)S(1)} copy-done((bf16[1024,256]{1,0:T(8,128)(2,1)S(1)}, bf16[1024,256]{1,0:T(8,128)(2,1)}, u32[]{:S(2)}) %copy-start.4) | copy-done | bytes 524312
  23.0 0.0 copy-start.1
  23.0 0.0 copy-start.3
  23.0 0.0 copy-start.5
  23.0 1.7 %n_own.1 = (bf16[256,256]{1,0:T(8,128)(2,1)S(1)}, bf16[256,512]{1,0:T(8,128)(2,1)S(1)}) custom-call(s32[3]{0:T(128)S(1)} %pad_add_fusion.info, bf16[256,1024]{1,0:T(8,128)(2,1)} %x.1, bf16[1024,256]{1,0:T(8,128)(2,1)S(1)} %copy-done, bf16[1024,256]{1,0:T(8,128)(2,1)S(1)} %copy-done.2, bf16[1024,256]{1,0:T(8,128)(2,1)S(1)} %copy-done.4), custom_call_target="tpu_custom_call" | custom-call | tf_op jit(solution)/shard_map/n_own/pallas_call | solution.py:48
  24.8 6.7 %collective-permute-done.xc = bf16[256,1024]{1,0:T(8,128)(2,1)S(1)} collective-permute-done((bf16[256,1024]{1,0:T(8,128)(2,1)}, bf16[256,1024]{1,0:T(8,128)(2,1)S(1)}, u32[]{:S(2)}, u32[]{:S(2)}) %collective-permute-start) | collective-permute-done | bytes 524320 | tf_op jit(solution)/shard_map/n_xc/ppermute | solution.py:276
  31.5 8.5 %collective-permute-done.1.xb = bf16[256,1024]{1,0:T(8,128)(2,1)S(1)} collective-permute-done((bf16[256,1024]{1,0:T(8,128)(2,1)}, bf16[256,1024]{1,0:T(8,128)(2,1)S(1)}, u32[]{:S(2)}, u32[]{:S(2)}) %collective-permute-start.1) | collective-permute-done | bytes 524320 | tf_op jit(solution)/shard_map/n_xb/ppermute | solution.py:276
  40.0 1.3 %collective-permute-start.9 = (bf16[256,512]{1,0:T(8,128)(2,1)S(1)}, bf16[256,512]{1,0:T(8,128)(2,1)S(1)}, u32[]{:S(2)}, u32[]{:S(2)}) collective-permute-start(bf16[256,512]{1,0:T(8,128)(2,1)S(1)} %get-tuple-element.42.kva), channel_id=1, source_target_pairs={{508,0},{509,1},{510,2},{511,3},{28,32},{29,33},{30,34},{31,35},{6... | collective-permute-start | bytes 786440 | tf_op jit(solution)/shard_map/n_across0/ppermute | solution.py:276
  41.3 4.3 %collective-permute-start.5 = (bf16[256,1024]{1,0:T(8,128)(2,1)S(1)}, bf16[256,1024]{1,0:T(8,128)(2,1)S(1)}, u32[]{:S(2)}, u32[]{:S(2)}) collective-permute-start(bf16[256,1024]{1,0:T(8,128)(2,1)S(1)} %collective-permute-done.xc), channel_id=1, source_target_pairs={{2,3},{1,0},{6,7},{5,4},{10,11},{9,8},{14,15},{13,12},{18,19},{17,... | collective-permute-start | bytes 1572872 | tf_op jit(solution)/shard_map/n_outer/ppermute | solution.py:276
  45.6 0.0 collective-permute-done.7.xd
  45.6 1.9 %collective-permute-start.8 = (bf16[256,1024]{1,0:T(8,128)(2,1)}, bf16[256,1024]{1,0:T(8,128)(2,1)S(1)}, u32[]{:S(2)}, u32[]{:S(2)}) collective-permute-start(bf16[256,1024]{1,0:T(8,128)(2,1)} %x.1), channel_id=1, source_target_pairs={{1,2},{2,1},{5,6},{6,5},{9,10},{10,9},{13,14},{14,13},{17,18},{18,... | collective-permute-start | bytes 1572872 | tf_op jit(solution)/shard_map/n_inner/ppermute | solution.py:276
  47.6 0.0 copy-done.1
  47.6 0.0 copy-done.3
  47.6 0.0 copy-done.5
  47.6 1.0 %n_middle.1 = (bf16[768,256]{1,0:T(8,128)(2,1)S(1)}, bf16[768,512]{1,0:T(8,128)(2,1)S(1)}) custom-call(bf16[256,1024]{1,0:T(8,128)(2,1)S(1)} %collective-permute-done.1.xb, bf16[256,1024]{1,0:T(8,128)(2,1)S(1)} %collective-permute-done.xc, bf16[256,256]{1,0:T(8,128)(2,1)S(1)} %get-tuple-element.41.qa, bf16[256,512]{1,0:T(8,128)(2,1)S(1)} %get-tuple-element.42.kva, ...), custom_call_target="tpu_custom_call" | custom-call | tf_op jit(solution)/shard_map/n_middle/pallas_call | solution.py:48
  48.6 0.0 collective-permute-done.3.xc
  48.6 1.3 %collective-permute-start.4 = (bf16[768,512]{1,0:T(8,128)(2,1)S(1)}, bf16[768,512]{1,0:T(8,128)(2,1)S(1)}, u32[]{:S(2)}, u32[]{:S(2)}) collective-permute-start(bf16[768,512]{1,0:T(8,128)(2,1)S(1)} %get-tuple-element.45.kv), channel_id=1, source_target_pairs={{0,4},{1,5},{2,6},{3,7},{4,8},{5,9},{6,10},{7,11},{8,12},{9,13},{1... | collective-permute-start | bytes 2359304 | tf_op jit(solution)/shard_map/n_near/ppermute | solution.py:276
  50.0 2.6 %n_attend_own.1 = (f32[8,1024]{1,0:T(8,128)S(1)}, f32[256,1024]{1,0:T(8,128)S(1)}) custom-call(s32[3]{0:T(128)S(1)} %pad_add_fusion.info, bf16[768,256]{1,0:T(8,128)(2,1)S(1)} %get-tuple-element.43.q, bf16[768,512]{1,0:T(8,128)(2,1)S(1)} %get-tuple-element.45.kv), custom_call_target="tpu_custom_call" | custom-call | tf_op jit(solution)/shard_map/n_attend_own/pallas_call | solution.py:48
  52.6 7.6 %collective-permute-done.9.kva = bf16[256,512]{1,0:T(8,128)(2,1)S(1)} collective-permute-done((bf16[256,512]{1,0:T(8,128)(2,1)S(1)}, bf16[256,512]{1,0:T(8,128)(2,1)S(1)}, u32[]{:S(2)}, u32[]{:S(2)}) %collective-permute-start.9) | collective-permute-done | bytes 262176 | tf_op jit(solution)/shard_map/n_across0/ppermute | solution.py:276
  60.1 0.0 collective-permute-done.11.xb
  60.1 1.8 %n_far.1 = (bf16[768,512]{1,0:T(8,128)(2,1)S(1)}, bf16[256,512]{1,0:T(8,128)(2,1)S(1)}) custom-call(s32[3]{0:T(128)S(1)} %pad_add_fusion.info, bf16[256,512]{1,0:T(8,128)(2,1)S(1)} %collective-permute-done.9.kva, bf16[256,1024]{1,0:T(8,128)(2,1)S(1)} %collective-permute-done.11.xb, bf16[256,1024]{1,0:T(8,128)(2,1)S(1)} %collective-permute-done.3.xc, ...), custom_call_target="tpu_custom_call" | custom-call | flops 4000000000 | tf_op jit(solution)/shard_map/n_far/pallas_call | solution.py:48
  61.9 0.0 collective-permute-done.5.outer
  61.9 0.0 collective-permute-done.8.inner
  62.0 1.1 %n_last.1 = (bf16[256,256]{1,0:T(8,128)(2,1)S(1)}, bf16[256,512]{1,0:T(8,128)(2,1)S(1)}) custom-call(s32[3]{0:T(128)S(1)} %pad_add_fusion.info, bf16[256,1024]{1,0:T(8,128)(2,1)S(1)} %collective-permute-done.5.outer, bf16[256,1024]{1,0:T(8,128)(2,1)S(1)} %collective-permute-done.8.inner, bf16[1024,256]{1,0:T(8,128)(2,1)S(1)} %copy-done.1, ...), custom_call_target="tpu_custom_call" | custom-call | flops 20000000000 | tf_op jit(solution)/shard_map/n_last/pallas_call | solution.py:48
  63.1 1.3 %collective-permute-start.12 = (bf16[256,512]{1,0:T(8,128)(2,1)S(1)}, bf16[256,512]{1,0:T(8,128)(2,1)S(1)}, u32[]{:S(2)}, u32[]{:S(2)}) collective-permute-start(bf16[256,512]{1,0:T(8,128)(2,1)S(1)} %get-tuple-element.61.kvd), channel_id=1, source_target_pairs={{0,4},{1,5},{2,6},{3,7},{4,8},{5,9},{6,10},{7,11},{8,12},{9,13},{1... | collective-permute-start | bytes 786440 | tf_op jit(solution)/shard_map/n_near_last/ppermute | solution.py:276
  64.4 0.0 collective-permute-done.4.near
  64.4 4.5 %n_attend_most.1 = (f32[8,1024]{1,0:T(8,128)S(1)}, f32[256,1024]{1,0:T(8,128)S(1)}) custom-call(s32[3]{0:T(128)S(1)} %pad_add_fusion.info, bf16[768,256]{1,0:T(8,128)(2,1)S(1)} %get-tuple-element.43.q, bf16[256,256]{1,0:T(8,128)(2,1)S(1)} %get-tuple-element.60.qd, ...), custom_call_target="tpu_custom_call", output_to_operand_aliasing={{0}: (7, {}), {1}: (8, {})} | custom-call | tf_op jit(solution)/shard_map/n_attend_most/pallas_call | solution.py:48
  69.0 0.0 collective-permute-done.12.near
  69.0 2.8 %n_attend_last.1 = bf16[1024,256]{1,0:T(8,128)(2,1)} custom-call(s32[3]{0:T(128)S(1)} %pad_add_fusion.info, bf16[768,256]{1,0:T(8,128)(2,1)S(1)} %get-tuple-element.43.q, bf16[256,256]{1,0:T(8,128)(2,1)S(1)} %get-tuple-element.60.qd, bf16[256,512]{1,0:T(8,128)(2,1)S(1)} %collective-permute-done.12.near, bf16[256,512]{1,0:T(8,128)(2,1)S(1)} %get-tuple-element.62.far, ...), custom_call_target="tpu_custom_call" | custom-call | tf_op jit(solution)/shard_map/n_attend_last/pallas_call | solution.py:48
Async XLA Ops:
  0.0 13.3 %collective-permute-start.6 = (bf16[256,1024]{1,0:T(8,128)(2,1)}, bf16[256,1024]{1,0:T(8,128)(2,1)}, u32[]{:S(2)}, u32[]{:S(2)}) collective-permute-start(bf16[256,1024]{1,0:T(8,128)(2,1)} %x.1), channel_id=1, source_target_pairs={{508,60},{509,45},{510,46},{511,63},{28,28},{29,13},{30,14},{31,31... | collective-permute-start | bytes 1572872 | tf_op jit(solution)/shard_map/n_aside3/ppermute | solution.py:276
  1.5 13.1 %collective-permute-start.2 = (bf16[256,1024]{1,0:T(8,128)(2,1)}, bf16[256,1024]{1,0:T(8,128)(2,1)}, u32[]{:S(2)}, u32[]{:S(2)}) collective-permute-start(bf16[256,1024]{1,0:T(8,128)(2,1)} %x.1), channel_id=1, source_target_pairs={{508,52},{509,53},{510,54},{511,55},{28,20},{29,21},{30,22},{31,23... | collective-permute-start | bytes 1572872 | tf_op jit(solution)/shard_map/n_aside2/ppermute | solution.py:276
  2.9 13.0 %collective-permute-start.10 = (bf16[256,1024]{1,0:T(8,128)(2,1)}, bf16[256,1024]{1,0:T(8,128)(2,1)S(1)}, u32[]{:S(2)}, u32[]{:S(2)}) collective-permute-start(bf16[256,1024]{1,0:T(8,128)(2,1)} %x.1), channel_id=1, source_target_pairs={{508,44},{509,37},{510,38},{511,47},{28,12},{29,5},{30,6},{31,15},... | collective-permute-start | bytes 1572872 | tf_op jit(solution)/shard_map/n_aside1/ppermute | solution.py:276
  3.6 27.9 %collective-permute-start = (bf16[256,1024]{1,0:T(8,128)(2,1)}, bf16[256,1024]{1,0:T(8,128)(2,1)S(1)}, u32[]{:S(2)}, u32[]{:S(2)}) collective-permute-start(bf16[256,1024]{1,0:T(8,128)(2,1)} %x.1), channel_id=1, source_target_pairs={{0,2},{1,3},{2,0},{3,1},{4,6},{5,7},{6,4},{7,5},{8,10},{9,11},{10,... | collective-permute-start | bytes 1572872 | tf_op jit(solution)/shard_map/n_xc/ppermute | solution.py:276
  8.1 31.9 %collective-permute-start.1 = (bf16[256,1024]{1,0:T(8,128)(2,1)}, bf16[256,1024]{1,0:T(8,128)(2,1)S(1)}, u32[]{:S(2)}, u32[]{:S(2)}) collective-permute-start(bf16[256,1024]{1,0:T(8,128)(2,1)} %x.1), channel_id=1, source_target_pairs={{0,1},{1,0},{2,3},{3,2},{4,5},{5,4},{6,7},{7,6},{8,9},{9,8},{10,11... | collective-permute-start | bytes 1572872 | tf_op jit(solution)/shard_map/n_xb/ppermute | solution.py:276
  13.3 32.3 %collective-permute-start.7 = (bf16[256,1024]{1,0:T(8,128)(2,1)}, bf16[256,1024]{1,0:T(8,128)(2,1)S(1)}, u32[]{:S(2)}, u32[]{:S(2)}) collective-permute-start(bf16[256,1024]{1,0:T(8,128)(2,1)} %collective-permute-done.6), channel_id=1, source_target_pairs={{63,0},{46,1},{45,2},{60,3},{31,32},{14,33},{13,34},{28,35},{127,6... | collective-permute-start | bytes 1572872 | tf_op jit(solution)/shard_map/n_across3/ppermute | solution.py:276
  14.6 34.0 %collective-permute-start.3 = (bf16[256,1024]{1,0:T(8,128)(2,1)}, bf16[256,1024]{1,0:T(8,128)(2,1)S(1)}, u32[]{:S(2)}, u32[]{:S(2)}) collective-permute-start(bf16[256,1024]{1,0:T(8,128)(2,1)} %collective-permute-done.2), channel_id=1, source_target_pairs={{54,0},{55,1},{52,2},{53,3},{22,32},{23,33},{20,34},{21,35},{118,6... | collective-permute-start | bytes 1572872 | tf_op jit(solution)/shard_map/n_across2/ppermute | solution.py:276
  15.9 44.2 %collective-permute-start.11 = (bf16[256,1024]{1,0:T(8,128)(2,1)S(1)}, bf16[256,1024]{1,0:T(8,128)(2,1)S(1)}, u32[]{:S(2)}, u32[]{:S(2)}) collective-permute-start(bf16[256,1024]{1,0:T(8,128)(2,1)S(1)} %collective-permute-done.10), channel_id=1, source_target_pairs={{37,0},{44,1},{47,2},{38,3},{5,32},{12,33},{15,34},{6,35},{101,64}... | collective-permute-start | bytes 1572872 | tf_op jit(solution)/shard_map/n_across1/ppermute | solution.py:276
  17.2 0.7 copy-start.6
  19.9 1.0 %copy-start = (bf16[1024,256]{1,0:T(8,128)(2,1)S(1)}, bf16[1024,256]{1,0:T(8,128)(2,1)}, u32[]{:S(2)}) copy-start(bf16[1024,256]{1,0:T(8,128)(2,1)} %wq.5) | copy-start | bytes 1572868
  20.9 1.0 %copy-start.2 = (bf16[1024,256]{1,0:T(8,128)(2,1)S(1)}, bf16[1024,256]{1,0:T(8,128)(2,1)}, u32[]{:S(2)}) copy-start(bf16[1024,256]{1,0:T(8,128)(2,1)} %wk.7) | copy-start | bytes 1572868
  22.0 1.0 %copy-start.4 = (bf16[1024,256]{1,0:T(8,128)(2,1)S(1)}, bf16[1024,256]{1,0:T(8,128)(2,1)}, u32[]{:S(2)}) copy-start(bf16[1024,256]{1,0:T(8,128)(2,1)} %wv.7) | copy-start | bytes 1572868
  23.0 24.5 %copy-start.1 = (bf16[1024,256]{1,0:T(8,128)(2,1)S(1)}, bf16[1024,256]{1,0:T(8,128)(2,1)}, u32[]{:S(2)}) copy-start(bf16[1024,256]{1,0:T(8,128)(2,1)} %wq.5) | copy-start | bytes 1572868
  23.0 24.5 %copy-start.3 = (bf16[1024,256]{1,0:T(8,128)(2,1)S(1)}, bf16[1024,256]{1,0:T(8,128)(2,1)}, u32[]{:S(2)}) copy-start(bf16[1024,256]{1,0:T(8,128)(2,1)} %wk.7) | copy-start | bytes 1572868
  23.0 24.6 %copy-start.5 = (bf16[1024,256]{1,0:T(8,128)(2,1)S(1)}, bf16[1024,256]{1,0:T(8,128)(2,1)}, u32[]{:S(2)}) copy-start(bf16[1024,256]{1,0:T(8,128)(2,1)} %wv.7) | copy-start | bytes 1572868
  40.0 20.1 %collective-permute-start.9 = (bf16[256,512]{1,0:T(8,128)(2,1)S(1)}, bf16[256,512]{1,0:T(8,128)(2,1)S(1)}, u32[]{:S(2)}, u32[]{:S(2)}) collective-permute-start(bf16[256,512]{1,0:T(8,128)(2,1)S(1)} %get-tuple-element.42.kva), channel_id=1, source_target_pairs={{508,0},{509,1},{510,2},{511,3},{28,32},{29,33},{30,34},{31,35},{6... | collective-permute-start | bytes 786440 | tf_op jit(solution)/shard_map/n_across0/ppermute | solution.py:276
  41.3 20.6 %collective-permute-start.5 = (bf16[256,1024]{1,0:T(8,128)(2,1)S(1)}, bf16[256,1024]{1,0:T(8,128)(2,1)S(1)}, u32[]{:S(2)}, u32[]{:S(2)}) collective-permute-start(bf16[256,1024]{1,0:T(8,128)(2,1)S(1)} %collective-permute-done.xc), channel_id=1, source_target_pairs={{2,3},{1,0},{6,7},{5,4},{10,11},{9,8},{14,15},{13,12},{18,19},{17,... | collective-permute-start | bytes 1572872 | tf_op jit(solution)/shard_map/n_outer/ppermute | solution.py:276
  45.6 16.3 %collective-permute-start.8 = (bf16[256,1024]{1,0:T(8,128)(2,1)}, bf16[256,1024]{1,0:T(8,128)(2,1)S(1)}, u32[]{:S(2)}, u32[]{:S(2)}) collective-permute-start(bf16[256,1024]{1,0:T(8,128)(2,1)} %x.1), channel_id=1, source_target_pairs={{1,2},{2,1},{5,6},{6,5},{9,10},{10,9},{13,14},{14,13},{17,18},{18,... | collective-permute-start | bytes 1572872 | tf_op jit(solution)/shard_map/n_inner/ppermute | solution.py:276
  48.6 15.8 %collective-permute-start.4 = (bf16[768,512]{1,0:T(8,128)(2,1)S(1)}, bf16[768,512]{1,0:T(8,128)(2,1)S(1)}, u32[]{:S(2)}, u32[]{:S(2)}) collective-permute-start(bf16[768,512]{1,0:T(8,128)(2,1)S(1)} %get-tuple-element.45.kv), channel_id=1, source_target_pairs={{0,4},{1,5},{2,6},{3,7},{4,8},{5,9},{6,10},{7,11},{8,12},{9,13},{1... | collective-permute-start | bytes 2359304 | tf_op jit(solution)/shard_map/n_near/ppermute | solution.py:276
  63.1 5.9 %collective-permute-start.12 = (bf16[256,512]{1,0:T(8,128)(2,1)S(1)}, bf16[256,512]{1,0:T(8,128)(2,1)S(1)}, u32[]{:S(2)}, u32[]{:S(2)}) collective-permute-start(bf16[256,512]{1,0:T(8,128)(2,1)S(1)} %get-tuple-element.61.kvd), channel_id=1, source_target_pairs={{0,4},{1,5},{2,6},{3,7},{4,8},{5,9},{6,10},{7,11},{8,12},{9,13},{1... | collective-permute-start | bytes 786440 | tf_op jit(solution)/shard_map/n_near_last/ppermute | solution.py:276

commit v3 on v2

--- a/solution.py
+++ b/solution.py
@@ -17,7 +17,7 @@
 SCALE = math.log2(math.e) / math.sqrt(HD)
 ROW = 8
 LAST = ROW - 1
-LEAVE = (None, (3, 1, 1, 3), (5,) * 4, (LAST, 3, 3, LAST))
+LEAVE = ((3,) * 4, (5, 1, 1, 5), None, (LAST, 5, 5, LAST))
 
 BF16 = jnp.bfloat16
 F32 = jnp.float32
@@ -56,12 +56,16 @@
     return jnp.dot(rows, weight, preferred_element_type=F32).astype(BF16)
 
 
+def project_query(rows, weight):
+    return (jnp.dot(rows, weight, preferred_element_type=F32) * SCALE).astype(BF16)
+
+
 def head(number):
     return slice(number * HD, (number + 1) * HD)
 
 
 def scores(keys, query):
-    return dot(keys, query, ((1,), (1,))) * SCALE
+    return dot(keys, query, ((1,), (1,)))
 
 
 def mixed(values, weights):
@@ -91,7 +95,7 @@
 
 
 def project_own_body(info, x, wq, wk, wv, q, kv):
-    q[...] = project(x[...], wq[...])
+    q[...] = project_query(x[...], wq[...])
     kv[:, :WIDTH] = project(x[...], wk[...])
     kv[:, WIDTH:] = project(x[...], wv[...])
 
@@ -101,17 +105,23 @@
     kv[:CHUNK] = kva[...]
     for place, x in ((1, xb), (2, xc)):
         rows = slice(place * CHUNK, (place + 1) * CHUNK)
-        q[rows] = project(x[...], wq[...])
+        q[rows] = project_query(x[...], wq[...])
         kv[rows, :WIDTH] = project(x[...], wk[...])
         kv[rows, WIDTH:] = project(x[...], wv[...])
 
 
-def project_last_body(info, outer, inner, wq, wk, wv, q, kv):
+def gate_body(*refs):
+    refs[-1][...] = jnp.zeros_like(refs[-1])
+
+
+def project_last_body(info, passed, outer, inner, wk, wv, kv):
+    def work(x):
+        kv[:, :WIDTH] = project(x[...], wk[...])
+        kv[:, WIDTH:] = project(x[...], wv[...])
+
     middle = jnp.logical_or(info[0] == 1, info[0] == 2)
-    x = jnp.where(middle, inner[...], outer[...])
-    q[...] = project(x, wq[...])
-    kv[:, :WIDTH] = project(x, wk[...])
-    kv[:, WIDTH:] = project(x, wv[...])
+    pl.when(middle)(lambda: work(inner))
+    pl.when(jnp.logical_not(middle))(lambda: work(outer))
 
 
 def project_far_body(info, kva, xb, xc, xd, wk, wv, kv, kvd, x, w, sems):
@@ -168,7 +178,19 @@
     return results
 
 
-def middle_body(info, q, qd, kv, kvd, near, far, state0, mix0, state, mix):
+def middle_body(info, outer, inner, wq, q, kv, kvd, near, far, state0, mix0, state, mix, qd, held):
+    middle = jnp.logical_or(info[0] == 1, info[0] == 2)
+
+    def query(x):
+        qd[...] = project_query(x[...], wq[...])
+
+    def hold(x):
+        held[...] = x[...]
+
+    pl.when(middle)(lambda: query(inner))
+    pl.when(jnp.logical_not(middle))(lambda: query(outer))
+    pl.when(info[2] == 1)(lambda: hold(far))
+    pl.when(info[2] == 0)(lambda: hold(near))
     tp = info[0]
     last = tp ^ 3
     diagonal = positions(tp, (3,), 0) <= positions(tp, (3,), 1)
@@ -178,7 +200,7 @@
             k, v = head(h), head(HEADS + h)
             s, l = slice(h, h + 1), slice(HEADS + h, HEADS + h + 1)
             units, states, columns = [], [], []
-            before = tuple(jnp.where(info[2] == 1, far[:, p], near[:, p]) for p in (k, v)) if visible else ()
+            before = (held[:, k], held[:, v])
             for chunk in range(4):
                 rows = slice(chunk * CHUNK, (chunk + 1) * CHUNK)
                 columns.append(rows)
@@ -227,14 +249,16 @@
 
     @pl.when(info[1] == 1)
     def _():
+        units, states = [], []
         for chunk in range(4):
             rows = slice(chunk * CHUNK, (chunk + 1) * CHUNK)
-            units, states = [], []
             for h in range(HEADS):
                 k, v = head(h), head(HEADS + h)
                 units.append((q[rows, k] if chunk < 3 else qd[:, k], [(done[:, k], done[:, v], None)]))
                 states.append((state[h : h + 1, rows], state[HEADS + h : HEADS + h + 1, rows], mix[k, rows]))
-            finish(chunk, [(total, part) for _, total, part in pieces(units, states)])
+        results = [(total, part) for _, total, part in pieces(units, states)]
+        for chunk in range(4):
+            finish(chunk, results[chunk * HEADS : (chunk + 1) * HEADS])
 
     @pl.when(info[1] == 0)
     def _():
@@ -249,6 +273,8 @@
 
 EARLY = 20_000_000_000
 FAR = 4_000_000_000
+GATE = 1_000_000_000
+GATE0 = 1_000_000_000
 TP = 4
 
 
@@ -308,13 +334,17 @@
         series,
         *weights,
     )
-    far_b, far_c, far_d = (aside(f"aside{chunk}", series, LEAVE[chunk]) for chunk in (1, 2, 3))
-    xc, xb, own, qa, kva = lax.optimization_barrier((xc, xb, series, qa, kva))
+    far_c = across("across2", series, 2)
+    far_b, far_d = (
+        across(f"across{chunk}", aside(f"aside{chunk}", series, LEAVE[chunk]), chunk, LEAVE[chunk]) for chunk in (1, 3)
+    )
+    kva, far_c = lax.optimization_barrier((kva, far_c))
+    far_a = across("across0", aside("aside0", kva, LEAVE[0]), 0, LEAVE[0])
+    passed = run("gate0", gate_body, shape(8, 128, F32), [ANY], GATE0, xc)
+    xc, own, qa, kva, passed = lax.optimization_barrier((xc, series, qa, kva, passed))
     outer = swap("outer", xc, [(2, 3), (1, 0)])
-    far_a, far_b, far_c, far_d = (
-        across(f"across{chunk}", x, chunk, LEAVE[chunk]) for chunk, x in enumerate((kva, far_b, far_c, far_d))
-    )
-    own, far_d = lax.optimization_barrier((own, far_d))
+    passed = run("gate1", gate_body, shape(8, 128, F32), [ANY] * 2, GATE0, passed, far_c)
+    own, far_c, passed = lax.optimization_barrier((own, far_c, passed))
     inner = swap("inner", own, [(1, 2), (2, 1)])
     q, kv = run(
         "middle",
@@ -328,7 +358,7 @@
         kva,
         *weights,
     )
-    kv, far_c = lax.optimization_barrier((kv, far_c))
+    kv, far_d = lax.optimization_barrier((kv, far_d))
     near = to_next("near", kv)
     state, mix = run(
         "attend_own",
@@ -353,36 +383,43 @@
             pltpu.SemaphoreType.DMA((6,)),
         ),
     )
-    outer, inner, mix, far = lax.optimization_barrier((outer, inner, mix, far))
-    qd, kvd = run(
+    outer, far = lax.optimization_barrier((outer, far))
+    passed = run("gate", gate_body, shape(8, 128, F32), [ANY] * 2, GATE, outer, passed)
+    inner, passed = lax.optimization_barrier((inner, passed))
+    kvd = run(
         "last",
         project_last_body,
-        (shape(CHUNK, WIDTH), shape(CHUNK, 2 * WIDTH)),
-        [SMEM] + [VMEM] * 5,
+        shape(CHUNK, 2 * WIDTH),
+        [SMEM, ANY] + [VMEM] * 4,
         EARLY,
+        info,
+        passed,
+        outer,
+        inner,
+        w_key,
+        w_value,
+    )
+    near_last = to_next("near_last", kvd)
+    near, kvd, outer, inner = lax.optimization_barrier((near, kvd, outer, inner))
+    state, mix, qd = run(
+        "attend_most",
+        middle_body,
+        (*STATE, shape(CHUNK, WIDTH)),
+        [SMEM] + [VMEM] * 10,
+        0,
         info,
         outer,
         inner,
-        *weights,
-    )
-    near_last = to_next("near_last", kvd)
-    near, qd = lax.optimization_barrier((near, qd))
-    state, mix = run(
-        "attend_most",
-        middle_body,
-        STATE,
-        [SMEM] + [VMEM] * 8,
-        0,
-        info,
+        w_query,
         q,
-        qd,
         kv,
         kvd,
         near,
         far,
         state,
         mix,
-        alias={7: 0, 8: 1},
+        alias={9: 0, 10: 1},
+        scratch=(pltpu.VMEM((HEAD, 2 * WIDTH), BF16),),
     )
     return run(
         "attend_last",

time: 72.6 us -> 68.7 us (0.946)
  the two profiles are of different devices: /device:TPU:8 before, /device:TPU:52 now
where the time goes in v3:
time: 68.7 us; the launch traced here: 68.1 us
  waiting for transfers between devices  27.1 us (39%)
  starting transfers between devices  20.8 us (30%)
  Pallas kernels  13 us (19%)
  local copies, waits for them, and re-layouts  5.47 us (8%)
  between operations  1.65 us (2%)
    ppermute x13, waiting for transfers between devices, send(): return lax.ppermute(x, ('ctx', 'tp'), route)  27.1 us
    ppermute x13, starting transfers between devices, send(): return lax.ppermute(x, ('ctx', 'tp'), route)  20.8 us
    pallas_call x10, Pallas kernels, run(): return call(*args)  13 us
    unnamed x18, local copies, waits for them, and re-layouts  4.82 us
  transfers between devices with their start and end apart: 13, of which 4 were waited for; matrix products, arithmetic and copies ran while one was open for 1% of the time, Pallas kernels for 16%

profile of v3, /device:TPU:52, one launch (start us, length us, event | category | flops | bytes accessed | tf_op | source)
XLA Modules:
  0.0 68.1 jit_solution(2163794438779923046)
XLA Ops:
  0.0 0.7 %collective-permute-start.3 = (bf16[256,1024]{1,0:T(8,128)(2,1)}, bf16[256,1024]{1,0:T(8,128)(2,1)S(1)}, u32[]{:S(2)}, u32[]{:S(2)}) collective-permute-start(bf16[256,1024]{1,0:T(8,128)(2,1)} %x.1), channel_id=1, source_target_pairs={{508,60},{509,53},{510,54},{511,63},{28,28},{29,21},{30,22},{31,31... | collective-permute-start | bytes 1572872 | tf_op jit(solution)/shard_map/n_aside3/ppermute | solution.py:302
  0.7 0.7 %collective-permute-start.2 = (bf16[256,1024]{1,0:T(8,128)(2,1)}, bf16[256,1024]{1,0:T(8,128)(2,1)S(1)}, u32[]{:S(2)}, u32[]{:S(2)}) collective-permute-start(bf16[256,1024]{1,0:T(8,128)(2,1)} %x.1), channel_id=1, source_target_pairs={{510,0},{511,1},{508,2},{509,3},{30,32},{31,33},{28,34},{29,35},{6... | collective-permute-start | bytes 1572872 | tf_op jit(solution)/shard_map/n_across2/ppermute | solution.py:302
  1.4 0.7 %collective-permute-start.10 = (bf16[256,1024]{1,0:T(8,128)(2,1)}, bf16[256,1024]{1,0:T(8,128)(2,1)S(1)}, u32[]{:S(2)}, u32[]{:S(2)}) collective-permute-start(bf16[256,1024]{1,0:T(8,128)(2,1)} %x.1), channel_id=1, source_target_pairs={{508,52},{509,37},{510,38},{511,55},{28,20},{29,5},{30,6},{31,23},... | collective-permute-start | bytes 1572872 | tf_op jit(solution)/shard_map/n_aside1/ppermute | solution.py:302
  2.1 4.0 %collective-permute-start.1 = (bf16[256,1024]{1,0:T(8,128)(2,1)}, bf16[256,1024]{1,0:T(8,128)(2,1)S(1)}, u32[]{:S(2)}, u32[]{:S(2)}) collective-permute-start(bf16[256,1024]{1,0:T(8,128)(2,1)} %x.1), channel_id=1, source_target_pairs={{0,2},{1,3},{2,0},{3,1},{4,6},{5,7},{6,4},{7,5},{8,10},{9,11},{10,... | collective-permute-start | bytes 1572872 | tf_op jit(solution)/shard_map/n_xc/ppermute | solution.py:302
  6.1 2.6 %collective-permute-start = (bf16[256,1024]{1,0:T(8,128)(2,1)}, bf16[256,1024]{1,0:T(8,128)(2,1)S(1)}, u32[]{:S(2)}, u32[]{:S(2)}) collective-permute-start(bf16[256,1024]{1,0:T(8,128)(2,1)} %x.1), channel_id=1, source_target_pairs={{0,1},{1,0},{2,3},{3,2},{4,5},{5,4},{6,7},{7,6},{8,9},{9,8},{10,11... | collective-permute-start | bytes 1572872 | tf_op jit(solution)/shard_map/n_xb/ppermute | solution.py:302
  8.8 0.0 copy-start.8
  8.8 0.6 copy-done.8
  9.4 0.6 fusion
  11.4 0.1 pad_add_fusion.info
  11.5 0.0 collective-permute-done.3
  11.5 0.7 %collective-permute-start.4 = (bf16[256,1024]{1,0:T(8,128)(2,1)S(1)}, bf16[256,1024]{1,0:T(8,128)(2,1)S(1)}, u32[]{:S(2)}, u32[]{:S(2)}) collective-permute-start(bf16[256,1024]{1,0:T(8,128)(2,1)S(1)} %collective-permute-done.3), channel_id=1, source_target_pairs={{63,0},{54,1},{53,2},{60,3},{31,32},{22,33},{21,34},{28,35},{127,6... | collective-permute-start | bytes 1572872 | tf_op jit(solution)/shard_map/n_across3/ppermute | solution.py:302
  12.2 0.0 copy-start
  12.2 1.0 %copy-done = bf16[1024,256]{1,0:T(8,128)(2,1)S(1)} copy-done((bf16[1024,256]{1,0:T(8,128)(2,1)S(1)}, bf16[1024,256]{1,0:T(8,128)(2,1)}, u32[]{:S(2)}) %copy-start) | copy-done | bytes 524312
  13.2 0.0 copy-start.2
  13.2 1.0 %copy-done.2 = bf16[1024,256]{1,0:T(8,128)(2,1)S(1)} copy-done((bf16[1024,256]{1,0:T(8,128)(2,1)S(1)}, bf16[1024,256]{1,0:T(8,128)(2,1)}, u32[]{:S(2)}) %copy-start.2) | copy-done | bytes 524312
  14.3 0.0 copy-start.4
  14.3 1.0 %copy-done.4 = bf16[1024,256]{1,0:T(8,128)(2,1)S(1)} copy-done((bf16[1024,256]{1,0:T(8,128)(2,1)S(1)}, bf16[1024,256]{1,0:T(8,128)(2,1)}, u32[]{:S(2)}) %copy-start.4) | copy-done | bytes 524312
  15.3 0.0 copy-start.6
  15.3 1.0 %copy-done.6 = bf16[256,1024]{1,0:T(8,128)(2,1)S(1)} copy-done((bf16[256,1024]{1,0:T(8,128)(2,1)S(1)}, bf16[256,1024]{1,0:T(8,128)(2,1)}, u32[]{:S(2)}) %copy-start.6) | copy-done | bytes 524312
  16.4 1.1 %n_own.1 = (bf16[256,256]{1,0:T(8,128)(2,1)S(1)}, bf16[256,512]{1,0:T(8,128)(2,1)S(1)}) custom-call(s32[3]{0:T(128)S(1)} %pad_add_fusion.info, bf16[256,1024]{1,0:T(8,128)(2,1)S(1)} %copy-done.6, bf16[1024,256]{1,0:T(8,128)(2,1)S(1)} %copy-done, bf16[1024,256]{1,0:T(8,128)(2,1)S(1)} %copy-done.2, bf16[1024,256]{1,0:T(8,128)(2,1)S(1)} %copy-done.4), custom_call_target="tpu_custom_call" | custom-call | tf_op jit(solution)/shard_map/n_own/pallas_call | solution.py:48
  17.5 0.0 collective-permute-done.2.refs_1_.xc
  17.5 0.7 collective-permute-start.8
  18.2 0.0 collective-permute-done.10
  18.2 0.7 %collective-permute-start.11 = (bf16[256,1024]{1,0:T(8,128)(2,1)S(1)}, bf16[256,1024]{1,0:T(8,128)(2,1)S(1)}, u32[]{:S(2)}, u32[]{:S(2)}) collective-permute-start(bf16[256,1024]{1,0:T(8,128)(2,1)S(1)} %collective-permute-done.10), channel_id=1, source_target_pairs={{37,0},{52,1},{55,2},{38,3},{5,32},{20,33},{23,34},{6,35},{101,64}... | collective-permute-start | bytes 1572872 | tf_op jit(solution)/shard_map/n_across1/ppermute | solution.py:302
  18.9 0.0 collective-permute-done.8
  18.9 0.7 collective-permute-start.9
  19.6 15.3 %collective-permute-done.1.refs_0_.xc = bf16[256,1024]{1,0:T(8,128)(2,1)S(1)} collective-permute-done((bf16[256,1024]{1,0:T(8,128)(2,1)}, bf16[256,1024]{1,0:T(8,128)(2,1)S(1)}, u32[]{:S(2)}, u32[]{:S(2)}) %collective-permute-start.1) | collective-permute-done | bytes 524320 | tf_op jit(solution)/shard_map/n_xc/ppermute | solution.py:302
  34.8 0.0 copy-start.7
  34.8 0.0 copy-start.1
  34.8 0.0 copy-start.3
  34.8 0.0 copy-start.5
  34.9 2.9 %collective-permute-start.7 = (bf16[256,1024]{1,0:T(8,128)(2,1)S(1)}, bf16[256,1024]{1,0:T(8,128)(2,1)S(1)}, u32[]{:S(2)}, u32[]{:S(2)}) collective-permute-start(bf16[256,1024]{1,0:T(8,128)(2,1)S(1)} %collective-permute-done.1.refs_0_.xc), channel_id=1, source_target_pairs={{2,3},{1,0},{6,7},{5,4},{10,11},{9,8},{14,15},{13,12},{18,19},{17,... | collective-permute-start | bytes 1572872 | tf_op jit(solution)/shard_map/n_outer/ppermute | solution.py:302
  37.8 4.0 %collective-permute-done.xb = bf16[256,1024]{1,0:T(8,128)(2,1)S(1)} collective-permute-done((bf16[256,1024]{1,0:T(8,128)(2,1)}, bf16[256,1024]{1,0:T(8,128)(2,1)S(1)}, u32[]{:S(2)}, u32[]{:S(2)}) %collective-permute-start) | collective-permute-done | bytes 524320 | tf_op jit(solution)/shard_map/n_xb/ppermute | solution.py:302
  41.8 0.0 copy-done.7
  41.8 2.6 %collective-permute-start.6 = (bf16[256,1024]{1,0:T(8,128)(2,1)S(1)}, bf16[256,1024]{1,0:T(8,128)(2,1)S(1)}, u32[]{:S(2)}, u32[]{:S(2)}) collective-permute-start(bf16[256,1024]{1,0:T(8,128)(2,1)S(1)} %copy-done.7), channel_id=1, source_target_pairs={{1,2},{2,1},{5,6},{6,5},{9,10},{10,9},{13,14},{14,13},{17,18},{18,... | collective-permute-start | bytes 1572872 | tf_op jit(solution)/shard_map/n_inner/ppermute | solution.py:302
  44.4 0.0 copy-done.1
  44.4 0.0 copy-done.3
  44.4 0.0 copy-done.5
  44.4 1.0 %n_middle.1 = (bf16[768,256]{1,0:T(8,128)(2,1)S(1)}, bf16[768,512]{1,0:T(8,128)(2,1)S(1)}) custom-call(bf16[256,1024]{1,0:T(8,128)(2,1)S(1)} %collective-permute-done.xb, bf16[256,1024]{1,0:T(8,128)(2,1)S(1)} %collective-permute-done.1.refs_0_.xc, bf16[256,256]{1,0:T(8,128)(2,1)S(1)} %get-tuple-element.45.qa, bf16[256,512]{1,0:T(8,128)(2,1)S(1)} %get-tuple-element.46.kva, ...), custom_call_target="tpu_custom_call" | custom-call | tf_op jit(solution)/shard_map/n_middle/pallas_call | solution.py:48
  45.4 0.0 collective-permute-done.4.xd
  45.4 1.9 %collective-permute-start.5 = (bf16[768,512]{1,0:T(8,128)(2,1)S(1)}, bf16[768,512]{1,0:T(8,128)(2,1)S(1)}, u32[]{:S(2)}, u32[]{:S(2)}) collective-permute-start(bf16[768,512]{1,0:T(8,128)(2,1)S(1)} %get-tuple-element.49.kv), channel_id=1, source_target_pairs={{0,4},{1,5},{2,6},{3,7},{4,8},{5,9},{6,10},{7,11},{8,12},{9,13},{1... | collective-permute-start | bytes 2359304 | tf_op jit(solution)/shard_map/n_near/ppermute | solution.py:302
  47.3 2.4 %n_attend_own.1 = (f32[8,1024]{1,0:T(8,128)S(1)}, f32[256,1024]{1,0:T(8,128)S(1)}) custom-call(s32[3]{0:T(128)S(1)} %pad_add_fusion.info, bf16[768,256]{1,0:T(8,128)(2,1)S(1)} %get-tuple-element.47.q, bf16[768,512]{1,0:T(8,128)(2,1)S(1)} %get-tuple-element.49.kv), custom_call_target="tpu_custom_call" | custom-call | tf_op jit(solution)/shard_map/n_attend_own/pallas_call | solution.py:48
  49.8 0.0 collective-permute-done.9.kva
  49.8 0.0 collective-permute-done.11.xb
  49.8 0.6 n_far.1
  50.4 0.0 collective-permute-done.7.refs_0_.outer
  50.4 6.7 %collective-permute-done.6.inner = bf16[256,1024]{1,0:T(8,128)(2,1)S(1)} collective-permute-done((bf16[256,1024]{1,0:T(8,128)(2,1)S(1)}, bf16[256,1024]{1,0:T(8,128)(2,1)S(1)}, u32[]{:S(2)}, u32[]{:S(2)}) %collective-permute-start.6) | collective-permute-done | bytes 524320 | tf_op jit(solution)/shard_map/n_inner/ppermute | solution.py:302
  57.2 1.0 %n_last.1.kvd = bf16[256,512]{1,0:T(8,128)(2,1)S(1)} custom-call(s32[3]{0:T(128)S(1)} %pad_add_fusion.info, f32[8,128]{1,0:T(8,128)S(1)} %n_gate.1.passed, bf16[256,1024]{1,0:T(8,128)(2,1)S(1)} %collective-permute-done.7.refs_0_.outer, bf16[256,1024]{1,0:T(8,128)(2,1)S(1)} %collective-permute-done.6.inner, bf16[1024,256]{1,0:T(8,128)(2,1)S(1)} %copy-done.3, ...), custom_call_target="tpu_custom_call" | custom-call | flops 20000000000 | tf_op jit(solution)/shard_map/n_last/pallas_call | solution.py:48
  58.1 1.9 %collective-permute-start.12 = (bf16[256,512]{1,0:T(8,128)(2,1)S(1)}, bf16[256,512]{1,0:T(8,128)(2,1)S(1)}, u32[]{:S(2)}, u32[]{:S(2)}) collective-permute-start(bf16[256,512]{1,0:T(8,128)(2,1)S(1)} %n_last.1.kvd), channel_id=1, source_target_pairs={{0,4},{1,5},{2,6},{3,7},{4,8},{5,9},{6,10},{7,11},{8,12},{9,13},{1... | collective-permute-start | bytes 786440 | tf_op jit(solution)/shard_map/n_near_last/ppermute | solution.py:302
  60.1 0.0 collective-permute-done.5.near
  60.1 4.6 %n_attend_most.1 = (f32[8,1024]{1,0:T(8,128)S(1)}, f32[256,1024]{1,0:T(8,128)S(1)}, bf16[256,256]{1,0:T(8,128)(2,1)S(1)}) custom-call(s32[3]{0:T(128)S(1)} %pad_add_fusion.info, bf16[256,1024]{1,0:T(8,128)(2,1)S(1)} %collective-permute-done.7.refs_0_.outer, ...), custom_call_target="tpu_custom_call", output_to_operand_aliasing={{0}: (9, {}), {1}: (10, {})} | custom-call | tf_op jit(solution)/shard_map/n_attend_most/pallas_call | solution.py:48
  64.7 1.1 %collective-permute-done.12.near = bf16[256,512]{1,0:T(8,128)(2,1)S(1)} collective-permute-done((bf16[256,512]{1,0:T(8,128)(2,1)S(1)}, bf16[256,512]{1,0:T(8,128)(2,1)S(1)}, u32[]{:S(2)}, u32[]{:S(2)}) %collective-permute-start.12) | collective-permute-done | bytes 262176 | tf_op jit(solution)/shard_map/n_near_last/ppermute | solution.py:302
  65.8 2.3 %n_attend_last.1 = bf16[1024,256]{1,0:T(8,128)(2,1)} custom-call(s32[3]{0:T(128)S(1)} %pad_add_fusion.info, bf16[768,256]{1,0:T(8,128)(2,1)S(1)} %get-tuple-element.47.q, bf16[256,256]{1,0:T(8,128)(2,1)S(1)} %get-tuple-element.73.qd, bf16[256,512]{1,0:T(8,128)(2,1)S(1)} %collective-permute-done.12.near, bf16[256,512]{1,0:T(8,128)(2,1)S(1)} %get-tuple-element.74.far, ...), custom_call_target="tpu_custom_call" | custom-call | tf_op jit(solution)/shard_map/n_attend_last/pallas_call | solution.py:48
  (3 shorter events, 0.0 us)
Async XLA Ops:
  0.0 11.5 %collective-permute-start.3 = (bf16[256,1024]{1,0:T(8,128)(2,1)}, bf16[256,1024]{1,0:T(8,128)(2,1)S(1)}, u32[]{:S(2)}, u32[]{:S(2)}) collective-permute-start(bf16[256,1024]{1,0:T(8,128)(2,1)} %x.1), channel_id=1, source_target_pairs={{508,60},{509,53},{510,54},{511,63},{28,28},{29,21},{30,22},{31,31... | collective-permute-start | bytes 1572872 | tf_op jit(solution)/shard_map/n_aside3/ppermute | solution.py:302
  0.7 16.8 %collective-permute-start.2 = (bf16[256,1024]{1,0:T(8,128)(2,1)}, bf16[256,1024]{1,0:T(8,128)(2,1)S(1)}, u32[]{:S(2)}, u32[]{:S(2)}) collective-permute-start(bf16[256,1024]{1,0:T(8,128)(2,1)} %x.1), channel_id=1, source_target_pairs={{510,0},{511,1},{508,2},{509,3},{30,32},{31,33},{28,34},{29,35},{6... | collective-permute-start | bytes 1572872 | tf_op jit(solution)/shard_map/n_across2/ppermute | solution.py:302
  1.4 16.8 %collective-permute-start.10 = (bf16[256,1024]{1,0:T(8,128)(2,1)}, bf16[256,1024]{1,0:T(8,128)(2,1)S(1)}, u32[]{:S(2)}, u32[]{:S(2)}) collective-permute-start(bf16[256,1024]{1,0:T(8,128)(2,1)} %x.1), channel_id=1, source_target_pairs={{508,52},{509,37},{510,38},{511,55},{28,20},{29,5},{30,6},{31,23},... | collective-permute-start | bytes 1572872 | tf_op jit(solution)/shard_map/n_aside1/ppermute | solution.py:302
  2.1 32.7 %collective-permute-start.1 = (bf16[256,1024]{1,0:T(8,128)(2,1)}, bf16[256,1024]{1,0:T(8,128)(2,1)S(1)}, u32[]{:S(2)}, u32[]{:S(2)}) collective-permute-start(bf16[256,1024]{1,0:T(8,128)(2,1)} %x.1), channel_id=1, source_target_pairs={{0,2},{1,3},{2,0},{3,1},{4,6},{5,7},{6,4},{7,5},{8,10},{9,11},{10,... | collective-permute-start | bytes 1572872 | tf_op jit(solution)/shard_map/n_xc/ppermute | solution.py:302
  6.1 35.6 %collective-permute-start = (bf16[256,1024]{1,0:T(8,128)(2,1)}, bf16[256,1024]{1,0:T(8,128)(2,1)S(1)}, u32[]{:S(2)}, u32[]{:S(2)}) collective-permute-start(bf16[256,1024]{1,0:T(8,128)(2,1)} %x.1), channel_id=1, source_target_pairs={{0,1},{1,0},{2,3},{3,2},{4,5},{5,4},{6,7},{7,6},{8,9},{9,8},{10,11... | collective-permute-start | bytes 1572872 | tf_op jit(solution)/shard_map/n_xb/ppermute | solution.py:302
  8.8 0.7 copy-start.8
  11.5 33.9 %collective-permute-start.4 = (bf16[256,1024]{1,0:T(8,128)(2,1)S(1)}, bf16[256,1024]{1,0:T(8,128)(2,1)S(1)}, u32[]{:S(2)}, u32[]{:S(2)}) collective-permute-start(bf16[256,1024]{1,0:T(8,128)(2,1)S(1)} %collective-permute-done.3), channel_id=1, source_target_pairs={{63,0},{54,1},{53,2},{60,3},{31,32},{22,33},{21,34},{28,35},{127,6... | collective-permute-start | bytes 1572872 | tf_op jit(solution)/shard_map/n_across3/ppermute | solution.py:302
  12.2 1.0 %copy-start = (bf16[1024,256]{1,0:T(8,128)(2,1)S(1)}, bf16[1024,256]{1,0:T(8,128)(2,1)}, u32[]{:S(2)}) copy-start(bf16[1024,256]{1,0:T(8,128)(2,1)} %wq.5) | copy-start | bytes 1572868
  13.2 1.0 %copy-start.2 = (bf16[1024,256]{1,0:T(8,128)(2,1)S(1)}, bf16[1024,256]{1,0:T(8,128)(2,1)}, u32[]{:S(2)}) copy-start(bf16[1024,256]{1,0:T(8,128)(2,1)} %wk.7) | copy-start | bytes 1572868
  14.3 1.0 %copy-start.4 = (bf16[1024,256]{1,0:T(8,128)(2,1)S(1)}, bf16[1024,256]{1,0:T(8,128)(2,1)}, u32[]{:S(2)}) copy-start(bf16[1024,256]{1,0:T(8,128)(2,1)} %wv.7) | copy-start | bytes 1572868
  15.3 1.0 %copy-start.6 = (bf16[256,1024]{1,0:T(8,128)(2,1)S(1)}, bf16[256,1024]{1,0:T(8,128)(2,1)}, u32[]{:S(2)}) copy-start(bf16[256,1024]{1,0:T(8,128)(2,1)} %x.1) | copy-start | bytes 1572868
  17.5 1.4 %collective-permute-start.8 = (bf16[256,512]{1,0:T(8,128)(2,1)S(1)}, bf16[256,512]{1,0:T(8,128)(2,1)S(1)}, u32[]{:S(2)}, u32[]{:S(2)}) collective-permute-start(bf16[256,512]{1,0:T(8,128)(2,1)S(1)} %get-tuple-element.46.kva), channel_id=1, source_target_pairs={{508,44},{509,45},{510,46},{511,47},{28,12},{29,13},{30,14},{31,15... | collective-permute-start | bytes 786440 | tf_op jit(solution)/shard_map/n_aside0/ppermute | solution.py:302
  18.2 31.6 %collective-permute-start.11 = (bf16[256,1024]{1,0:T(8,128)(2,1)S(1)}, bf16[256,1024]{1,0:T(8,128)(2,1)S(1)}, u32[]{:S(2)}, u32[]{:S(2)}) collective-permute-start(bf16[256,1024]{1,0:T(8,128)(2,1)S(1)} %collective-permute-done.10), channel_id=1, source_target_pairs={{37,0},{52,1},{55,2},{38,3},{5,32},{20,33},{23,34},{6,35},{101,64}... | collective-permute-start | bytes 1572872 | tf_op jit(solution)/shard_map/n_across1/ppermute | solution.py:302
  18.9 30.9 %collective-permute-start.9 = (bf16[256,512]{1,0:T(8,128)(2,1)S(1)}, bf16[256,512]{1,0:T(8,128)(2,1)S(1)}, u32[]{:S(2)}, u32[]{:S(2)}) collective-permute-start(bf16[256,512]{1,0:T(8,128)(2,1)S(1)} %collective-permute-done.8), channel_id=1, source_target_pairs={{44,0},{45,1},{46,2},{47,3},{12,32},{13,33},{14,34},{15,35},{108,6... | collective-permute-start | bytes 786440 | tf_op jit(solution)/shard_map/n_across0/ppermute | solution.py:302
  34.8 6.9 %copy-start.7 = (bf16[256,1024]{1,0:T(8,128)(2,1)S(1)}, bf16[256,1024]{1,0:T(8,128)(2,1)}, u32[]{:S(2)}) copy-start(bf16[256,1024]{1,0:T(8,128)(2,1)} %x.1) | copy-start | bytes 1572868
  34.8 9.5 %copy-start.1 = (bf16[1024,256]{1,0:T(8,128)(2,1)S(1)}, bf16[1024,256]{1,0:T(8,128)(2,1)}, u32[]{:S(2)}) copy-start(bf16[1024,256]{1,0:T(8,128)(2,1)} %wq.5) | copy-start | bytes 1572868
  34.8 9.5 %copy-start.3 = (bf16[1024,256]{1,0:T(8,128)(2,1)S(1)}, bf16[1024,256]{1,0:T(8,128)(2,1)}, u32[]{:S(2)}) copy-start(bf16[1024,256]{1,0:T(8,128)(2,1)} %wk.7) | copy-start | bytes 1572868
  34.8 9.5 %copy-start.5 = (bf16[1024,256]{1,0:T(8,128)(2,1)S(1)}, bf16[1024,256]{1,0:T(8,128)(2,1)}, u32[]{:S(2)}) copy-start(bf16[1024,256]{1,0:T(8,128)(2,1)} %wv.7) | copy-start | bytes 1572868
  34.9 15.6 %collective-permute-start.7 = (bf16[256,1024]{1,0:T(8,128)(2,1)S(1)}, bf16[256,1024]{1,0:T(8,128)(2,1)S(1)}, u32[]{:S(2)}, u32[]{:S(2)}) collective-permute-start(bf16[256,1024]{1,0:T(8,128)(2,1)S(1)} %collective-permute-done.1.refs_0_.xc), channel_id=1, source_target_pairs={{2,3},{1,0},{6,7},{5,4},{10,11},{9,8},{14,15},{13,12},{18,19},{17,... | collective-permute-start | bytes 1572872 | tf_op jit(solution)/shard_map/n_outer/ppermute | solution.py:302
  41.8 15.4 %collective-permute-start.6 = (bf16[256,1024]{1,0:T(8,128)(2,1)S(1)}, bf16[256,1024]{1,0:T(8,128)(2,1)S(1)}, u32[]{:S(2)}, u32[]{:S(2)}) collective-permute-start(bf16[256,1024]{1,0:T(8,128)(2,1)S(1)} %copy-done.7), channel_id=1, source_target_pairs={{1,2},{2,1},{5,6},{6,5},{9,10},{10,9},{13,14},{14,13},{17,18},{18,... | collective-permute-start | bytes 1572872 | tf_op jit(solution)/shard_map/n_inner/ppermute | solution.py:302
  45.4 14.7 %collective-permute-start.5 = (bf16[768,512]{1,0:T(8,128)(2,1)S(1)}, bf16[768,512]{1,0:T(8,128)(2,1)S(1)}, u32[]{:S(2)}, u32[]{:S(2)}) collective-permute-start(bf16[768,512]{1,0:T(8,128)(2,1)S(1)} %get-tuple-element.49.kv), channel_id=1, source_target_pairs={{0,4},{1,5},{2,6},{3,7},{4,8},{5,9},{6,10},{7,11},{8,12},{9,13},{1... | collective-permute-start | bytes 2359304 | tf_op jit(solution)/shard_map/n_near/ppermute | solution.py:302
  58.1 7.7 %collective-permute-start.12 = (bf16[256,512]{1,0:T(8,128)(2,1)S(1)}, bf16[256,512]{1,0:T(8,128)(2,1)S(1)}, u32[]{:S(2)}, u32[]{:S(2)}) collective-permute-start(bf16[256,512]{1,0:T(8,128)(2,1)S(1)} %n_last.1.kvd), channel_id=1, source_target_pairs={{0,4},{1,5},{2,6},{3,7},{4,8},{5,9},{6,10},{7,11},{8,12},{9,13},{1... | collective-permute-start | bytes 786440 | tf_op jit(solution)/shard_map/n_near_last/ppermute | solution.py:302

commit v4 on v3

--- a/solution.py
+++ b/solution.py
@@ -17,7 +17,7 @@
 SCALE = math.log2(math.e) / math.sqrt(HD)
 ROW = 8
 LAST = ROW - 1
-LEAVE = ((3,) * 4, (5, 1, 1, 5), None, (LAST, 5, 5, LAST))
+LEAVE = ((1,) * 4, (5, 3, 3, 5), None, (LAST, 5, 5, LAST))
 
 BF16 = jnp.bfloat16
 F32 = jnp.float32
@@ -56,16 +56,12 @@
     return jnp.dot(rows, weight, preferred_element_type=F32).astype(BF16)
 
 
-def project_query(rows, weight):
-    return (jnp.dot(rows, weight, preferred_element_type=F32) * SCALE).astype(BF16)
-
-
 def head(number):
     return slice(number * HD, (number + 1) * HD)
 
 
 def scores(keys, query):
-    return dot(keys, query, ((1,), (1,)))
+    return dot(keys, query, ((1,), (1,))) * SCALE
 
 
 def mixed(values, weights):
@@ -95,7 +91,7 @@
 
 
 def project_own_body(info, x, wq, wk, wv, q, kv):
-    q[...] = project_query(x[...], wq[...])
+    q[...] = project(x[...], wq[...])
     kv[:, :WIDTH] = project(x[...], wk[...])
     kv[:, WIDTH:] = project(x[...], wv[...])
 
@@ -105,7 +101,7 @@
     kv[:CHUNK] = kva[...]
     for place, x in ((1, xb), (2, xc)):
         rows = slice(place * CHUNK, (place + 1) * CHUNK)
-        q[rows] = project_query(x[...], wq[...])
+        q[rows] = project(x[...], wq[...])
         kv[rows, :WIDTH] = project(x[...], wk[...])
         kv[rows, WIDTH:] = project(x[...], wv[...])
 
@@ -124,18 +120,17 @@
     pl.when(jnp.logical_not(middle))(lambda: work(outer))
 
 
-def project_far_body(info, kva, xb, xc, xd, wk, wv, kv, kvd, x, w, sems):
+def project_far_body(info, xb, xc, xd, wk, wv, kv, kvd, x, w, sems):
     @pl.when(info[2] == 1)
     def _():
         copies = [pltpu.make_async_copy(source, x.at[n], sems.at[n]) for n, source in enumerate((xb, xc, xd))]
         copies += [pltpu.make_async_copy(source, w.at[n], sems.at[3 + n]) for n, source in enumerate((wk, wv))]
-        copies.append(pltpu.make_async_copy(kva, kv.at[:CHUNK], sems.at[5]))
         for copy in copies:
             copy.start()
         for copy in copies:
             copy.wait()
         for n in range(3):
-            out, rows = (kv, slice((n + 1) * CHUNK, (n + 2) * CHUNK)) if n < 2 else (kvd, slice(0, CHUNK))
+            out, rows = (kv, slice(n * CHUNK, (n + 1) * CHUNK)) if n < 2 else (kvd, slice(0, CHUNK))
             out[rows, :WIDTH] = project(x[n], w[0])
             out[rows, WIDTH:] = project(x[n], w[1])
 
@@ -178,18 +173,21 @@
     return results
 
 
-def middle_body(info, outer, inner, wq, q, kv, kvd, near, far, state0, mix0, state, mix, qd, held):
+def middle_body(info, outer, inner, wq, q, kv, kvd, near, far_a, far, state0, mix0, state, mix, qd, held):
     middle = jnp.logical_or(info[0] == 1, info[0] == 2)
 
     def query(x):
-        qd[...] = project_query(x[...], wq[...])
-
-    def hold(x):
-        held[...] = x[...]
+        qd[...] = project(x[...], wq[...])
+
+    def hold(*parts):
+        start = 0
+        for part in parts:
+            held[start : start + part.shape[0]] = part[...]
+            start += part.shape[0]
 
     pl.when(middle)(lambda: query(inner))
     pl.when(jnp.logical_not(middle))(lambda: query(outer))
-    pl.when(info[2] == 1)(lambda: hold(far))
+    pl.when(info[2] == 1)(lambda: hold(far_a, far))
     pl.when(info[2] == 0)(lambda: hold(near))
     tp = info[0]
     last = tp ^ 3
@@ -363,15 +361,14 @@
     state, mix = run(
         "attend_own",
         own_first_body, STATE, [SMEM] + [VMEM] * 2, 0, info, q, kv)
-    mix, far_a, far_b, far_c, far_d = lax.optimization_barrier((mix, far_a, far_b, far_c, far_d))
+    mix, far_b, far_c, far_d = lax.optimization_barrier((mix, far_b, far_c, far_d))
     far, far_last = run(
         "far",
         project_far_body,
-        (shape(HEAD, 2 * WIDTH), shape(CHUNK, 2 * WIDTH)),
-        [SMEM] + [ANY] * 6,
+        (shape(2 * CHUNK, 2 * WIDTH), shape(CHUNK, 2 * WIDTH)),
+        [SMEM] + [ANY] * 5,
         FAR,
         info,
-        far_a,
         far_b,
         far_c,
         far_d,
@@ -380,10 +377,10 @@
         scratch=(
             pltpu.VMEM((3, CHUNK, DEPTH), BF16),
             pltpu.VMEM((2, DEPTH, WIDTH), BF16),
-            pltpu.SemaphoreType.DMA((6,)),
+            pltpu.SemaphoreType.DMA((5,)),
         ),
     )
-    outer, far = lax.optimization_barrier((outer, far))
+    outer, far, far_a = lax.optimization_barrier((outer, far, far_a))
     passed = run("gate", gate_body, shape(8, 128, F32), [ANY] * 2, GATE, outer, passed)
     inner, passed = lax.optimization_barrier((inner, passed))
     kvd = run(
@@ -405,7 +402,7 @@
         "attend_most",
         middle_body,
         (*STATE, shape(CHUNK, WIDTH)),
-        [SMEM] + [VMEM] * 10,
+        [SMEM] + [VMEM] * 11,
         0,
         info,
         outer,
@@ -415,10 +412,11 @@
         kv,
         kvd,
         near,
+        far_a,
         far,
         state,
         mix,
-        alias={9: 0, 10: 1},
+        alias={10: 0, 11: 1},
         scratch=(pltpu.VMEM((HEAD, 2 * WIDTH), BF16),),
     )
     return run(

time: 68.7 us -> 69 us (level)
  the two profiles are of different devices: /device:TPU:52 before, /device:TPU:179 now
where the time goes in v4:
time: 69 us; the launch traced here: 68.2 us
  starting transfers between devices  35 us (51%)
  Pallas kernels  13.5 us (20%)
  waiting for transfers between devices  12.4 us (18%)
  local copies, waits for them, and re-layouts  5.48 us (8%)
  between operations  1.65 us (2%)
    ppermute x13, starting transfers between devices, send(): return lax.ppermute(x, ('ctx', 'tp'), route)  35 us
    pallas_call x10, Pallas kernels, run(): return call(*args)  13.5 us
    ppermute x13, waiting for transfers between devices, send(): return lax.ppermute(x, ('ctx', 'tp'), route)  12.4 us
    unnamed x18, local copies, waits for them, and re-layouts  4.83 us
  transfers between devices with their start and end apart: 13, of which 3 were waited for; matrix products, arithmetic and copies ran while one was open for 1% of the time, Pallas kernels for 16%

profile of v4, /device:TPU:179, one launch (start us, length us, event | category | flops | bytes accessed | tf_op | source)
XLA Modules:
  0.0 68.2 jit_solution(10301039881985428371)
XLA Ops:
  0.0 1.5 %collective-permute-start.3 = (bf16[256,1024]{1,0:T(8,128)(2,1)}, bf16[256,1024]{1,0:T(8,128)(2,1)}, u32[]{:S(2)}, u32[]{:S(2)}) collective-permute-start(bf16[256,1024]{1,0:T(8,128)(2,1)} %x.1), channel_id=1, source_target_pairs={{508,60},{509,53},{510,54},{511,63},{28,28},{29,21},{30,22},{31,31... | collective-permute-start | bytes 1572872 | tf_op jit(solution)/shard_map/n_aside3/ppermute | solution.py:300
  1.5 1.3 %collective-permute-start.8 = (bf16[256,1024]{1,0:T(8,128)(2,1)}, bf16[256,1024]{1,0:T(8,128)(2,1)S(1)}, u32[]{:S(2)}, u32[]{:S(2)}) collective-permute-start(bf16[256,1024]{1,0:T(8,128)(2,1)} %x.1), channel_id=1, source_target_pairs={{508,52},{509,45},{510,46},{511,55},{28,20},{29,13},{30,14},{31,23... | collective-permute-start | bytes 1572872 | tf_op jit(solution)/shard_map/n_aside1/ppermute | solution.py:300
  2.8 0.7 %collective-permute-start.2 = (bf16[256,1024]{1,0:T(8,128)(2,1)}, bf16[256,1024]{1,0:T(8,128)(2,1)S(1)}, u32[]{:S(2)}, u32[]{:S(2)}) collective-permute-start(bf16[256,1024]{1,0:T(8,128)(2,1)} %x.1), channel_id=1, source_target_pairs={{510,0},{511,1},{508,2},{509,3},{30,32},{31,33},{28,34},{29,35},{6... | collective-permute-start | bytes 1572872 | tf_op jit(solution)/shard_map/n_across2/ppermute | solution.py:300
  3.5 3.2 %collective-permute-start.1 = (bf16[256,1024]{1,0:T(8,128)(2,1)}, bf16[256,1024]{1,0:T(8,128)(2,1)S(1)}, u32[]{:S(2)}, u32[]{:S(2)}) collective-permute-start(bf16[256,1024]{1,0:T(8,128)(2,1)} %x.1), channel_id=1, source_target_pairs={{0,2},{1,3},{2,0},{3,1},{4,6},{5,7},{6,4},{7,5},{8,10},{9,11},{10,... | collective-permute-start | bytes 1572872 | tf_op jit(solution)/shard_map/n_xc/ppermute | solution.py:300
  6.6 2.9 %collective-permute-start = (bf16[256,1024]{1,0:T(8,128)(2,1)}, bf16[256,1024]{1,0:T(8,128)(2,1)S(1)}, u32[]{:S(2)}, u32[]{:S(2)}) collective-permute-start(bf16[256,1024]{1,0:T(8,128)(2,1)} %x.1), channel_id=1, source_target_pairs={{0,1},{1,0},{2,3},{3,2},{4,5},{5,4},{6,7},{7,6},{8,9},{9,8},{10,11... | collective-permute-start | bytes 1572872 | tf_op jit(solution)/shard_map/n_xb/ppermute | solution.py:300
  9.6 0.0 collective-permute-done.3
  9.6 0.7 %collective-permute-start.4 = (bf16[256,1024]{1,0:T(8,128)(2,1)}, bf16[256,1024]{1,0:T(8,128)(2,1)S(1)}, u32[]{:S(2)}, u32[]{:S(2)}) collective-permute-start(bf16[256,1024]{1,0:T(8,128)(2,1)} %collective-permute-done.3), channel_id=1, source_target_pairs={{63,0},{54,1},{53,2},{60,3},{31,32},{22,33},{21,34},{28,35},{127,6... | collective-permute-start | bytes 1572872 | tf_op jit(solution)/shard_map/n_across3/ppermute | solution.py:300
  10.3 7.3 %collective-permute-done.8 = bf16[256,1024]{1,0:T(8,128)(2,1)S(1)} collective-permute-done((bf16[256,1024]{1,0:T(8,128)(2,1)}, bf16[256,1024]{1,0:T(8,128)(2,1)S(1)}, u32[]{:S(2)}, u32[]{:S(2)}) %collective-permute-start.8) | collective-permute-done | bytes 524320 | tf_op jit(solution)/shard_map/n_aside1/ppermute | solution.py:300
  17.6 1.3 %collective-permute-start.9 = (bf16[256,1024]{1,0:T(8,128)(2,1)S(1)}, bf16[256,1024]{1,0:T(8,128)(2,1)S(1)}, u32[]{:S(2)}, u32[]{:S(2)}) collective-permute-start(bf16[256,1024]{1,0:T(8,128)(2,1)S(1)} %collective-permute-done.8), channel_id=1, source_target_pairs={{45,0},{52,1},{55,2},{46,3},{13,32},{20,33},{23,34},{14,35},{109,6... | collective-permute-start | bytes 1572872 | tf_op jit(solution)/shard_map/n_across1/ppermute | solution.py:300
  18.9 0.0 copy-start.8
  18.9 0.6 copy-done.8
  19.6 0.7 fusion
  21.6 0.1 pad_add_fusion.info
  21.6 0.0 copy-start
  21.6 1.0 %copy-done = bf16[1024,256]{1,0:T(8,128)(2,1)S(1)} copy-done((bf16[1024,256]{1,0:T(8,128)(2,1)S(1)}, bf16[1024,256]{1,0:T(8,128)(2,1)}, u32[]{:S(2)}) %copy-start) | copy-done | bytes 524312
  22.7 0.0 copy-start.2
  22.7 1.0 %copy-done.2 = bf16[1024,256]{1,0:T(8,128)(2,1)S(1)} copy-done((bf16[1024,256]{1,0:T(8,128)(2,1)S(1)}, bf16[1024,256]{1,0:T(8,128)(2,1)}, u32[]{:S(2)}) %copy-start.2) | copy-done | bytes 524312
  23.7 0.0 copy-start.4
  23.7 1.0 %copy-done.4 = bf16[1024,256]{1,0:T(8,128)(2,1)S(1)} copy-done((bf16[1024,256]{1,0:T(8,128)(2,1)S(1)}, bf16[1024,256]{1,0:T(8,128)(2,1)}, u32[]{:S(2)}) %copy-start.4) | copy-done | bytes 524312
  24.8 0.0 copy-start.6
  24.8 1.0 %copy-done.6 = bf16[256,1024]{1,0:T(8,128)(2,1)S(1)} copy-done((bf16[256,1024]{1,0:T(8,128)(2,1)S(1)}, bf16[256,1024]{1,0:T(8,128)(2,1)}, u32[]{:S(2)}) %copy-start.6) | copy-done | bytes 524312
  25.8 1.1 %n_own.1 = (bf16[256,256]{1,0:T(8,128)(2,1)S(1)}, bf16[256,512]{1,0:T(8,128)(2,1)S(1)}) custom-call(s32[3]{0:T(128)S(1)} %pad_add_fusion.info, bf16[256,1024]{1,0:T(8,128)(2,1)S(1)} %copy-done.6, bf16[1024,256]{1,0:T(8,128)(2,1)S(1)} %copy-done, bf16[1024,256]{1,0:T(8,128)(2,1)S(1)} %copy-done.2, bf16[1024,256]{1,0:T(8,128)(2,1)S(1)} %copy-done.4), custom_call_target="tpu_custom_call" | custom-call | tf_op jit(solution)/shard_map/n_own/pallas_call | solution.py:48
  26.9 0.0 collective-permute-done.2.refs_1_.xc
  26.9 0.7 collective-permute-start.10
  27.6 1.5 %collective-permute-done.1.refs_0_.xc = bf16[256,1024]{1,0:T(8,128)(2,1)S(1)} collective-permute-done((bf16[256,1024]{1,0:T(8,128)(2,1)}, bf16[256,1024]{1,0:T(8,128)(2,1)S(1)}, u32[]{:S(2)}, u32[]{:S(2)}) %collective-permute-start.1) | collective-permute-done | bytes 524320 | tf_op jit(solution)/shard_map/n_xc/ppermute | solution.py:300
  29.1 0.0 copy-start.7
  29.1 0.0 copy-start.1
  29.1 0.0 copy-start.3
  29.1 0.0 copy-start.5
  29.1 3.5 %collective-permute-start.7 = (bf16[256,1024]{1,0:T(8,128)(2,1)S(1)}, bf16[256,1024]{1,0:T(8,128)(2,1)S(1)}, u32[]{:S(2)}, u32[]{:S(2)}) collective-permute-start(bf16[256,1024]{1,0:T(8,128)(2,1)S(1)} %collective-permute-done.1.refs_0_.xc), channel_id=1, source_target_pairs={{2,3},{1,0},{6,7},{5,4},{10,11},{9,8},{14,15},{13,12},{18,19},{17,... | collective-permute-start | bytes 1572872 | tf_op jit(solution)/shard_map/n_outer/ppermute | solution.py:300
  32.7 3.6 %collective-permute-done.xb = bf16[256,1024]{1,0:T(8,128)(2,1)S(1)} collective-permute-done((bf16[256,1024]{1,0:T(8,128)(2,1)}, bf16[256,1024]{1,0:T(8,128)(2,1)S(1)}, u32[]{:S(2)}, u32[]{:S(2)}) %collective-permute-start) | collective-permute-done | bytes 524320 | tf_op jit(solution)/shard_map/n_xb/ppermute | solution.py:300
  36.3 0.0 copy-done.7
  36.3 2.7 %collective-permute-start.6 = (bf16[256,1024]{1,0:T(8,128)(2,1)S(1)}, bf16[256,1024]{1,0:T(8,128)(2,1)S(1)}, u32[]{:S(2)}, u32[]{:S(2)}) collective-permute-start(bf16[256,1024]{1,0:T(8,128)(2,1)S(1)} %copy-done.7), channel_id=1, source_target_pairs={{1,2},{2,1},{5,6},{6,5},{9,10},{10,9},{13,14},{14,13},{17,18},{18,... | collective-permute-start | bytes 1572872 | tf_op jit(solution)/shard_map/n_inner/ppermute | solution.py:300
  39.0 0.0 copy-done.1
  39.0 0.0 copy-done.3
  39.0 0.0 copy-done.5
  39.0 1.0 %n_middle.1 = (bf16[768,256]{1,0:T(8,128)(2,1)S(1)}, bf16[768,512]{1,0:T(8,128)(2,1)S(1)}) custom-call(bf16[256,1024]{1,0:T(8,128)(2,1)S(1)} %collective-permute-done.xb, bf16[256,1024]{1,0:T(8,128)(2,1)S(1)} %collective-permute-done.1.refs_0_.xc, bf16[256,256]{1,0:T(8,128)(2,1)S(1)} %get-tuple-element.45.qa, bf16[256,512]{1,0:T(8,128)(2,1)S(1)} %get-tuple-element.46.kva, ...), custom_call_target="tpu_custom_call" | custom-call | tf_op jit(solution)/shard_map/n_middle/pallas_call | solution.py:48
  40.1 0.0 collective-permute-done.10
  40.1 0.7 collective-permute-start.11
  40.8 0.0 collective-permute-done.4.xd
  40.8 9.3 %collective-permute-start.5 = (bf16[768,512]{1,0:T(8,128)(2,1)S(1)}, bf16[768,512]{1,0:T(8,128)(2,1)S(1)}, u32[]{:S(2)}, u32[]{:S(2)}) collective-permute-start(bf16[768,512]{1,0:T(8,128)(2,1)S(1)} %get-tuple-element.49.kv), channel_id=1, source_target_pairs={{0,4},{1,5},{2,6},{3,7},{4,8},{5,9},{6,10},{7,11},{8,12},{9,13},{1... | collective-permute-start | bytes 2359304 | tf_op jit(solution)/shard_map/n_near/ppermute | solution.py:300
  50.1 2.6 %n_attend_own.1 = (f32[8,1024]{1,0:T(8,128)S(1)}, f32[256,1024]{1,0:T(8,128)S(1)}) custom-call(s32[3]{0:T(128)S(1)} %pad_add_fusion.info, bf16[768,256]{1,0:T(8,128)(2,1)S(1)} %get-tuple-element.47.q, bf16[768,512]{1,0:T(8,128)(2,1)S(1)} %get-tuple-element.49.kv), custom_call_target="tpu_custom_call" | custom-call | tf_op jit(solution)/shard_map/n_attend_own/pallas_call | solution.py:48
  52.7 0.0 collective-permute-done.9.xb
  52.7 0.6 n_far.1
  53.3 0.0 collective-permute-done.7.refs_0_.outer
  53.3 0.0 collective-permute-done.11.far_a
  53.3 0.0 collective-permute-done.6.inner
  53.3 1.0 %n_last.1.kvd = bf16[256,512]{1,0:T(8,128)(2,1)S(1)} custom-call(s32[3]{0:T(128)S(1)} %pad_add_fusion.info, f32[8,128]{1,0:T(8,128)S(1)} %n_gate.1.passed, bf16[256,1024]{1,0:T(8,128)(2,1)S(1)} %collective-permute-done.7.refs_0_.outer, bf16[256,1024]{1,0:T(8,128)(2,1)S(1)} %collective-permute-done.6.inner, bf16[1024,256]{1,0:T(8,128)(2,1)S(1)} %copy-done.3, ...), custom_call_target="tpu_custom_call" | custom-call | flops 20000000000 | tf_op jit(solution)/shard_map/n_last/pallas_call | solution.py:48
  54.3 6.6 %collective-permute-start.12 = (bf16[256,512]{1,0:T(8,128)(2,1)S(1)}, bf16[256,512]{1,0:T(8,128)(2,1)S(1)}, u32[]{:S(2)}, u32[]{:S(2)}) collective-permute-start(bf16[256,512]{1,0:T(8,128)(2,1)S(1)} %n_last.1.kvd), channel_id=1, source_target_pairs={{0,4},{1,5},{2,6},{3,7},{4,8},{5,9},{6,10},{7,11},{8,12},{9,13},{1... | collective-permute-start | bytes 786440 | tf_op jit(solution)/shard_map/n_near_last/ppermute | solution.py:300
  60.9 0.0 collective-permute-done.5.near
  60.9 4.8 %n_attend_most.1 = (f32[8,1024]{1,0:T(8,128)S(1)}, f32[256,1024]{1,0:T(8,128)S(1)}, bf16[256,256]{1,0:T(8,128)(2,1)S(1)}) custom-call(s32[3]{0:T(128)S(1)} %pad_add_fusion.info, bf16[256,1024]{1,0:T(8,128)(2,1)S(1)} %collective-permute-done.7.refs_0_.outer, ...), custom_call_target="tpu_custom_call", output_to_operand_aliasing={{0}: (10, {}), {1}: (11, {})} | custom-call | tf_op jit(solution)/shard_map/n_attend_most/pallas_call | solution.py:48
  65.8 0.0 collective-permute-done.12.near
  65.8 2.4 %n_attend_last.1 = bf16[1024,256]{1,0:T(8,128)(2,1)} custom-call(s32[3]{0:T(128)S(1)} %pad_add_fusion.info, bf16[768,256]{1,0:T(8,128)(2,1)S(1)} %get-tuple-element.47.q, bf16[256,256]{1,0:T(8,128)(2,1)S(1)} %get-tuple-element.73.qd, bf16[256,512]{1,0:T(8,128)(2,1)S(1)} %collective-permute-done.12.near, bf16[256,512]{1,0:T(8,128)(2,1)S(1)} %get-tuple-element.74.far, ...), custom_call_target="tpu_custom_call" | custom-call | tf_op jit(solution)/shard_map/n_attend_last/pallas_call | solution.py:48
  (3 shorter events, 0.0 us)
Async XLA Ops:
  0.0 9.6 %collective-permute-start.3 = (bf16[256,1024]{1,0:T(8,128)(2,1)}, bf16[256,1024]{1,0:T(8,128)(2,1)}, u32[]{:S(2)}, u32[]{:S(2)}) collective-permute-start(bf16[256,1024]{1,0:T(8,128)(2,1)} %x.1), channel_id=1, source_target_pairs={{508,60},{509,53},{510,54},{511,63},{28,28},{29,21},{30,22},{31,31... | collective-permute-start | bytes 1572872 | tf_op jit(solution)/shard_map/n_aside3/ppermute | solution.py:300
  1.5 16.1 %collective-permute-start.8 = (bf16[256,1024]{1,0:T(8,128)(2,1)}, bf16[256,1024]{1,0:T(8,128)(2,1)S(1)}, u32[]{:S(2)}, u32[]{:S(2)}) collective-permute-start(bf16[256,1024]{1,0:T(8,128)(2,1)} %x.1), channel_id=1, source_target_pairs={{508,52},{509,45},{510,46},{511,55},{28,20},{29,13},{30,14},{31,23... | collective-permute-start | bytes 1572872 | tf_op jit(solution)/shard_map/n_aside1/ppermute | solution.py:300
  2.8 24.2 %collective-permute-start.2 = (bf16[256,1024]{1,0:T(8,128)(2,1)}, bf16[256,1024]{1,0:T(8,128)(2,1)S(1)}, u32[]{:S(2)}, u32[]{:S(2)}) collective-permute-start(bf16[256,1024]{1,0:T(8,128)(2,1)} %x.1), channel_id=1, source_target_pairs={{510,0},{511,1},{508,2},{509,3},{30,32},{31,33},{28,34},{29,35},{6... | collective-permute-start | bytes 1572872 | tf_op jit(solution)/shard_map/n_across2/ppermute | solution.py:300
  3.5 25.6 %collective-permute-start.1 = (bf16[256,1024]{1,0:T(8,128)(2,1)}, bf16[256,1024]{1,0:T(8,128)(2,1)S(1)}, u32[]{:S(2)}, u32[]{:S(2)}) collective-permute-start(bf16[256,1024]{1,0:T(8,128)(2,1)} %x.1), channel_id=1, source_target_pairs={{0,2},{1,3},{2,0},{3,1},{4,6},{5,7},{6,4},{7,5},{8,10},{9,11},{10,... | collective-permute-start | bytes 1572872 | tf_op jit(solution)/shard_map/n_xc/ppermute | solution.py:300
  6.6 29.6 %collective-permute-start = (bf16[256,1024]{1,0:T(8,128)(2,1)}, bf16[256,1024]{1,0:T(8,128)(2,1)S(1)}, u32[]{:S(2)}, u32[]{:S(2)}) collective-permute-start(bf16[256,1024]{1,0:T(8,128)(2,1)} %x.1), channel_id=1, source_target_pairs={{0,1},{1,0},{2,3},{3,2},{4,5},{5,4},{6,7},{7,6},{8,9},{9,8},{10,11... | collective-permute-start | bytes 1572872 | tf_op jit(solution)/shard_map/n_xb/ppermute | solution.py:300
  9.6 31.2 %collective-permute-start.4 = (bf16[256,1024]{1,0:T(8,128)(2,1)}, bf16[256,1024]{1,0:T(8,128)(2,1)S(1)}, u32[]{:S(2)}, u32[]{:S(2)}) collective-permute-start(bf16[256,1024]{1,0:T(8,128)(2,1)} %collective-permute-done.3), channel_id=1, source_target_pairs={{63,0},{54,1},{53,2},{60,3},{31,32},{22,33},{21,34},{28,35},{127,6... | collective-permute-start | bytes 1572872 | tf_op jit(solution)/shard_map/n_across3/ppermute | solution.py:300
  17.6 35.1 %collective-permute-start.9 = (bf16[256,1024]{1,0:T(8,128)(2,1)S(1)}, bf16[256,1024]{1,0:T(8,128)(2,1)S(1)}, u32[]{:S(2)}, u32[]{:S(2)}) collective-permute-start(bf16[256,1024]{1,0:T(8,128)(2,1)S(1)} %collective-permute-done.8), channel_id=1, source_target_pairs={{45,0},{52,1},{55,2},{46,3},{13,32},{20,33},{23,34},{14,35},{109,6... | collective-permute-start | bytes 1572872 | tf_op jit(solution)/shard_map/n_across1/ppermute | solution.py:300
  18.9 0.7 copy-start.8
  21.6 1.0 %copy-start = (bf16[1024,256]{1,0:T(8,128)(2,1)S(1)}, bf16[1024,256]{1,0:T(8,128)(2,1)}, u32[]{:S(2)}) copy-start(bf16[1024,256]{1,0:T(8,128)(2,1)} %wq.5) | copy-start | bytes 1572868
  22.7 1.0 %copy-start.2 = (bf16[1024,256]{1,0:T(8,128)(2,1)S(1)}, bf16[1024,256]{1,0:T(8,128)(2,1)}, u32[]{:S(2)}) copy-start(bf16[1024,256]{1,0:T(8,128)(2,1)} %wk.7) | copy-start | bytes 1572868
  23.7 1.0 %copy-start.4 = (bf16[1024,256]{1,0:T(8,128)(2,1)S(1)}, bf16[1024,256]{1,0:T(8,128)(2,1)}, u32[]{:S(2)}) copy-start(bf16[1024,256]{1,0:T(8,128)(2,1)} %wv.7) | copy-start | bytes 1572868
  24.8 1.0 %copy-start.6 = (bf16[256,1024]{1,0:T(8,128)(2,1)S(1)}, bf16[256,1024]{1,0:T(8,128)(2,1)}, u32[]{:S(2)}) copy-start(bf16[256,1024]{1,0:T(8,128)(2,1)} %x.1) | copy-start | bytes 1572868
  26.9 13.1 %collective-permute-start.10 = (bf16[256,512]{1,0:T(8,128)(2,1)S(1)}, bf16[256,512]{1,0:T(8,128)(2,1)S(1)}, u32[]{:S(2)}, u32[]{:S(2)}) collective-permute-start(bf16[256,512]{1,0:T(8,128)(2,1)S(1)} %get-tuple-element.46.kva), channel_id=1, source_target_pairs={{508,36},{509,37},{510,38},{511,39},{28,4},{29,5},{30,6},{31,7},{6... | collective-permute-start | bytes 786440 | tf_op jit(solution)/shard_map/n_aside0/ppermute | solution.py:300
  29.1 7.2 %copy-start.7 = (bf16[256,1024]{1,0:T(8,128)(2,1)S(1)}, bf16[256,1024]{1,0:T(8,128)(2,1)}, u32[]{:S(2)}) copy-start(bf16[256,1024]{1,0:T(8,128)(2,1)} %x.1) | copy-start | bytes 1572868
  29.1 9.9 %copy-start.1 = (bf16[1024,256]{1,0:T(8,128)(2,1)S(1)}, bf16[1024,256]{1,0:T(8,128)(2,1)}, u32[]{:S(2)}) copy-start(bf16[1024,256]{1,0:T(8,128)(2,1)} %wq.5) | copy-start | bytes 1572868
  29.1 9.9 %copy-start.3 = (bf16[1024,256]{1,0:T(8,128)(2,1)S(1)}, bf16[1024,256]{1,0:T(8,128)(2,1)}, u32[]{:S(2)}) copy-start(bf16[1024,256]{1,0:T(8,128)(2,1)} %wk.7) | copy-start | bytes 1572868
  29.1 9.9 %copy-start.5 = (bf16[1024,256]{1,0:T(8,128)(2,1)S(1)}, bf16[1024,256]{1,0:T(8,128)(2,1)}, u32[]{:S(2)}) copy-start(bf16[1024,256]{1,0:T(8,128)(2,1)} %wv.7) | copy-start | bytes 1572868
  29.1 24.1 %collective-permute-start.7 = (bf16[256,1024]{1,0:T(8,128)(2,1)S(1)}, bf16[256,1024]{1,0:T(8,128)(2,1)S(1)}, u32[]{:S(2)}, u32[]{:S(2)}) collective-permute-start(bf16[256,1024]{1,0:T(8,128)(2,1)S(1)} %collective-permute-done.1.refs_0_.xc), channel_id=1, source_target_pairs={{2,3},{1,0},{6,7},{5,4},{10,11},{9,8},{14,15},{13,12},{18,19},{17,... | collective-permute-start | bytes 1572872 | tf_op jit(solution)/shard_map/n_outer/ppermute | solution.py:300
  36.3 17.0 %collective-permute-start.6 = (bf16[256,1024]{1,0:T(8,128)(2,1)S(1)}, bf16[256,1024]{1,0:T(8,128)(2,1)S(1)}, u32[]{:S(2)}, u32[]{:S(2)}) collective-permute-start(bf16[256,1024]{1,0:T(8,128)(2,1)S(1)} %copy-done.7), channel_id=1, source_target_pairs={{1,2},{2,1},{5,6},{6,5},{9,10},{10,9},{13,14},{14,13},{17,18},{18,... | collective-permute-start | bytes 1572872 | tf_op jit(solution)/shard_map/n_inner/ppermute | solution.py:300
  40.1 13.2 %collective-permute-start.11 = (bf16[256,512]{1,0:T(8,128)(2,1)S(1)}, bf16[256,512]{1,0:T(8,128)(2,1)S(1)}, u32[]{:S(2)}, u32[]{:S(2)}) collective-permute-start(bf16[256,512]{1,0:T(8,128)(2,1)S(1)} %collective-permute-done.10), channel_id=1, source_target_pairs={{36,0},{37,1},{38,2},{39,3},{4,32},{5,33},{6,34},{7,35},{100,64},{... | collective-permute-start | bytes 786440 | tf_op jit(solution)/shard_map/n_across0/ppermute | solution.py:300
  40.8 20.2 %collective-permute-start.5 = (bf16[768,512]{1,0:T(8,128)(2,1)S(1)}, bf16[768,512]{1,0:T(8,128)(2,1)S(1)}, u32[]{:S(2)}, u32[]{:S(2)}) collective-permute-start(bf16[768,512]{1,0:T(8,128)(2,1)S(1)} %get-tuple-element.49.kv), channel_id=1, source_target_pairs={{0,4},{1,5},{2,6},{3,7},{4,8},{5,9},{6,10},{7,11},{8,12},{9,13},{1... | collective-permute-start | bytes 2359304 | tf_op jit(solution)/shard_map/n_near/ppermute | solution.py:300
  54.3 11.5 %collective-permute-start.12 = (bf16[256,512]{1,0:T(8,128)(2,1)S(1)}, bf16[256,512]{1,0:T(8,128)(2,1)S(1)}, u32[]{:S(2)}, u32[]{:S(2)}) collective-permute-start(bf16[256,512]{1,0:T(8,128)(2,1)S(1)} %n_last.1.kvd), channel_id=1, source_target_pairs={{0,4},{1,5},{2,6},{3,7},{4,8},{5,9},{6,10},{7,11},{8,12},{9,13},{1... | collective-permute-start | bytes 786440 | tf_op jit(solution)/shard_map/n_near_last/ppermute | solution.py:300

commit v5 on v4

--- a/solution.py
+++ b/solution.py
@@ -17,7 +17,7 @@
 SCALE = math.log2(math.e) / math.sqrt(HD)
 ROW = 8
 LAST = ROW - 1
-LEAVE = ((1,) * 4, (5, 3, 3, 5), None, (LAST, 5, 5, LAST))
+LEAVE = ((1,) * 4, (5, 3, 3, 5), None, (LAST, 1, 1, LAST))
 
 BF16 = jnp.bfloat16
 F32 = jnp.float32
@@ -173,7 +173,7 @@
     return results
 
 
-def middle_body(info, outer, inner, wq, q, kv, kvd, near, far_a, far, state0, mix0, state, mix, qd, held):
+def middle_body(info, passed, outer, inner, wq, q, kv, kvd, near, far_a, far, state0, mix0, state, mix, qd, held):
     middle = jnp.logical_or(info[0] == 1, info[0] == 2)
 
     def query(x):
@@ -380,7 +380,7 @@
             pltpu.SemaphoreType.DMA((5,)),
         ),
     )
-    outer, far, far_a = lax.optimization_barrier((outer, far, far_a))
+    outer, far = lax.optimization_barrier((outer, far))
     passed = run("gate", gate_body, shape(8, 128, F32), [ANY] * 2, GATE, outer, passed)
     inner, passed = lax.optimization_barrier((inner, passed))
     kvd = run(
@@ -388,7 +388,7 @@
         project_last_body,
         shape(CHUNK, 2 * WIDTH),
         [SMEM, ANY] + [VMEM] * 4,
-        EARLY,
+        0,
         info,
         passed,
         outer,
@@ -397,14 +397,16 @@
         w_value,
     )
     near_last = to_next("near_last", kvd)
-    near, kvd, outer, inner = lax.optimization_barrier((near, kvd, outer, inner))
+    passed = run("gate2", gate_body, shape(8, 128, F32), [ANY] * 2, EARLY, kvd, far_a)
+    near, kvd, outer, inner, passed = lax.optimization_barrier((near, kvd, outer, inner, passed))
     state, mix, qd = run(
         "attend_most",
         middle_body,
         (*STATE, shape(CHUNK, WIDTH)),
-        [SMEM] + [VMEM] * 11,
+        [SMEM, ANY] + [VMEM] * 11,
         0,
         info,
+        passed,
         outer,
         inner,
         w_query,
@@ -416,7 +418,7 @@
         far,
         state,
         mix,
-        alias={10: 0, 11: 1},
+        alias={11: 0, 12: 1},
         scratch=(pltpu.VMEM((HEAD, 2 * WIDTH), BF16),),
     )
     return run(

time: 69 us -> 68.2 us (0.988)
  the two profiles are of different devices: /device:TPU:179 before, /device:TPU:275 now
where the time goes in v5:
time: 68.2 us; the launch traced here: 67.4 us
  starting transfers between devices  40.8 us (60%)
  Pallas kernels  13.4 us (20%)
  waiting for transfers between devices  5.96 us (9%)
  local copies, waits for them, and re-layouts  5.48 us (8%)
  between operations  1.68 us (2%)
    ppermute x13, starting transfers between devices, send(): return lax.ppermute(x, ('ctx', 'tp'), route)  40.8 us
    pallas_call x11, Pallas kernels, run(): return call(*args)  13.4 us
    ppermute x13, waiting for transfers between devices, send(): return lax.ppermute(x, ('ctx', 'tp'), route)  5.96 us
    unnamed x18, local copies, waits for them, and re-layouts  4.83 us
  transfers between devices with their start and end apart: 13, of which 2 were waited for; matrix products, arithmetic and copies ran while one was open for 1% of the time, Pallas kernels for 16%

profile of v5, /device:TPU:275, one launch (start us, length us, event | category | flops | bytes accessed | tf_op | source)
XLA Modules:
  0.0 67.4 jit_solution(7397759241922561592)
XLA Ops:
  0.0 1.5 %collective-permute-start.3 = (bf16[256,1024]{1,0:T(8,128)(2,1)}, bf16[256,1024]{1,0:T(8,128)(2,1)}, u32[]{:S(2)}, u32[]{:S(2)}) collective-permute-start(bf16[256,1024]{1,0:T(8,128)(2,1)} %x.1), channel_id=1, source_target_pairs={{508,60},{509,37},{510,38},{511,63},{28,28},{29,5},{30,6},{31,31},... | collective-permute-start | bytes 1572872 | tf_op jit(solution)/shard_map/n_aside3/ppermute | solution.py:300
  1.5 1.3 %collective-permute-start.8 = (bf16[256,1024]{1,0:T(8,128)(2,1)}, bf16[256,1024]{1,0:T(8,128)(2,1)S(1)}, u32[]{:S(2)}, u32[]{:S(2)}) collective-permute-start(bf16[256,1024]{1,0:T(8,128)(2,1)} %x.1), channel_id=1, source_target_pairs={{508,52},{509,45},{510,46},{511,55},{28,20},{29,13},{30,14},{31,23... | collective-permute-start | bytes 1572872 | tf_op jit(solution)/shard_map/n_aside1/ppermute | solution.py:300
  2.8 0.7 %collective-permute-start.2 = (bf16[256,1024]{1,0:T(8,128)(2,1)}, bf16[256,1024]{1,0:T(8,128)(2,1)S(1)}, u32[]{:S(2)}, u32[]{:S(2)}) collective-permute-start(bf16[256,1024]{1,0:T(8,128)(2,1)} %x.1), channel_id=1, source_target_pairs={{510,0},{511,1},{508,2},{509,3},{30,32},{31,33},{28,34},{29,35},{6... | collective-permute-start | bytes 1572872 | tf_op jit(solution)/shard_map/n_across2/ppermute | solution.py:300
  3.5 1.9 %collective-permute-start.1 = (bf16[256,1024]{1,0:T(8,128)(2,1)}, bf16[256,1024]{1,0:T(8,128)(2,1)S(1)}, u32[]{:S(2)}, u32[]{:S(2)}) collective-permute-start(bf16[256,1024]{1,0:T(8,128)(2,1)} %x.1), channel_id=1, source_target_pairs={{0,2},{1,3},{2,0},{3,1},{4,6},{5,7},{6,4},{7,5},{8,10},{9,11},{10,... | collective-permute-start | bytes 1572872 | tf_op jit(solution)/shard_map/n_xc/ppermute | solution.py:300
  5.4 3.3 %collective-permute-start = (bf16[256,1024]{1,0:T(8,128)(2,1)}, bf16[256,1024]{1,0:T(8,128)(2,1)S(1)}, u32[]{:S(2)}, u32[]{:S(2)}) collective-permute-start(bf16[256,1024]{1,0:T(8,128)(2,1)} %x.1), channel_id=1, source_target_pairs={{0,1},{1,0},{2,3},{3,2},{4,5},{5,4},{6,7},{7,6},{8,9},{9,8},{10,11... | collective-permute-start | bytes 1572872 | tf_op jit(solution)/shard_map/n_xb/ppermute | solution.py:300
  8.7 0.0 collective-permute-done.3
  8.7 0.7 %collective-permute-start.4 = (bf16[256,1024]{1,0:T(8,128)(2,1)}, bf16[256,1024]{1,0:T(8,128)(2,1)S(1)}, u32[]{:S(2)}, u32[]{:S(2)}) collective-permute-start(bf16[256,1024]{1,0:T(8,128)(2,1)} %collective-permute-done.3), channel_id=1, source_target_pairs={{63,0},{38,1},{37,2},{60,3},{31,32},{6,33},{5,34},{28,35},{127,64}... | collective-permute-start | bytes 1572872 | tf_op jit(solution)/shard_map/n_across3/ppermute | solution.py:300
  9.4 4.0 %collective-permute-done.8 = bf16[256,1024]{1,0:T(8,128)(2,1)S(1)} collective-permute-done((bf16[256,1024]{1,0:T(8,128)(2,1)}, bf16[256,1024]{1,0:T(8,128)(2,1)S(1)}, u32[]{:S(2)}, u32[]{:S(2)}) %collective-permute-start.8) | collective-permute-done | bytes 524320 | tf_op jit(solution)/shard_map/n_aside1/ppermute | solution.py:300
  13.4 4.1 %collective-permute-start.9 = (bf16[256,1024]{1,0:T(8,128)(2,1)S(1)}, bf16[256,1024]{1,0:T(8,128)(2,1)S(1)}, u32[]{:S(2)}, u32[]{:S(2)}) collective-permute-start(bf16[256,1024]{1,0:T(8,128)(2,1)S(1)} %collective-permute-done.8), channel_id=1, source_target_pairs={{45,0},{52,1},{55,2},{46,3},{13,32},{20,33},{23,34},{14,35},{109,6... | collective-permute-start | bytes 1572872 | tf_op jit(solution)/shard_map/n_across1/ppermute | solution.py:300
  17.6 0.0 copy-start.8
  17.6 0.6 copy-done.8
  18.2 0.7 fusion
  20.2 0.1 pad_add_fusion.info
  20.3 0.0 copy-start
  20.3 1.0 %copy-done = bf16[1024,256]{1,0:T(8,128)(2,1)S(1)} copy-done((bf16[1024,256]{1,0:T(8,128)(2,1)S(1)}, bf16[1024,256]{1,0:T(8,128)(2,1)}, u32[]{:S(2)}) %copy-start) | copy-done | bytes 524312
  21.3 0.0 copy-start.2
  21.3 1.0 %copy-done.2 = bf16[1024,256]{1,0:T(8,128)(2,1)S(1)} copy-done((bf16[1024,256]{1,0:T(8,128)(2,1)S(1)}, bf16[1024,256]{1,0:T(8,128)(2,1)}, u32[]{:S(2)}) %copy-start.2) | copy-done | bytes 524312
  22.4 0.0 copy-start.4
  22.4 1.0 %copy-done.4 = bf16[1024,256]{1,0:T(8,128)(2,1)S(1)} copy-done((bf16[1024,256]{1,0:T(8,128)(2,1)S(1)}, bf16[1024,256]{1,0:T(8,128)(2,1)}, u32[]{:S(2)}) %copy-start.4) | copy-done | bytes 524312
  23.4 0.0 copy-start.6
  23.4 1.0 %copy-done.6 = bf16[256,1024]{1,0:T(8,128)(2,1)S(1)} copy-done((bf16[256,1024]{1,0:T(8,128)(2,1)S(1)}, bf16[256,1024]{1,0:T(8,128)(2,1)}, u32[]{:S(2)}) %copy-start.6) | copy-done | bytes 524312
  24.5 1.1 %n_own.1 = (bf16[256,256]{1,0:T(8,128)(2,1)S(1)}, bf16[256,512]{1,0:T(8,128)(2,1)S(1)}) custom-call(s32[3]{0:T(128)S(1)} %pad_add_fusion.info, bf16[256,1024]{1,0:T(8,128)(2,1)S(1)} %copy-done.6, bf16[1024,256]{1,0:T(8,128)(2,1)S(1)} %copy-done, bf16[1024,256]{1,0:T(8,128)(2,1)S(1)} %copy-done.2, bf16[1024,256]{1,0:T(8,128)(2,1)S(1)} %copy-done.4), custom_call_target="tpu_custom_call" | custom-call | tf_op jit(solution)/shard_map/n_own/pallas_call | solution.py:48
  25.6 0.0 collective-permute-done.2.refs_1_.xc
  25.6 0.7 %collective-permute-start.10 = (bf16[256,512]{1,0:T(8,128)(2,1)S(1)}, bf16[256,512]{1,0:T(8,128)(2,1)S(1)}, u32[]{:S(2)}, u32[]{:S(2)}) collective-permute-start(bf16[256,512]{1,0:T(8,128)(2,1)S(1)} %get-tuple-element.46.kva), channel_id=1, source_target_pairs={{508,36},{509,37},{510,38},{511,39},{28,4},{29,5},{30,6},{31,7},{6... | collective-permute-start | bytes 786440 | tf_op jit(solution)/shard_map/n_aside0/ppermute | solution.py:300
  26.3 1.9 %collective-permute-done.1.refs_0_.xc = bf16[256,1024]{1,0:T(8,128)(2,1)S(1)} collective-permute-done((bf16[256,1024]{1,0:T(8,128)(2,1)}, bf16[256,1024]{1,0:T(8,128)(2,1)S(1)}, u32[]{:S(2)}, u32[]{:S(2)}) %collective-permute-start.1) | collective-permute-done | bytes 524320 | tf_op jit(solution)/shard_map/n_xc/ppermute | solution.py:300
  28.2 0.0 copy-start.7
  28.2 0.0 copy-start.1
  28.2 0.0 copy-start.3
  28.2 0.0 copy-start.5
  28.2 5.7 %collective-permute-start.7 = (bf16[256,1024]{1,0:T(8,128)(2,1)S(1)}, bf16[256,1024]{1,0:T(8,128)(2,1)S(1)}, u32[]{:S(2)}, u32[]{:S(2)}) collective-permute-start(bf16[256,1024]{1,0:T(8,128)(2,1)S(1)} %collective-permute-done.1.refs_0_.xc), channel_id=1, source_target_pairs={{2,3},{1,0},{6,7},{5,4},{10,11},{9,8},{14,15},{13,12},{18,19},{17,... | collective-permute-start | bytes 1572872 | tf_op jit(solution)/shard_map/n_outer/ppermute | solution.py:300
  33.9 0.0 collective-permute-done.xb
  33.9 0.0 copy-done.7
  33.9 4.9 %collective-permute-start.6 = (bf16[256,1024]{1,0:T(8,128)(2,1)S(1)}, bf16[256,1024]{1,0:T(8,128)(2,1)S(1)}, u32[]{:S(2)}, u32[]{:S(2)}) collective-permute-start(bf16[256,1024]{1,0:T(8,128)(2,1)S(1)} %copy-done.7), channel_id=1, source_target_pairs={{1,2},{2,1},{5,6},{6,5},{9,10},{10,9},{13,14},{14,13},{17,18},{18,... | collective-permute-start | bytes 1572872 | tf_op jit(solution)/shard_map/n_inner/ppermute | solution.py:300
  38.8 0.0 copy-done.1
  38.8 0.0 copy-done.3
  38.8 0.0 copy-done.5
  38.8 1.0 %n_middle.1 = (bf16[768,256]{1,0:T(8,128)(2,1)S(1)}, bf16[768,512]{1,0:T(8,128)(2,1)S(1)}) custom-call(bf16[256,1024]{1,0:T(8,128)(2,1)S(1)} %collective-permute-done.xb, bf16[256,1024]{1,0:T(8,128)(2,1)S(1)} %collective-permute-done.1.refs_0_.xc, bf16[256,256]{1,0:T(8,128)(2,1)S(1)} %get-tuple-element.45.qa, bf16[256,512]{1,0:T(8,128)(2,1)S(1)} %get-tuple-element.46.kva, ...), custom_call_target="tpu_custom_call" | custom-call | tf_op jit(solution)/shard_map/n_middle/pallas_call | solution.py:48
  39.9 0.0 collective-permute-done.10
  39.9 0.7 %collective-permute-start.11 = (bf16[256,512]{1,0:T(8,128)(2,1)S(1)}, bf16[256,512]{1,0:T(8,128)(2,1)S(1)}, u32[]{:S(2)}, u32[]{:S(2)}) collective-permute-start(bf16[256,512]{1,0:T(8,128)(2,1)S(1)} %collective-permute-done.10), channel_id=1, source_target_pairs={{36,0},{37,1},{38,2},{39,3},{4,32},{5,33},{6,34},{7,35},{100,64},{... | collective-permute-start | bytes 786440 | tf_op jit(solution)/shard_map/n_across0/ppermute | solution.py:300
  40.6 0.0 collective-permute-done.4.xd
  40.6 6.9 %collective-permute-start.5 = (bf16[768,512]{1,0:T(8,128)(2,1)S(1)}, bf16[768,512]{1,0:T(8,128)(2,1)S(1)}, u32[]{:S(2)}, u32[]{:S(2)}) collective-permute-start(bf16[768,512]{1,0:T(8,128)(2,1)S(1)} %get-tuple-element.49.kv), channel_id=1, source_target_pairs={{0,4},{1,5},{2,6},{3,7},{4,8},{5,9},{6,10},{7,11},{8,12},{9,13},{1... | collective-permute-start | bytes 2359304 | tf_op jit(solution)/shard_map/n_near/ppermute | solution.py:300
  47.4 2.5 %n_attend_own.1 = (f32[8,1024]{1,0:T(8,128)S(1)}, f32[256,1024]{1,0:T(8,128)S(1)}) custom-call(s32[3]{0:T(128)S(1)} %pad_add_fusion.info, bf16[768,256]{1,0:T(8,128)(2,1)S(1)} %get-tuple-element.47.q, bf16[768,512]{1,0:T(8,128)(2,1)S(1)} %get-tuple-element.49.kv), custom_call_target="tpu_custom_call" | custom-call | tf_op jit(solution)/shard_map/n_attend_own/pallas_call | solution.py:48
  50.0 0.0 collective-permute-done.9.xb
  50.0 0.6 n_far.1
  50.6 0.0 collective-permute-done.7.refs_0_.outer
  50.6 0.0 collective-permute-done.6.inner
  50.6 1.0 %n_last.1.refs_0_.kvd = bf16[256,512]{1,0:T(8,128)(2,1)S(1)} custom-call(s32[3]{0:T(128)S(1)} %pad_add_fusion.info, f32[8,128]{1,0:T(8,128)S(1)} %n_gate.1.passed, bf16[256,1024]{1,0:T(8,128)(2,1)S(1)} %collective-permute-done.7.refs_0_.outer, bf16[256,1024]{1,0:T(8,128)(2,1)S(1)} %collective-permute-done.6.inner, bf16[1024,256]{1,0:T(8,128)(2,1)S(1)} %copy-done.3, ...), custom_call_target="tpu_custom_call" | custom-call | tf_op jit(solution)/shard_map/n_last/pallas_call | solution.py:48
  51.6 8.6 %collective-permute-start.12 = (bf16[256,512]{1,0:T(8,128)(2,1)S(1)}, bf16[256,512]{1,0:T(8,128)(2,1)S(1)}, u32[]{:S(2)}, u32[]{:S(2)}) collective-permute-start(bf16[256,512]{1,0:T(8,128)(2,1)S(1)} %n_last.1.refs_0_.kvd), channel_id=1, source_target_pairs={{0,4},{1,5},{2,6},{3,7},{4,8},{5,9},{6,10},{7,11},{8,12},{9,13},{1... | collective-permute-start | bytes 786440 | tf_op jit(solution)/shard_map/n_near_last/ppermute | solution.py:300
  60.2 0.0 collective-permute-done.11.refs_1_.far_a
  60.2 0.0 collective-permute-done.5.near
  60.3 4.7 %n_attend_most.1 = (f32[8,1024]{1,0:T(8,128)S(1)}, f32[256,1024]{1,0:T(8,128)S(1)}, bf16[256,256]{1,0:T(8,128)(2,1)S(1)}) custom-call(s32[3]{0:T(128)S(1)} %pad_add_fusion.info, f32[8,128]{1,0:T(8,128)S(1)} %n_gate2.1.passed, bf16[256,1024]{1,0:T(8,128)(2,1)S(1)} %collective-permute-done.7.refs_0_.outer, ...), custom_call_target="tpu_custom_call", output_to_operand_aliasing={{0}: (11, {}), {1}: (12, {})} | custom-call | tf_op jit(solution)/shard_map/n_attend_most/pallas_call | solution.py:48
  65.0 0.0 collective-permute-done.12.near
  65.0 2.4 %n_attend_last.1 = bf16[1024,256]{1,0:T(8,128)(2,1)} custom-call(s32[3]{0:T(128)S(1)} %pad_add_fusion.info, bf16[768,256]{1,0:T(8,128)(2,1)S(1)} %get-tuple-element.47.q, bf16[256,256]{1,0:T(8,128)(2,1)S(1)} %get-tuple-element.73.qd, bf16[256,512]{1,0:T(8,128)(2,1)S(1)} %collective-permute-done.12.near, bf16[256,512]{1,0:T(8,128)(2,1)S(1)} %get-tuple-element.74.far, ...), custom_call_target="tpu_custom_call" | custom-call | tf_op jit(solution)/shard_map/n_attend_last/pallas_call | solution.py:48
  (4 shorter events, 0.0 us)
Async XLA Ops:
  0.0 8.7 %collective-permute-start.3 = (bf16[256,1024]{1,0:T(8,128)(2,1)}, bf16[256,1024]{1,0:T(8,128)(2,1)}, u32[]{:S(2)}, u32[]{:S(2)}) collective-permute-start(bf16[256,1024]{1,0:T(8,128)(2,1)} %x.1), channel_id=1, source_target_pairs={{508,60},{509,37},{510,38},{511,63},{28,28},{29,5},{30,6},{31,31},... | collective-permute-start | bytes 1572872 | tf_op jit(solution)/shard_map/n_aside3/ppermute | solution.py:300
  1.5 11.9 %collective-permute-start.8 = (bf16[256,1024]{1,0:T(8,128)(2,1)}, bf16[256,1024]{1,0:T(8,128)(2,1)S(1)}, u32[]{:S(2)}, u32[]{:S(2)}) collective-permute-start(bf16[256,1024]{1,0:T(8,128)(2,1)} %x.1), channel_id=1, source_target_pairs={{508,52},{509,45},{510,46},{511,55},{28,20},{29,13},{30,14},{31,23... | collective-permute-start | bytes 1572872 | tf_op jit(solution)/shard_map/n_aside1/ppermute | solution.py:300
  2.8 22.8 %collective-permute-start.2 = (bf16[256,1024]{1,0:T(8,128)(2,1)}, bf16[256,1024]{1,0:T(8,128)(2,1)S(1)}, u32[]{:S(2)}, u32[]{:S(2)}) collective-permute-start(bf16[256,1024]{1,0:T(8,128)(2,1)} %x.1), channel_id=1, source_target_pairs={{510,0},{511,1},{508,2},{509,3},{30,32},{31,33},{28,34},{29,35},{6... | collective-permute-start | bytes 1572872 | tf_op jit(solution)/shard_map/n_across2/ppermute | solution.py:300
  3.5 24.7 %collective-permute-start.1 = (bf16[256,1024]{1,0:T(8,128)(2,1)}, bf16[256,1024]{1,0:T(8,128)(2,1)S(1)}, u32[]{:S(2)}, u32[]{:S(2)}) collective-permute-start(bf16[256,1024]{1,0:T(8,128)(2,1)} %x.1), channel_id=1, source_target_pairs={{0,2},{1,3},{2,0},{3,1},{4,6},{5,7},{6,4},{7,5},{8,10},{9,11},{10,... | collective-permute-start | bytes 1572872 | tf_op jit(solution)/shard_map/n_xc/ppermute | solution.py:300
  5.4 28.5 %collective-permute-start = (bf16[256,1024]{1,0:T(8,128)(2,1)}, bf16[256,1024]{1,0:T(8,128)(2,1)S(1)}, u32[]{:S(2)}, u32[]{:S(2)}) collective-permute-start(bf16[256,1024]{1,0:T(8,128)(2,1)} %x.1), channel_id=1, source_target_pairs={{0,1},{1,0},{2,3},{3,2},{4,5},{5,4},{6,7},{7,6},{8,9},{9,8},{10,11... | collective-permute-start | bytes 1572872 | tf_op jit(solution)/shard_map/n_xb/ppermute | solution.py:300
  8.7 31.9 %collective-permute-start.4 = (bf16[256,1024]{1,0:T(8,128)(2,1)}, bf16[256,1024]{1,0:T(8,128)(2,1)S(1)}, u32[]{:S(2)}, u32[]{:S(2)}) collective-permute-start(bf16[256,1024]{1,0:T(8,128)(2,1)} %collective-permute-done.3), channel_id=1, source_target_pairs={{63,0},{38,1},{37,2},{60,3},{31,32},{6,33},{5,34},{28,35},{127,64}... | collective-permute-start | bytes 1572872 | tf_op jit(solution)/shard_map/n_across3/ppermute | solution.py:300
  13.4 36.6 %collective-permute-start.9 = (bf16[256,1024]{1,0:T(8,128)(2,1)S(1)}, bf16[256,1024]{1,0:T(8,128)(2,1)S(1)}, u32[]{:S(2)}, u32[]{:S(2)}) collective-permute-start(bf16[256,1024]{1,0:T(8,128)(2,1)S(1)} %collective-permute-done.8), channel_id=1, source_target_pairs={{45,0},{52,1},{55,2},{46,3},{13,32},{20,33},{23,34},{14,35},{109,6... | collective-permute-start | bytes 1572872 | tf_op jit(solution)/shard_map/n_across1/ppermute | solution.py:300
  17.6 0.7 copy-start.8
  20.3 1.0 %copy-start = (bf16[1024,256]{1,0:T(8,128)(2,1)S(1)}, bf16[1024,256]{1,0:T(8,128)(2,1)}, u32[]{:S(2)}) copy-start(bf16[1024,256]{1,0:T(8,128)(2,1)} %wq.5) | copy-start | bytes 1572868
  21.3 1.0 %copy-start.2 = (bf16[1024,256]{1,0:T(8,128)(2,1)S(1)}, bf16[1024,256]{1,0:T(8,128)(2,1)}, u32[]{:S(2)}) copy-start(bf16[1024,256]{1,0:T(8,128)(2,1)} %wk.7) | copy-start | bytes 1572868
  22.4 1.0 %copy-start.4 = (bf16[1024,256]{1,0:T(8,128)(2,1)S(1)}, bf16[1024,256]{1,0:T(8,128)(2,1)}, u32[]{:S(2)}) copy-start(bf16[1024,256]{1,0:T(8,128)(2,1)} %wv.7) | copy-start | bytes 1572868
  23.4 1.0 %copy-start.6 = (bf16[256,1024]{1,0:T(8,128)(2,1)S(1)}, bf16[256,1024]{1,0:T(8,128)(2,1)}, u32[]{:S(2)}) copy-start(bf16[256,1024]{1,0:T(8,128)(2,1)} %x.1) | copy-start | bytes 1572868
  25.6 14.3 %collective-permute-start.10 = (bf16[256,512]{1,0:T(8,128)(2,1)S(1)}, bf16[256,512]{1,0:T(8,128)(2,1)S(1)}, u32[]{:S(2)}, u32[]{:S(2)}) collective-permute-start(bf16[256,512]{1,0:T(8,128)(2,1)S(1)} %get-tuple-element.46.kva), channel_id=1, source_target_pairs={{508,36},{509,37},{510,38},{511,39},{28,4},{29,5},{30,6},{31,7},{6... | collective-permute-start | bytes 786440 | tf_op jit(solution)/shard_map/n_aside0/ppermute | solution.py:300
  28.2 5.7 %copy-start.7 = (bf16[256,1024]{1,0:T(8,128)(2,1)S(1)}, bf16[256,1024]{1,0:T(8,128)(2,1)}, u32[]{:S(2)}) copy-start(bf16[256,1024]{1,0:T(8,128)(2,1)} %x.1) | copy-start | bytes 1572868
  28.2 10.6 %copy-start.1 = (bf16[1024,256]{1,0:T(8,128)(2,1)S(1)}, bf16[1024,256]{1,0:T(8,128)(2,1)}, u32[]{:S(2)}) copy-start(bf16[1024,256]{1,0:T(8,128)(2,1)} %wq.5) | copy-start | bytes 1572868
  28.2 10.6 %copy-start.3 = (bf16[1024,256]{1,0:T(8,128)(2,1)S(1)}, bf16[1024,256]{1,0:T(8,128)(2,1)}, u32[]{:S(2)}) copy-start(bf16[1024,256]{1,0:T(8,128)(2,1)} %wk.7) | copy-start | bytes 1572868
  28.2 10.6 %copy-start.5 = (bf16[1024,256]{1,0:T(8,128)(2,1)S(1)}, bf16[1024,256]{1,0:T(8,128)(2,1)}, u32[]{:S(2)}) copy-start(bf16[1024,256]{1,0:T(8,128)(2,1)} %wv.7) | copy-start | bytes 1572868
  28.2 22.4 %collective-permute-start.7 = (bf16[256,1024]{1,0:T(8,128)(2,1)S(1)}, bf16[256,1024]{1,0:T(8,128)(2,1)S(1)}, u32[]{:S(2)}, u32[]{:S(2)}) collective-permute-start(bf16[256,1024]{1,0:T(8,128)(2,1)S(1)} %collective-permute-done.1.refs_0_.xc), channel_id=1, source_target_pairs={{2,3},{1,0},{6,7},{5,4},{10,11},{9,8},{14,15},{13,12},{18,19},{17,... | collective-permute-start | bytes 1572872 | tf_op jit(solution)/shard_map/n_outer/ppermute | solution.py:300
  33.9 16.7 %collective-permute-start.6 = (bf16[256,1024]{1,0:T(8,128)(2,1)S(1)}, bf16[256,1024]{1,0:T(8,128)(2,1)S(1)}, u32[]{:S(2)}, u32[]{:S(2)}) collective-permute-start(bf16[256,1024]{1,0:T(8,128)(2,1)S(1)} %copy-done.7), channel_id=1, source_target_pairs={{1,2},{2,1},{5,6},{6,5},{9,10},{10,9},{13,14},{14,13},{17,18},{18,... | collective-permute-start | bytes 1572872 | tf_op jit(solution)/shard_map/n_inner/ppermute | solution.py:300
  39.9 20.4 %collective-permute-start.11 = (bf16[256,512]{1,0:T(8,128)(2,1)S(1)}, bf16[256,512]{1,0:T(8,128)(2,1)S(1)}, u32[]{:S(2)}, u32[]{:S(2)}) collective-permute-start(bf16[256,512]{1,0:T(8,128)(2,1)S(1)} %collective-permute-done.10), channel_id=1, source_target_pairs={{36,0},{37,1},{38,2},{39,3},{4,32},{5,33},{6,34},{7,35},{100,64},{... | collective-permute-start | bytes 786440 | tf_op jit(solution)/shard_map/n_across0/ppermute | solution.py:300
  40.6 19.7 %collective-permute-start.5 = (bf16[768,512]{1,0:T(8,128)(2,1)S(1)}, bf16[768,512]{1,0:T(8,128)(2,1)S(1)}, u32[]{:S(2)}, u32[]{:S(2)}) collective-permute-start(bf16[768,512]{1,0:T(8,128)(2,1)S(1)} %get-tuple-element.49.kv), channel_id=1, source_target_pairs={{0,4},{1,5},{2,6},{3,7},{4,8},{5,9},{6,10},{7,11},{8,12},{9,13},{1... | collective-permute-start | bytes 2359304 | tf_op jit(solution)/shard_map/n_near/ppermute | solution.py:300
  51.6 13.4 %collective-permute-start.12 = (bf16[256,512]{1,0:T(8,128)(2,1)S(1)}, bf16[256,512]{1,0:T(8,128)(2,1)S(1)}, u32[]{:S(2)}, u32[]{:S(2)}) collective-permute-start(bf16[256,512]{1,0:T(8,128)(2,1)S(1)} %n_last.1.refs_0_.kvd), channel_id=1, source_target_pairs={{0,4},{1,5},{2,6},{3,7},{4,8},{5,9},{6,10},{7,11},{8,12},{9,13},{1... | collective-permute-start | bytes 786440 | tf_op jit(solution)/shard_map/n_near_last/ppermute | solution.py:300

commit v6 on v5

--- a/solution.py
+++ b/solution.py
@@ -194,14 +194,14 @@
     diagonal = positions(tp, (3,), 0) <= positions(tp, (3,), 1)
 
     def work(visible):
+        units, states, places = [], [], []
         for h in range(HEADS):
             k, v = head(h), head(HEADS + h)
             s, l = slice(h, h + 1), slice(HEADS + h, HEADS + h + 1)
-            units, states, columns = [], [], []
             before = (held[:, k], held[:, v])
             for chunk in range(4):
                 rows = slice(chunk * CHUNK, (chunk + 1) * CHUNK)
-                columns.append(rows)
+                places.append((s, l, k, rows))
                 if chunk < 3:
                     parts = [(kvd[:, k], kvd[:, v], last < (tp ^ chunk))]
                     states.append((state0[s, rows], state0[l, rows], mix0[k, rows]))
@@ -214,10 +214,10 @@
                 if visible:
                     parts.append((*before, None))
                 units.append((q[rows, k] if chunk < 3 else qd[:, k], parts))
-            for rows, (top, total, part) in zip(columns, pieces(units, states), strict=True):
-                state[s, rows] = top
-                state[l, rows] = total
-                mix[k, rows] = part
+        for (s, l, k, rows), (top, total, part) in zip(places, pieces(units, states), strict=True):
+            state[s, rows] = top
+            state[l, rows] = total
+            mix[k, rows] = part
 
     @pl.when(info[1] == 1)
     def _():

time: 68.2 us -> 68 us (level)
  the two profiles are of different devices: /device:TPU:275 before, /device:TPU:403 now
where the time goes in v6:
time: 68 us; the launch traced here: 67.2 us
  starting transfers between devices  40.8 us (60%)
  Pallas kernels  13.2 us (19%)
  waiting for transfers between devices  5.96 us (9%)
  local copies, waits for them, and re-layouts  5.48 us (8%)
  between operations  1.68 us (2%)
    ppermute x13, starting transfers between devices, send(): return lax.ppermute(x, ('ctx', 'tp'), route)  40.8 us
    pallas_call x11, Pallas kernels, run(): return call(*args)  13.2 us
    ppermute x13, waiting for transfers between devices, send(): return lax.ppermute(x, ('ctx', 'tp'), route)  5.96 us
    unnamed x18, local copies, waits for them, and re-layouts  4.83 us
  transfers between devices with their start and end apart: 13, of which 2 were waited for; matrix products, arithmetic and copies ran while one was open for 1% of the time, Pallas kernels for 16%

profile of v6, /device:TPU:403, one launch (start us, length us, event | category | flops | bytes accessed | tf_op | source)
XLA Modules:
  0.0 67.2 jit_solution(8973961643892225796)
XLA Ops:
  0.0 1.5 %collective-permute-start.3 = (bf16[256,1024]{1,0:T(8,128)(2,1)}, bf16[256,1024]{1,0:T(8,128)(2,1)}, u32[]{:S(2)}, u32[]{:S(2)}) collective-permute-start(bf16[256,1024]{1,0:T(8,128)(2,1)} %x.1), channel_id=1, source_target_pairs={{508,60},{509,37},{510,38},{511,63},{28,28},{29,5},{30,6},{31,31},... | collective-permute-start | bytes 1572872 | tf_op jit(solution)/shard_map/n_aside3/ppermute | solution.py:300
  1.5 1.3 %collective-permute-start.8 = (bf16[256,1024]{1,0:T(8,128)(2,1)}, bf16[256,1024]{1,0:T(8,128)(2,1)S(1)}, u32[]{:S(2)}, u32[]{:S(2)}) collective-permute-start(bf16[256,1024]{1,0:T(8,128)(2,1)} %x.1), channel_id=1, source_target_pairs={{508,52},{509,45},{510,46},{511,55},{28,20},{29,13},{30,14},{31,23... | collective-permute-start | bytes 1572872 | tf_op jit(solution)/shard_map/n_aside1/ppermute | solution.py:300
  2.8 0.7 %collective-permute-start.2 = (bf16[256,1024]{1,0:T(8,128)(2,1)}, bf16[256,1024]{1,0:T(8,128)(2,1)S(1)}, u32[]{:S(2)}, u32[]{:S(2)}) collective-permute-start(bf16[256,1024]{1,0:T(8,128)(2,1)} %x.1), channel_id=1, source_target_pairs={{510,0},{511,1},{508,2},{509,3},{30,32},{31,33},{28,34},{29,35},{6... | collective-permute-start | bytes 1572872 | tf_op jit(solution)/shard_map/n_across2/ppermute | solution.py:300
  3.5 1.9 %collective-permute-start.1 = (bf16[256,1024]{1,0:T(8,128)(2,1)}, bf16[256,1024]{1,0:T(8,128)(2,1)S(1)}, u32[]{:S(2)}, u32[]{:S(2)}) collective-permute-start(bf16[256,1024]{1,0:T(8,128)(2,1)} %x.1), channel_id=1, source_target_pairs={{0,2},{1,3},{2,0},{3,1},{4,6},{5,7},{6,4},{7,5},{8,10},{9,11},{10,... | collective-permute-start | bytes 1572872 | tf_op jit(solution)/shard_map/n_xc/ppermute | solution.py:300
  5.4 3.3 %collective-permute-start = (bf16[256,1024]{1,0:T(8,128)(2,1)}, bf16[256,1024]{1,0:T(8,128)(2,1)S(1)}, u32[]{:S(2)}, u32[]{:S(2)}) collective-permute-start(bf16[256,1024]{1,0:T(8,128)(2,1)} %x.1), channel_id=1, source_target_pairs={{0,1},{1,0},{2,3},{3,2},{4,5},{5,4},{6,7},{7,6},{8,9},{9,8},{10,11... | collective-permute-start | bytes 1572872 | tf_op jit(solution)/shard_map/n_xb/ppermute | solution.py:300
  8.7 0.0 collective-permute-done.3
  8.7 0.7 %collective-permute-start.4 = (bf16[256,1024]{1,0:T(8,128)(2,1)}, bf16[256,1024]{1,0:T(8,128)(2,1)S(1)}, u32[]{:S(2)}, u32[]{:S(2)}) collective-permute-start(bf16[256,1024]{1,0:T(8,128)(2,1)} %collective-permute-done.3), channel_id=1, source_target_pairs={{63,0},{38,1},{37,2},{60,3},{31,32},{6,33},{5,34},{28,35},{127,64}... | collective-permute-start | bytes 1572872 | tf_op jit(solution)/shard_map/n_across3/ppermute | solution.py:300
  9.4 4.0 %collective-permute-done.8 = bf16[256,1024]{1,0:T(8,128)(2,1)S(1)} collective-permute-done((bf16[256,1024]{1,0:T(8,128)(2,1)}, bf16[256,1024]{1,0:T(8,128)(2,1)S(1)}, u32[]{:S(2)}, u32[]{:S(2)}) %collective-permute-start.8) | collective-permute-done | bytes 524320 | tf_op jit(solution)/shard_map/n_aside1/ppermute | solution.py:300
  13.4 4.1 %collective-permute-start.9 = (bf16[256,1024]{1,0:T(8,128)(2,1)S(1)}, bf16[256,1024]{1,0:T(8,128)(2,1)S(1)}, u32[]{:S(2)}, u32[]{:S(2)}) collective-permute-start(bf16[256,1024]{1,0:T(8,128)(2,1)S(1)} %collective-permute-done.8), channel_id=1, source_target_pairs={{45,0},{52,1},{55,2},{46,3},{13,32},{20,33},{23,34},{14,35},{109,6... | collective-permute-start | bytes 1572872 | tf_op jit(solution)/shard_map/n_across1/ppermute | solution.py:300
  17.6 0.0 copy-start.8
  17.6 0.6 copy-done.8
  18.2 0.7 fusion
  20.2 0.1 pad_add_fusion.info
  20.3 0.0 copy-start
  20.3 1.0 %copy-done = bf16[1024,256]{1,0:T(8,128)(2,1)S(1)} copy-done((bf16[1024,256]{1,0:T(8,128)(2,1)S(1)}, bf16[1024,256]{1,0:T(8,128)(2,1)}, u32[]{:S(2)}) %copy-start) | copy-done | bytes 524312
  21.3 0.0 copy-start.2
  21.3 1.0 %copy-done.2 = bf16[1024,256]{1,0:T(8,128)(2,1)S(1)} copy-done((bf16[1024,256]{1,0:T(8,128)(2,1)S(1)}, bf16[1024,256]{1,0:T(8,128)(2,1)}, u32[]{:S(2)}) %copy-start.2) | copy-done | bytes 524312
  22.4 0.0 copy-start.4
  22.4 1.0 %copy-done.4 = bf16[1024,256]{1,0:T(8,128)(2,1)S(1)} copy-done((bf16[1024,256]{1,0:T(8,128)(2,1)S(1)}, bf16[1024,256]{1,0:T(8,128)(2,1)}, u32[]{:S(2)}) %copy-start.4) | copy-done | bytes 524312
  23.4 0.0 copy-start.6
  23.4 1.0 %copy-done.6 = bf16[256,1024]{1,0:T(8,128)(2,1)S(1)} copy-done((bf16[256,1024]{1,0:T(8,128)(2,1)S(1)}, bf16[256,1024]{1,0:T(8,128)(2,1)}, u32[]{:S(2)}) %copy-start.6) | copy-done | bytes 524312
  24.5 1.1 %n_own.1 = (bf16[256,256]{1,0:T(8,128)(2,1)S(1)}, bf16[256,512]{1,0:T(8,128)(2,1)S(1)}) custom-call(s32[3]{0:T(128)S(1)} %pad_add_fusion.info, bf16[256,1024]{1,0:T(8,128)(2,1)S(1)} %copy-done.6, bf16[1024,256]{1,0:T(8,128)(2,1)S(1)} %copy-done, bf16[1024,256]{1,0:T(8,128)(2,1)S(1)} %copy-done.2, bf16[1024,256]{1,0:T(8,128)(2,1)S(1)} %copy-done.4), custom_call_target="tpu_custom_call" | custom-call | tf_op jit(solution)/shard_map/n_own/pallas_call | solution.py:48
  25.6 0.0 collective-permute-done.2.refs_1_.xc
  25.6 0.7 %collective-permute-start.10 = (bf16[256,512]{1,0:T(8,128)(2,1)S(1)}, bf16[256,512]{1,0:T(8,128)(2,1)S(1)}, u32[]{:S(2)}, u32[]{:S(2)}) collective-permute-start(bf16[256,512]{1,0:T(8,128)(2,1)S(1)} %get-tuple-element.46.kva), channel_id=1, source_target_pairs={{508,36},{509,37},{510,38},{511,39},{28,4},{29,5},{30,6},{31,7},{6... | collective-permute-start | bytes 786440 | tf_op jit(solution)/shard_map/n_aside0/ppermute | solution.py:300
  26.3 1.9 %collective-permute-done.1.refs_0_.xc = bf16[256,1024]{1,0:T(8,128)(2,1)S(1)} collective-permute-done((bf16[256,1024]{1,0:T(8,128)(2,1)}, bf16[256,1024]{1,0:T(8,128)(2,1)S(1)}, u32[]{:S(2)}, u32[]{:S(2)}) %collective-permute-start.1) | collective-permute-done | bytes 524320 | tf_op jit(solution)/shard_map/n_xc/ppermute | solution.py:300
  28.2 0.0 copy-start.7
  28.2 0.0 copy-start.1
  28.2 0.0 copy-start.3
  28.2 0.0 copy-start.5
  28.2 5.7 %collective-permute-start.7 = (bf16[256,1024]{1,0:T(8,128)(2,1)S(1)}, bf16[256,1024]{1,0:T(8,128)(2,1)S(1)}, u32[]{:S(2)}, u32[]{:S(2)}) collective-permute-start(bf16[256,1024]{1,0:T(8,128)(2,1)S(1)} %collective-permute-done.1.refs_0_.xc), channel_id=1, source_target_pairs={{2,3},{1,0},{6,7},{5,4},{10,11},{9,8},{14,15},{13,12},{18,19},{17,... | collective-permute-start | bytes 1572872 | tf_op jit(solution)/shard_map/n_outer/ppermute | solution.py:300
  33.9 0.0 collective-permute-done.xb
  33.9 0.0 copy-done.7
  33.9 4.9 %collective-permute-start.6 = (bf16[256,1024]{1,0:T(8,128)(2,1)S(1)}, bf16[256,1024]{1,0:T(8,128)(2,1)S(1)}, u32[]{:S(2)}, u32[]{:S(2)}) collective-permute-start(bf16[256,1024]{1,0:T(8,128)(2,1)S(1)} %copy-done.7), channel_id=1, source_target_pairs={{1,2},{2,1},{5,6},{6,5},{9,10},{10,9},{13,14},{14,13},{17,18},{18,... | collective-permute-start | bytes 1572872 | tf_op jit(solution)/shard_map/n_inner/ppermute | solution.py:300
  38.8 0.0 copy-done.1
  38.8 0.0 copy-done.3
  38.8 0.0 copy-done.5
  38.8 1.0 %n_middle.1 = (bf16[768,256]{1,0:T(8,128)(2,1)S(1)}, bf16[768,512]{1,0:T(8,128)(2,1)S(1)}) custom-call(bf16[256,1024]{1,0:T(8,128)(2,1)S(1)} %collective-permute-done.xb, bf16[256,1024]{1,0:T(8,128)(2,1)S(1)} %collective-permute-done.1.refs_0_.xc, bf16[256,256]{1,0:T(8,128)(2,1)S(1)} %get-tuple-element.45.qa, bf16[256,512]{1,0:T(8,128)(2,1)S(1)} %get-tuple-element.46.kva, ...), custom_call_target="tpu_custom_call" | custom-call | tf_op jit(solution)/shard_map/n_middle/pallas_call | solution.py:48
  39.9 0.0 collective-permute-done.10
  39.9 0.7 %collective-permute-start.11 = (bf16[256,512]{1,0:T(8,128)(2,1)S(1)}, bf16[256,512]{1,0:T(8,128)(2,1)S(1)}, u32[]{:S(2)}, u32[]{:S(2)}) collective-permute-start(bf16[256,512]{1,0:T(8,128)(2,1)S(1)} %collective-permute-done.10), channel_id=1, source_target_pairs={{36,0},{37,1},{38,2},{39,3},{4,32},{5,33},{6,34},{7,35},{100,64},{... | collective-permute-start | bytes 786440 | tf_op jit(solution)/shard_map/n_across0/ppermute | solution.py:300
  40.6 0.0 collective-permute-done.4.xd
  40.6 6.9 %collective-permute-start.5 = (bf16[768,512]{1,0:T(8,128)(2,1)S(1)}, bf16[768,512]{1,0:T(8,128)(2,1)S(1)}, u32[]{:S(2)}, u32[]{:S(2)}) collective-permute-start(bf16[768,512]{1,0:T(8,128)(2,1)S(1)} %get-tuple-element.49.kv), channel_id=1, source_target_pairs={{0,4},{1,5},{2,6},{3,7},{4,8},{5,9},{6,10},{7,11},{8,12},{9,13},{1... | collective-permute-start | bytes 2359304 | tf_op jit(solution)/shard_map/n_near/ppermute | solution.py:300
  47.4 2.5 %n_attend_own.1 = (f32[8,1024]{1,0:T(8,128)S(1)}, f32[256,1024]{1,0:T(8,128)S(1)}) custom-call(s32[3]{0:T(128)S(1)} %pad_add_fusion.info, bf16[768,256]{1,0:T(8,128)(2,1)S(1)} %get-tuple-element.47.q, bf16[768,512]{1,0:T(8,128)(2,1)S(1)} %get-tuple-element.49.kv), custom_call_target="tpu_custom_call" | custom-call | tf_op jit(solution)/shard_map/n_attend_own/pallas_call | solution.py:48
  50.0 0.0 collective-permute-done.9.xb
  50.0 0.6 n_far.1
  50.6 0.0 collective-permute-done.7.refs_0_.outer
  50.6 0.0 collective-permute-done.6.inner
  50.6 1.0 %n_last.1.refs_0_.kvd = bf16[256,512]{1,0:T(8,128)(2,1)S(1)} custom-call(s32[3]{0:T(128)S(1)} %pad_add_fusion.info, f32[8,128]{1,0:T(8,128)S(1)} %n_gate.1.passed, bf16[256,1024]{1,0:T(8,128)(2,1)S(1)} %collective-permute-done.7.refs_0_.outer, bf16[256,1024]{1,0:T(8,128)(2,1)S(1)} %collective-permute-done.6.inner, bf16[1024,256]{1,0:T(8,128)(2,1)S(1)} %copy-done.3, ...), custom_call_target="tpu_custom_call" | custom-call | tf_op jit(solution)/shard_map/n_last/pallas_call | solution.py:48
  51.6 8.6 %collective-permute-start.12 = (bf16[256,512]{1,0:T(8,128)(2,1)S(1)}, bf16[256,512]{1,0:T(8,128)(2,1)S(1)}, u32[]{:S(2)}, u32[]{:S(2)}) collective-permute-start(bf16[256,512]{1,0:T(8,128)(2,1)S(1)} %n_last.1.refs_0_.kvd), channel_id=1, source_target_pairs={{0,4},{1,5},{2,6},{3,7},{4,8},{5,9},{6,10},{7,11},{8,12},{9,13},{1... | collective-permute-start | bytes 786440 | tf_op jit(solution)/shard_map/n_near_last/ppermute | solution.py:300
  60.2 0.0 collective-permute-done.11.refs_1_.far_a
  60.2 0.0 collective-permute-done.5.near
  60.2 4.6 %n_attend_most.1 = (f32[8,1024]{1,0:T(8,128)S(1)}, f32[256,1024]{1,0:T(8,128)S(1)}, bf16[256,256]{1,0:T(8,128)(2,1)S(1)}) custom-call(s32[3]{0:T(128)S(1)} %pad_add_fusion.info, f32[8,128]{1,0:T(8,128)S(1)} %n_gate2.1.passed, bf16[256,1024]{1,0:T(8,128)(2,1)S(1)} %collective-permute-done.7.refs_0_.outer, ...), custom_call_target="tpu_custom_call", output_to_operand_aliasing={{0}: (11, {}), {1}: (12, {})} | custom-call | tf_op jit(solution)/shard_map/n_attend_most/pallas_call | solution.py:48
  64.8 0.0 collective-permute-done.12.near
  64.8 2.4 %n_attend_last.1 = bf16[1024,256]{1,0:T(8,128)(2,1)} custom-call(s32[3]{0:T(128)S(1)} %pad_add_fusion.info, bf16[768,256]{1,0:T(8,128)(2,1)S(1)} %get-tuple-element.47.q, bf16[256,256]{1,0:T(8,128)(2,1)S(1)} %get-tuple-element.73.qd, bf16[256,512]{1,0:T(8,128)(2,1)S(1)} %collective-permute-done.12.near, bf16[256,512]{1,0:T(8,128)(2,1)S(1)} %get-tuple-element.74.far, ...), custom_call_target="tpu_custom_call" | custom-call | tf_op jit(solution)/shard_map/n_attend_last/pallas_call | solution.py:48
  (4 shorter events, 0.0 us)
Async XLA Ops:
  0.0 8.7 %collective-permute-start.3 = (bf16[256,1024]{1,0:T(8,128)(2,1)}, bf16[256,1024]{1,0:T(8,128)(2,1)}, u32[]{:S(2)}, u32[]{:S(2)}) collective-permute-start(bf16[256,1024]{1,0:T(8,128)(2,1)} %x.1), channel_id=1, source_target_pairs={{508,60},{509,37},{510,38},{511,63},{28,28},{29,5},{30,6},{31,31},... | collective-permute-start | bytes 1572872 | tf_op jit(solution)/shard_map/n_aside3/ppermute | solution.py:300
  1.5 11.9 %collective-permute-start.8 = (bf16[256,1024]{1,0:T(8,128)(2,1)}, bf16[256,1024]{1,0:T(8,128)(2,1)S(1)}, u32[]{:S(2)}, u32[]{:S(2)}) collective-permute-start(bf16[256,1024]{1,0:T(8,128)(2,1)} %x.1), channel_id=1, source_target_pairs={{508,52},{509,45},{510,46},{511,55},{28,20},{29,13},{30,14},{31,23... | collective-permute-start | bytes 1572872 | tf_op jit(solution)/shard_map/n_aside1/ppermute | solution.py:300
  2.8 22.8 %collective-permute-start.2 = (bf16[256,1024]{1,0:T(8,128)(2,1)}, bf16[256,1024]{1,0:T(8,128)(2,1)S(1)}, u32[]{:S(2)}, u32[]{:S(2)}) collective-permute-start(bf16[256,1024]{1,0:T(8,128)(2,1)} %x.1), channel_id=1, source_target_pairs={{510,0},{511,1},{508,2},{509,3},{30,32},{31,33},{28,34},{29,35},{6... | collective-permute-start | bytes 1572872 | tf_op jit(solution)/shard_map/n_across2/ppermute | solution.py:300
  3.5 24.7 %collective-permute-start.1 = (bf16[256,1024]{1,0:T(8,128)(2,1)}, bf16[256,1024]{1,0:T(8,128)(2,1)S(1)}, u32[]{:S(2)}, u32[]{:S(2)}) collective-permute-start(bf16[256,1024]{1,0:T(8,128)(2,1)} %x.1), channel_id=1, source_target_pairs={{0,2},{1,3},{2,0},{3,1},{4,6},{5,7},{6,4},{7,5},{8,10},{9,11},{10,... | collective-permute-start | bytes 1572872 | tf_op jit(solution)/shard_map/n_xc/ppermute | solution.py:300
  5.4 28.5 %collective-permute-start = (bf16[256,1024]{1,0:T(8,128)(2,1)}, bf16[256,1024]{1,0:T(8,128)(2,1)S(1)}, u32[]{:S(2)}, u32[]{:S(2)}) collective-permute-start(bf16[256,1024]{1,0:T(8,128)(2,1)} %x.1), channel_id=1, source_target_pairs={{0,1},{1,0},{2,3},{3,2},{4,5},{5,4},{6,7},{7,6},{8,9},{9,8},{10,11... | collective-permute-start | bytes 1572872 | tf_op jit(solution)/shard_map/n_xb/ppermute | solution.py:300
  8.7 31.9 %collective-permute-start.4 = (bf16[256,1024]{1,0:T(8,128)(2,1)}, bf16[256,1024]{1,0:T(8,128)(2,1)S(1)}, u32[]{:S(2)}, u32[]{:S(2)}) collective-permute-start(bf16[256,1024]{1,0:T(8,128)(2,1)} %collective-permute-done.3), channel_id=1, source_target_pairs={{63,0},{38,1},{37,2},{60,3},{31,32},{6,33},{5,34},{28,35},{127,64}... | collective-permute-start | bytes 1572872 | tf_op jit(solution)/shard_map/n_across3/ppermute | solution.py:300
  13.4 36.6 %collective-permute-start.9 = (bf16[256,1024]{1,0:T(8,128)(2,1)S(1)}, bf16[256,1024]{1,0:T(8,128)(2,1)S(1)}, u32[]{:S(2)}, u32[]{:S(2)}) collective-permute-start(bf16[256,1024]{1,0:T(8,128)(2,1)S(1)} %collective-permute-done.8), channel_id=1, source_target_pairs={{45,0},{52,1},{55,2},{46,3},{13,32},{20,33},{23,34},{14,35},{109,6... | collective-permute-start | bytes 1572872 | tf_op jit(solution)/shard_map/n_across1/ppermute | solution.py:300
  17.6 0.7 copy-start.8
  20.3 1.0 %copy-start = (bf16[1024,256]{1,0:T(8,128)(2,1)S(1)}, bf16[1024,256]{1,0:T(8,128)(2,1)}, u32[]{:S(2)}) copy-start(bf16[1024,256]{1,0:T(8,128)(2,1)} %wq.5) | copy-start | bytes 1572868
  21.3 1.0 %copy-start.2 = (bf16[1024,256]{1,0:T(8,128)(2,1)S(1)}, bf16[1024,256]{1,0:T(8,128)(2,1)}, u32[]{:S(2)}) copy-start(bf16[1024,256]{1,0:T(8,128)(2,1)} %wk.7) | copy-start | bytes 1572868
  22.4 1.0 %copy-start.4 = (bf16[1024,256]{1,0:T(8,128)(2,1)S(1)}, bf16[1024,256]{1,0:T(8,128)(2,1)}, u32[]{:S(2)}) copy-start(bf16[1024,256]{1,0:T(8,128)(2,1)} %wv.7) | copy-start | bytes 1572868
  23.4 1.0 %copy-start.6 = (bf16[256,1024]{1,0:T(8,128)(2,1)S(1)}, bf16[256,1024]{1,0:T(8,128)(2,1)}, u32[]{:S(2)}) copy-start(bf16[256,1024]{1,0:T(8,128)(2,1)} %x.1) | copy-start | bytes 1572868
  25.6 14.3 %collective-permute-start.10 = (bf16[256,512]{1,0:T(8,128)(2,1)S(1)}, bf16[256,512]{1,0:T(8,128)(2,1)S(1)}, u32[]{:S(2)}, u32[]{:S(2)}) collective-permute-start(bf16[256,512]{1,0:T(8,128)(2,1)S(1)} %get-tuple-element.46.kva), channel_id=1, source_target_pairs={{508,36},{509,37},{510,38},{511,39},{28,4},{29,5},{30,6},{31,7},{6... | collective-permute-start | bytes 786440 | tf_op jit(solution)/shard_map/n_aside0/ppermute | solution.py:300
  28.2 5.7 %copy-start.7 = (bf16[256,1024]{1,0:T(8,128)(2,1)S(1)}, bf16[256,1024]{1,0:T(8,128)(2,1)}, u32[]{:S(2)}) copy-start(bf16[256,1024]{1,0:T(8,128)(2,1)} %x.1) | copy-start | bytes 1572868
  28.2 10.6 %copy-start.1 = (bf16[1024,256]{1,0:T(8,128)(2,1)S(1)}, bf16[1024,256]{1,0:T(8,128)(2,1)}, u32[]{:S(2)}) copy-start(bf16[1024,256]{1,0:T(8,128)(2,1)} %wq.5) | copy-start | bytes 1572868
  28.2 10.6 %copy-start.3 = (bf16[1024,256]{1,0:T(8,128)(2,1)S(1)}, bf16[1024,256]{1,0:T(8,128)(2,1)}, u32[]{:S(2)}) copy-start(bf16[1024,256]{1,0:T(8,128)(2,1)} %wk.7) | copy-start | bytes 1572868
  28.2 10.6 %copy-start.5 = (bf16[1024,256]{1,0:T(8,128)(2,1)S(1)}, bf16[1024,256]{1,0:T(8,128)(2,1)}, u32[]{:S(2)}) copy-start(bf16[1024,256]{1,0:T(8,128)(2,1)} %wv.7) | copy-start | bytes 1572868
  28.2 22.4 %collective-permute-start.7 = (bf16[256,1024]{1,0:T(8,128)(2,1)S(1)}, bf16[256,1024]{1,0:T(8,128)(2,1)S(1)}, u32[]{:S(2)}, u32[]{:S(2)}) collective-permute-start(bf16[256,1024]{1,0:T(8,128)(2,1)S(1)} %collective-permute-done.1.refs_0_.xc), channel_id=1, source_target_pairs={{2,3},{1,0},{6,7},{5,4},{10,11},{9,8},{14,15},{13,12},{18,19},{17,... | collective-permute-start | bytes 1572872 | tf_op jit(solution)/shard_map/n_outer/ppermute | solution.py:300
  33.9 16.7 %collective-permute-start.6 = (bf16[256,1024]{1,0:T(8,128)(2,1)S(1)}, bf16[256,1024]{1,0:T(8,128)(2,1)S(1)}, u32[]{:S(2)}, u32[]{:S(2)}) collective-permute-start(bf16[256,1024]{1,0:T(8,128)(2,1)S(1)} %copy-done.7), channel_id=1, source_target_pairs={{1,2},{2,1},{5,6},{6,5},{9,10},{10,9},{13,14},{14,13},{17,18},{18,... | collective-permute-start | bytes 1572872 | tf_op jit(solution)/shard_map/n_inner/ppermute | solution.py:300
  39.9 20.3 %collective-permute-start.11 = (bf16[256,512]{1,0:T(8,128)(2,1)S(1)}, bf16[256,512]{1,0:T(8,128)(2,1)S(1)}, u32[]{:S(2)}, u32[]{:S(2)}) collective-permute-start(bf16[256,512]{1,0:T(8,128)(2,1)S(1)} %collective-permute-done.10), channel_id=1, source_target_pairs={{36,0},{37,1},{38,2},{39,3},{4,32},{5,33},{6,34},{7,35},{100,64},{... | collective-permute-start | bytes 786440 | tf_op jit(solution)/shard_map/n_across0/ppermute | solution.py:300
  40.6 19.6 %collective-permute-start.5 = (bf16[768,512]{1,0:T(8,128)(2,1)S(1)}, bf16[768,512]{1,0:T(8,128)(2,1)S(1)}, u32[]{:S(2)}, u32[]{:S(2)}) collective-permute-start(bf16[768,512]{1,0:T(8,128)(2,1)S(1)} %get-tuple-element.49.kv), channel_id=1, source_target_pairs={{0,4},{1,5},{2,6},{3,7},{4,8},{5,9},{6,10},{7,11},{8,12},{9,13},{1... | collective-permute-start | bytes 2359304 | tf_op jit(solution)/shard_map/n_near/ppermute | solution.py:300
  51.6 13.2 %collective-permute-start.12 = (bf16[256,512]{1,0:T(8,128)(2,1)S(1)}, bf16[256,512]{1,0:T(8,128)(2,1)S(1)}, u32[]{:S(2)}, u32[]{:S(2)}) collective-permute-start(bf16[256,512]{1,0:T(8,128)(2,1)S(1)} %n_last.1.refs_0_.kvd), channel_id=1, source_target_pairs={{0,4},{1,5},{2,6},{3,7},{4,8},{5,9},{6,10},{7,11},{8,12},{9,13},{1... | collective-permute-start | bytes 786440 | tf_op jit(solution)/shard_map/n_near_last/ppermute | solution.py:300
